TPU v7x, 512 devices: a whole 4x8x8 slice. The times are simulated.
512 devices in a mesh: trace: 8 (over y), seq: 64 (over z, x, core).
Axes of the slice: x: 4, y: 8, z: 8, core: 2. Of those that a mesh axis runs over, the one named last changes fastest.
Arguments:
- sel_hidden: bfloat16 [8, 512, 8, 4096], P('trace', 'seq'), may hold values from -6 to 6
- w_qkv: bfloat16 [4096, 3072], P('seq', 'trace'), may hold values from -0.09375 to 0.09375
- cache_pool: bfloat16 [8, 65536, 1024], P('trace', 'seq'), may hold values from -6 to 6
- block_owner: int32 [8, 512], P(None, 'seq'), may hold values from 0 to 63, as said below
- doc_lengths: int32 [8, 32], replicated, may hold values from 1 to 32, 512 in all within a row
- sel_index: int32 [8, 512, 8], P('trace', 'seq'), may hold values from 0 to 127, as said below
- sel_count: int32 [8, 512], P('trace', 'seq'), may hold values from 4 to 8, as said below
Outputs:
- attended: bfloat16 [8, 512, 8, 2048], P('trace', 'seq')
- blended: bfloat16 [8, 65536, 1024], P('trace', 'seq')
Inputs may be any that keep to these rules, and one draw needn't show every extreme that they name: `block_owner`: for each index of seq, the entries of all traces' blocks held there name each of the 64 cached slots held at that index once; one owner serves at most 2 blocks of one shard, and exactly 2 to some shard at every index. `sel_index`: within each block the 8 offsets are distinct and rising. `sel_count`: some block of every trace has all 8 slots live. `doc_lengths`: lengths of one trace sum to 512.
All inputs are finite; a program needn't handle non-finite values.
Results may differ from a plain program's by a relative error of at most 0.015.
Values may be sent and summed in bfloat16 or wider, within the bound.
No kernel may reach another device: no remote copies, remote signals or barrier semaphores. Data moves between devices by JAX's collectives and lax.ppermute only.
A program may use at most 64 MiB of HBM per device.

v0:
```python
import jax
import jax.numpy as jnp
from jax import lax
from jax.sharding import PartitionSpec as P

QUERY_HEADS = 16
KEY_VALUE_HEADS = 4
HEAD_SIZE = 128
WINDOW_TOKENS = 2048


ROPE_BASE = 10000.0


def from_behind(array, axis, by):
    peers = lax.axis_size(axis)
    pairs = [(i, i + by) for i in range(peers) if 0 <= i + by < peers]
    return lax.ppermute(array, axis, pairs)


def apply_rotary(values, token_positions):
    half_width = values.shape[-1] // 2
    frequency = 1.0 / ROPE_BASE ** (
        jnp.arange(half_width, dtype=jnp.float32) * 2.0 / values.shape[-1]
    )
    angles = token_positions.astype(jnp.float32)[..., None, None] * frequency
    cos_part = jnp.cos(angles)
    sin_part = jnp.sin(angles)
    values = values.astype(jnp.float32)
    low_half = values[..., :half_width]
    high_half = values[..., half_width:]
    return jnp.concatenate(
        [low_half * cos_part - high_half * sin_part, high_half * cos_part + low_half * sin_part],
        axis=-1,
    )


def attend(grouped, query_positions, key_value_slice, key_pos):
    key_total_count = key_value_slice.shape[0]
    key_columns = KEY_VALUE_HEADS * HEAD_SIZE
    key_head_split = key_value_slice[:, :key_columns].reshape(
        key_total_count, KEY_VALUE_HEADS, HEAD_SIZE
    )
    value_head_split = key_value_slice[:, key_columns:].reshape(
        key_total_count, KEY_VALUE_HEADS, HEAD_SIZE
    )
    scores = jnp.einsum(
        "hrd,nhd->hrn", grouped, key_head_split, preferred_element_type=jnp.float32
    ) * HEAD_SIZE ** (-0.5)
    allowed = (
        (key_pos[None, :] <= query_positions[:, None])
        & (key_pos[None, :] > query_positions[:, None] - WINDOW_TOKENS)
        & (key_pos[None, :] >= 0)
    )
    weights = jnp.where(allowed[None], jnp.exp(scores), 0.0)
    denominator = jnp.sum(weights, axis=-1)
    numerator = jnp.einsum(
        "hrn,nhd->hrd",
        weights.astype(jnp.bfloat16),
        value_head_split,
        preferred_element_type=jnp.float32,
    )
    return (numerator, denominator)


def on_device(sel_hidden, w_qkv, cache_pool, block_owner, doc_lengths, sel_index, sel_count):
    traces = lax.axis_size("trace")
    trace_id = lax.axis_index("trace")
    shard_id = lax.axis_index("seq")
    blocks = sel_hidden.shape[1]
    slot_count = sel_hidden.shape[2]
    model_width = sel_hidden.shape[3]
    token_rows = cache_pool.shape[1]
    kv_width = cache_pool.shape[2]
    block_len = token_rows // blocks
    selected_rows = blocks * slot_count
    query_columns = QUERY_HEADS * HEAD_SIZE
    key_columns = KEY_VALUE_HEADS * HEAD_SIZE
    head_groups = QUERY_HEADS // KEY_VALUE_HEADS
    capacity = max(2, (blocks + traces - 1) // traces)
    gathered = lax.all_gather(
        sel_hidden.reshape(selected_rows, model_width), "trace", axis=0, tiled=True
    )
    projected = jnp.dot(
        gathered,
        lax.all_gather(w_qkv, "seq", axis=0, tiled=True),
        preferred_element_type=jnp.float32,
    ).astype(jnp.bfloat16)
    merged_rows = lax.all_to_all(projected, "trace", split_axis=0, concat_axis=1, tiled=True)
    index_row = jnp.arange(blocks, dtype=jnp.int32)
    offsets = (index_row[:, None] * block_len + sel_index[0]).reshape(selected_rows)
    query_positions = shard_id * token_rows + offsets
    is_live = jnp.arange(slot_count, dtype=jnp.int32)[None, :] < sel_count[0][:, None]
    query_rows = apply_rotary(
        merged_rows[:, :query_columns].reshape(selected_rows, QUERY_HEADS, HEAD_SIZE),
        query_positions,
    ).astype(jnp.bfloat16)
    recomputed_keys = apply_rotary(
        merged_rows[:, query_columns : query_columns + key_columns].reshape(
            selected_rows, KEY_VALUE_HEADS, HEAD_SIZE
        ),
        query_positions,
    ).astype(jnp.bfloat16)
    fresh_rows = jnp.concatenate(
        [
            recomputed_keys.reshape(selected_rows, key_columns),
            merged_rows[:, query_columns + key_columns :],
        ],
        axis=1,
    )
    owner_of = block_owner // blocks
    slot_of = block_owner % blocks
    served = owner_of == trace_id
    order_in = jnp.cumsum(served.astype(jnp.int32), axis=1) - 1
    pick_mask = (
        served[:, :, None, None]
        & (order_in[:, :, None, None] == jnp.arange(capacity, dtype=jnp.int32)[None, None, :, None])
        & (slot_of[:, :, None, None] == index_row[None, None, None, :])
    )
    pick_mask = jnp.any(pick_mask, axis=1).astype(jnp.bfloat16)
    stored = cache_pool[0].reshape(blocks, block_len * kv_width)
    outgoing = jnp.einsum(
        "tcq,qx->tcx", pick_mask, stored, preferred_element_type=jnp.float32
    ).astype(jnp.bfloat16)
    incoming = lax.all_to_all(outgoing, "trace", split_axis=0, concat_axis=0, tiled=True).reshape(
        traces * capacity, block_len * kv_width
    )
    my_owner = lax.dynamic_index_in_dim(owner_of, trace_id, 0, keepdims=False)
    earlier = jnp.sum(
        (my_owner[None, :] == my_owner[:, None]) & (index_row[None, :] < index_row[:, None]), axis=1
    )
    source_row = my_owner * capacity + earlier
    choose = (
        source_row[:, None] == jnp.arange(traces * capacity, dtype=jnp.int32)[None, :]
    ).astype(jnp.bfloat16)
    cached_values = jnp.dot(choose, incoming, preferred_element_type=jnp.float32).reshape(
        token_rows, kv_width
    )
    doc_ends = jnp.cumsum(doc_lengths, axis=1)
    my_ends = lax.dynamic_index_in_dim(doc_ends, trace_id, 0, keepdims=False)
    my_lengths = lax.dynamic_index_in_dim(doc_lengths, trace_id, 0, keepdims=False)
    global_block = shard_id * blocks + index_row
    start_block = jnp.sum(
        jnp.where(my_ends[None, :] <= global_block[:, None], my_lengths[None, :], 0), axis=1
    )
    token_offset = jnp.repeat(start_block * block_len, block_len, total_repeat_length=token_rows)
    stored_key_rows = apply_rotary(
        cached_values[:, :key_columns].reshape(token_rows, KEY_VALUE_HEADS, HEAD_SIZE), token_offset
    ).reshape(token_rows, key_columns)
    restored = jnp.concatenate([stored_key_rows, cached_values[:, key_columns:]], axis=1)
    slot_hits = (
        sel_index[0][:, :, None] == jnp.arange(block_len, dtype=jnp.int32)[None, None, :]
    ) & is_live[:, :, None]
    placed = jnp.einsum(
        "bsp,bsx->bpx",
        slot_hits.astype(jnp.bfloat16),
        fresh_rows.reshape(blocks, slot_count, kv_width),
        preferred_element_type=jnp.float32,
    ).reshape(token_rows, kv_width)
    chosen = jnp.any(slot_hits, axis=1).reshape(token_rows)
    blended = jnp.where(chosen[:, None], placed, restored).astype(jnp.bfloat16)
    grouped = (
        query_rows.reshape(selected_rows, KEY_VALUE_HEADS, head_groups, HEAD_SIZE)
        .transpose(1, 2, 0, 3)
        .reshape(KEY_VALUE_HEADS, head_groups * selected_rows, HEAD_SIZE)
    )
    tiled_pos = jnp.tile(query_positions, head_groups)
    local_keys = jnp.arange(token_rows, dtype=jnp.int32)
    own_pos = shard_id * token_rows + local_keys
    numerator, denominator = attend(grouped, tiled_pos, blended, own_pos)
    prev_shards = (WINDOW_TOKENS + token_rows - 1) // token_rows
    key_value_slice = blended
    for distance in range(1, prev_shards + 1):
        key_value_slice = from_behind(key_value_slice, "seq", 1)
        part_numer, part_total = attend(
            grouped, tiled_pos, key_value_slice, own_pos - distance * token_rows
        )
        numerator = numerator + part_numer
        denominator = denominator + part_total
    layer_output = numerator / denominator[..., None]
    layer_output = (
        layer_output.reshape(KEY_VALUE_HEADS, head_groups, selected_rows, HEAD_SIZE)
        .transpose(2, 0, 1, 3)
        .reshape(blocks, slot_count, query_columns)
    )
    attended = jnp.where(is_live[:, :, None], layer_output, 0.0).astype(jnp.bfloat16)
    return (attended[None], blended[None])


def solution(mesh):
    placed = (
        P("trace", "seq", None, None),
        P("seq", "trace"),
        P("trace", "seq", None),
        P(None, "seq"),
        P(),
        P("trace", "seq", None),
        P("trace", "seq"),
    )
    return jax.shard_map(
        on_device,
        mesh=mesh,
        in_specs=placed,
        out_specs=(P("trace", "seq", None, None), P("trace", "seq", None)),
        check_vma=False,
    )
```

profile of v0, /device:TPU:264, one launch (start us, length us, event | category | flops | bytes accessed | tf_op | source)
XLA Modules:
  0.0 282.6 jit_solution(16936703551227291407)
XLA Ops:
  10.3 2.6 reshape.781
  14.2 6.3 %copy.50 = bf16[8,2,131072]{2,1,0:T(2,128)(2,1)} copy(bf16[8,2,131072]{2,0,1:T(8,128)(2,1)S(1)} %convolution_convert_fusion) | data formatting | bytes 8388608 | tf_op jit(solution)/shard_map/convert_element_type | solution.py:124
  20.5 7.7 %all-to-all-start.1 = ((bf16[8,2,131072]{2,1,0:T(2,128)(2,1)}), bf16[8,2,131072]{2,1,0:T(2,128)(2,1)}, u32[]{:S(2)}, u32[]{:S(2)}) async-start(bf16[8,2,131072]{2,1,0:T(2,128)(2,1)} %copy.50), calls=%async_computation.1 | async-start | bytes 8388608 | tf_op jit(solution)/shard_map/all_to_all | solution.py:125
  30.5 4.5 %compare_select_fusion.1 = s32[1024,1]{0,1:T(1,128)S(1)} fusion(s32[]{:T(128)} %bitcast.20, s32[]{:T(128)} %bitcast.21, s32[]{:T(128)} %bitcast.22, s32[]{:T(128)} %bitcast.23, s32[]{:T(128)} %bitcast.24, s32[]{:T(128)} %bitcast.26, s32[]{:T(128)} %bitcast.25, s32[1024,1]{0,1:T(1,128)S(1)} %bitcast.99, s32[1024,1]{0,1:T(1,128)S(1)} %bitcast.101), kind=kLoop, calls=%fused_computation.62 | loop fusion | flops 14336 | bytes 12316 | tf_op jit(solution)/shard_map/jit(_take)/gather | solution.py:146
  36.4 1.8 multiply_cosine_fusion
  38.2 56.2 %all-gather.5.cloned.1.call-done = bf16[4096,384]{1,0:T(8,128)(2,1)} async-done(((bf16[64,384]{1,0:T(8,128)(2,1)}), bf16[4096,384]{1,0:T(8,128)(2,1)}) %all-gather.5.cloned.1.call-update) | async-done | bytes 3145744 | tf_op jit(solution)/shard_map/all_gather | solution.py:86
  94.4 66.3 %all-gather.3.cloned.1.call-done = bf16[512,4096]{1,0:T(8,128)(2,1)} async-done(((bf16[64,4096]{1,0:T(8,128)(2,1)}), bf16[512,4096]{1,0:T(8,128)(2,1)}) %all-gather.3.cloned.1.call-update) | async-done | bytes 4194320 | tf_op jit(solution)/shard_map/all_gather | solution.py:81
  160.7 6.3 %convolution_convert_fusion.1 = bf16[512,384]{1,0:T(8,128)(2,1)} fusion(bf16[512,4096]{1,0:T(8,128)(2,1)} %all-gather.3.cloned.1.call-done, bf16[4096,384]{1,0:T(8,128)(2,1)} %all-gather.5.cloned.1.call-done), kind=kOutput, calls=%fused_computation.27 | convolution fusion | flops 1610809344 | bytes 7733248 | tf_op jit(solution)/shard_map/dot_general | solution.py:84
  167.0 5.6 %all-to-all-start = ((bf16[8,64,384]{2,1,0:T(8,128)(2,1)}), bf16[8,64,384]{2,1,0:T(8,128)(2,1)S(1)}, u32[]{:S(2)}, u32[]{:S(2)}) async-start(bf16[8,64,384]{2,1,0:T(8,128)(2,1)} %bitcast.2), calls=%async_computation | async-start | bytes 786432 | tf_op jit(solution)/shard_map/all_to_all | solution.py:89
  172.5 4.6 %reshape.722 = bf16[16,131072]{1,0:T(8,128)(2,1)} reshape(bf16[8,2,131072]{2,1,0:T(2,128)(2,1)} %all-to-all-done.1) | data formatting | bytes 8388608 | tf_op jit(solution)/shard_map/reshape | solution.py:125
  177.1 4.9 %fusion.50 = f32[8,131072]{1,0:T(8,128)} fusion(bf16[16,131072]{1,0:T(8,128)(2,1)} %reshape.722, s32[8]{0:T(128)S(1)} %multiply_add_fusion.1), kind=kOutput, calls=%fused_computation.95 | convolution fusion | flops 33554560 | bytes 8388640 | tf_op jit(solution)/shard_map/dot_general | solution.py:136
  182.0 4.9 %reshape.723 = f32[1024,1024]{1,0:T(8,128)} reshape(f32[8,131072]{1,0:T(8,128)} %fusion.50) | data formatting | bytes 8388608 | tf_op jit(solution)/shard_map/reshape | solution.py:136
  186.9 2.8 %slice.103 = bf16[1024,512]{1,0:T(8,128)(2,1)} slice(f32[1024,1024]{1,0:T(8,128)} %reshape.723), slice={[0:1024], [512:1024]} | slice | bytes 2097152 | tf_op jit(solution)/shard_map/slice | solution.py:150
  189.8 1.5 copy.71
  191.3 1.8 copy.70
  193.1 2.0 multiply_subtract_fusion
  199.6 2.2 fusion.32
  201.8 2.6 copy.54
  204.4 4.2 %fusion = bf16[1024,1024]{0,1:T(8,128)(2,1)} fusion(bf16[1024,1024]{0,1:T(8,128)(2,1)} %copy.54, bf16[1024,512]{0,1:T(8,128)(2,1)S(1)} %copy.71, bf16[1024,512]{0,1:T(8,128)(2,1)} %bitcast.76, pred[1024]{0:T(1024)(128)(4,1)S(1)} %bitcast.103), kind=kLoop, calls=%fused_computation.2 | loop fusion | flops 5242880 | bytes 6292480 | tf_op jit(solution)/shard_map/convert_element_type | solution.py:161
  208.5 1.9 collective-permute-start
  210.6 1.6 and_and_fusion
  213.2 2.6 copy.62
  215.7 3.2 %fusion.67 = (bf16[1024,512]{0,1:T(8,128)(2,1)}, bf16[1024,512]{0,1:T(8,128)(2,1)}) fusion(bf16[1024,1024]{0,1:T(8,128)(2,1)} %fusion), kind=kLoop, calls=%fused_computation.126 | loop fusion | bytes 4194304 | tf_op jit(solution)/shard_map/slice | solution.py:41
  220.0 19.5 %collective-permute-done = bf16[1024,1024]{0,1:T(8,128)(2,1)} collective-permute-done((bf16[1024,1024]{0,1:T(8,128)(2,1)}, bf16[1024,1024]{0,1:T(8,128)(2,1)}, u32[]{:S(2)}, u32[]{:S(2)}) %collective-permute-start) | collective-permute-done | bytes 2097184 | tf_op jit(solution)/shard_map/ppermute | solution.py:18
  239.5 2.1 collective-permute-start.1
  242.1 2.6 copy.63
  244.8 2.7 fusion.2
  248.3 1.7 fusion.66
  250.1 1.4 fusion.4
  252.3 18.2 %collective-permute-done.1 = bf16[1024,1024]{0,1:T(8,128)(2,1)} collective-permute-done((bf16[1024,1024]{0,1:T(8,128)(2,1)}, bf16[1024,1024]{0,1:T(8,128)(2,1)}, u32[]{:S(2)}, u32[]{:S(2)}) %collective-permute-start.1) | collective-permute-done | bytes 2097184 | tf_op jit(solution)/shard_map/ppermute | solution.py:18
  270.5 1.7 fusion.65
  272.2 1.4 fusion.6
  (98 shorter events, 19.1 us)
Async XLA Ops:
  7.2 87.2 %all-gather.5.cloned.1.call-start = ((), (), s32[]{:S(2)}) async-start(), calls=%async_computation.3 | async-start | bytes 3194880 | tf_op jit(solution)/shard_map/all_gather | solution.py:86
  7.9 152.8 %all-gather.3.cloned.1.call-start = ((), (), s32[]{:S(2)}) async-start(), calls=%async_computation.2 | async-start | bytes 4718592 | tf_op jit(solution)/shard_map/all_gather | solution.py:81
  20.5 7.8 %copy-start.12 = (s32[1,8,8]{2,1,0:T(8,128)S(1)}, s32[1,8,8]{2,1,0:T(8,128)}, u32[]{:S(2)}) copy-start(s32[1,8,8]{2,1,0:T(8,128)} %param.14) | copy-start | bytes 772
  20.5 7.9 %copy-start.13 = (s32[8,32]{1,0:T(8,128)S(1)}, s32[8,32]{1,0:T(8,128)}, u32[]{:S(2)}) copy-start(s32[8,32]{1,0:T(8,128)} %param.13) | copy-start | bytes 3076
  20.5 9.3 %copy-start.15 = (s32[1,8]{1,0:T(1,128)S(1)}, s32[1,8]{1,0:T(1,128)}, u32[]{:S(2)}) copy-start(s32[1,8]{1,0:T(1,128)} %param.15) | copy-start | bytes 100
  20.5 146.4 %all-to-all-start.1 = ((bf16[8,2,131072]{2,1,0:T(2,128)(2,1)}), bf16[8,2,131072]{2,1,0:T(2,128)(2,1)}, u32[]{:S(2)}, u32[]{:S(2)}) async-start(bf16[8,2,131072]{2,1,0:T(2,128)(2,1)} %copy.50), calls=%async_computation.1 | async-start | bytes 8388608 | tf_op jit(solution)/shard_map/all_to_all | solution.py:125
  167.0 29.2 %all-to-all-start = ((bf16[8,64,384]{2,1,0:T(8,128)(2,1)}), bf16[8,64,384]{2,1,0:T(8,128)(2,1)S(1)}, u32[]{:S(2)}, u32[]{:S(2)}) async-start(bf16[8,64,384]{2,1,0:T(8,128)(2,1)} %bitcast.2), calls=%async_computation | async-start | bytes 786432 | tf_op jit(solution)/shard_map/all_to_all | solution.py:89
  186.9 4.3 %slice-start = ((f32[1024,1024]{1,0:T(8,128)}), f32[1024,512]{1,0:T(8,128)S(1)}, s32[]{:S(2)}) async-start(f32[1024,1024]{1,0:T(8,128)} %reshape.723), calls=%async_computation.4 | async-start | bytes 4194304 | tf_op jit(solution)/shard_map/slice | solution.py:148
  193.1 5.6 %copy-start.5 = (f32[64,64]{1,0:T(8,128)S(1)}, f32[64,64]{1,0:T(8,128)}, u32[]{:S(2)}) copy-start(f32[64,64]{1,0:T(8,128)} %get-tuple-element.44) | copy-start | bytes 49156
  193.1 5.6 %copy-start.7 = (f32[64,64]{1,0:T(8,128)S(1)}, f32[64,64]{1,0:T(8,128)}, u32[]{:S(2)}) copy-start(f32[64,64]{1,0:T(8,128)} %get-tuple-element.45) | copy-start | bytes 49156
  196.1 0.7 copy-start.3
  204.4 6.1 %copy-start.14 = (s32[64]{0:T(128)S(1)}, s32[64]{0:T(128)}, u32[]{:S(2)}) copy-start(s32[64]{0:T(128)} %get-tuple-element.24) | copy-start | bytes 772
  208.5 31.0 %collective-permute-start = (bf16[1024,1024]{0,1:T(8,128)(2,1)}, bf16[1024,1024]{0,1:T(8,128)(2,1)}, u32[]{:S(2)}, u32[]{:S(2)}) collective-permute-start(bf16[1024,1024]{0,1:T(8,128)(2,1)} %fusion), channel_id=1, source_target_pairs={{0,1},{1,2},{2,3},{3,4},{4,5},{5,6},{6,7},{7,8},{8,9},{9,10},{10,1... | collective-permute-start | bytes 6291464 | tf_op jit(solution)/shard_map/ppermute | solution.py:18
  215.7 3.2 %copy-start = (bf16[1024,4,128]{0,2,1:T(8,128)(2,1)S(1)}, bf16[1024,4,128]{0,2,1:T(8,128)(2,1)}, u32[]{:S(2)}) copy-start(bf16[1024,4,128]{0,2,1:T(8,128)(2,1)} %pad_maximum_fusion) | copy-start | bytes 3145732
  215.7 3.2 %copy-start.1 = (bf16[1,1024,1024]{1,2,0:T(8,128)(2,1)S(1)}, bf16[1,1024,1024]{1,2,0:T(8,128)(2,1)}, u32[]{:S(2)}) copy-start(bf16[1,1024,1024]{1,2,0:T(8,128)(2,1)} %copy.62) | copy-start | bytes 6291460
  218.9 22.7 %copy-start.2 = (f32[8,8,16,128]{3,2,1,0:T(8,128)S(1)}, f32[8,8,16,128]{3,2,1,0:T(8,128)}, u32[]{:S(2)}) copy-start(f32[8,8,16,128]{3,2,1,0:T(8,128)} %copy.73) | copy-start | bytes 1572868
  218.9 22.7 %copy-start.6 = (f32[64,64]{1,0:T(8,128)S(1)}, f32[64,64]{1,0:T(8,128)}, u32[]{:S(2)}) copy-start(f32[64,64]{1,0:T(8,128)} %get-tuple-element.44) | copy-start | bytes 49156
  218.9 22.7 %copy-start.8 = (f32[64,64]{1,0:T(8,128)S(1)}, f32[64,64]{1,0:T(8,128)}, u32[]{:S(2)}) copy-start(f32[64,64]{1,0:T(8,128)} %get-tuple-element.45) | copy-start | bytes 49156
  220.0 24.8 %copy-start.11 = (pred[256,1024]{1,0:T(8,128)(4,1)S(1)}, pred[256,1024]{1,0:T(8,128)(4,1)}, u32[]{:S(2)}) copy-start(pred[256,1024]{1,0:T(8,128)(4,1)} %get-tuple-element.43) | copy-start | bytes 786436
  239.5 31.0 %collective-permute-start.1 = (bf16[1024,1024]{0,1:T(8,128)(2,1)}, bf16[1024,1024]{0,1:T(8,128)(2,1)}, u32[]{:S(2)}, u32[]{:S(2)}) collective-permute-start(bf16[1024,1024]{0,1:T(8,128)(2,1)} %collective-permute-done), channel_id=1, source_target_pairs={{0,1},{1,2},{2,3},{3,4},{4,5},{5,6},{6,7},{7,8},{8,9},{9,10},{10,1... | collective-permute-start | bytes 6291464 | tf_op jit(solution)/shard_map/ppermute | solution.py:18
  244.6 2.8 %copy-start.4 = (bf16[1024,512]{0,1:T(8,128)(2,1)S(1)}, bf16[1024,512]{0,1:T(8,128)(2,1)}, u32[]{:S(2)}) copy-start(bf16[1024,512]{0,1:T(8,128)(2,1)} %get-tuple-element.32) | copy-start | bytes 3145732
  247.5 2.6 copy-start.10
  251.4 20.8 %copy-start.9 = (pred[256,1024]{1,0:T(8,128)(4,1)S(1)}, pred[256,1024]{1,0:T(8,128)(4,1)}, u32[]{:S(2)}) copy-start(pred[256,1024]{1,0:T(8,128)(4,1)} %get-tuple-element.41) | copy-start | bytes 786436
Sparse Core Ops, SparseCore 0:
  11.3 83.0 all-gather.4
  96.5 64.1 all-gather.2
where the time goes:
time: 283 us
  waiting for transfers between devices  162 us (57%)
  local copies, waits for them, and re-layouts  43.8 us (15%)
  other arithmetic  22.8 us (8%)
  matrix products  22.6 us (8%)
  starting transfers between devices  17.4 us (6%)
  between operations  14.4 us (5%)
    all_gather x1, waiting for transfers between devices, on_device(): lax.all_gather(sel_hidden.reshape(selected_rows, model_width), 'trace', a...  66.3 us
    all_gather x1, waiting for transfers between devices, on_device(): lax.all_gather(w_qkv, 'seq', axis=0, tiled=True)  56.2 us
    ppermute x2, waiting for transfers between devices, from_behind(): return lax.ppermute(array, axis, pairs)  37.7 us
    all_to_all x1, starting transfers between devices, on_device(): lax.all_to_all(outgoing, 'trace', split_axis=0, concat_axis=0, tiled=True)  7.68 us
    slice x3, local copies, waits for them, and re-layouts, attend(): key_value_slice[:, :key_columns]  6.65 us
    convert_element_type x1, local copies, waits for them, and re-layouts, on_device(): outgoing = jnp.einsum('tcq,qx->tcx', pick_mask, stored, preferred_element...  6.29 us
    dot_general x1, matrix products, on_device(): jnp.dot(gathered, lax.all_gather(w_qkv, 'seq', axis=0, tiled=True), prefe...  6.27 us
    unnamed x35, local copies, waits for them, and re-layouts  5.74 us
  transfers between devices with their start and end apart: 6, of which 4 were waited for; matrix products, arithmetic and copies ran while one was open for 25% of the time, Pallas kernels for 0%

commit v1 on v0

v1 whole, which is shorter than its diff:
```python
import jax
import jax.numpy as jnp
from jax import lax
from jax.experimental import pallas as pl
from jax.experimental.pallas import tpu as pltpu
from jax.sharding import Mesh
from jax.sharding import PartitionSpec as P

QH = 16
KH = 4
HD = 128
GROUP = QH // KH
WINDOW = 2048
BASE = 10000.0
NX, NC = 4, 2
CAP = 2
SEQ = ("z", "x", "c")
XC = ("x", "c")
F32 = jnp.float32
BF = jnp.bfloat16
VM = pl.BlockSpec(memory_space=pltpu.VMEM)
SM = pl.BlockSpec(memory_space=pltpu.SMEM)
ANY = pl.BlockSpec(memory_space=pl.ANY)


def call(kernel, out, ins, outs, scratch=(), flops=0, moved=0, vmem=48):
    return pl.pallas_call(
        kernel,
        out_shape=out,
        in_specs=ins,
        out_specs=outs,
        scratch_shapes=list(scratch),
        compiler_params=pltpu.CompilerParams(vmem_limit_bytes=vmem << 20),
        cost_estimate=pl.CostEstimate(flops=flops, bytes_accessed=moved, transcendentals=0),
    )


def pick_kernel(owner, me, pool, out, sem):
    blocks = owner.shape[1]
    rows = pool.shape[0] // blocks
    mine = me[0]
    for t in range(owner.shape[0]):
        count = jnp.int32(0)
        for b in range(blocks):
            o = owner[t, b]
            slot = o % blocks
            hit = o // blocks == mine

            @pl.when(hit)
            def _(slot=slot, count=count):
                start = pl.multiple_of(slot * rows, rows)
                pltpu.make_async_copy(
                    pool.at[pl.ds(start, rows)], out.at[t * CAP + count], sem.at[slot]
                ).start()

            count = count + hit.astype(jnp.int32)
    for slot in range(blocks):
        pltpu.make_async_copy(pool.at[pl.ds(slot * rows, rows)], out.at[0], sem.at[slot]).wait()


def head(ref, n):
    return ref[n // 3, :, pl.ds((n % 3) * HD, HD)]


def rotated(x, cos, sin):
    x = x.astype(F32)
    return x * cos + pltpu.roll(x, HD // 2, 1) * sin


def rope_kernel(proj, cos, sin, sel, q_out, fresh):
    for n in range(QH):
        q_out[:, n * HD : (n + 1) * HD] = rotated(head(proj, n), cos[...], sin[...]).astype(BF)
    rows = q_out.shape[0]
    q_out[:, QH * HD :] = jnp.broadcast_to(sel[...].astype(F32), (rows, HD)).astype(BF)
    for n in range(KH):
        k = rotated(head(proj, QH + n), cos[...], sin[...])
        fresh[:, n * HD : (n + 1) * HD] = k.astype(BF)
        fresh[:, (KH + n) * HD : (KH + n + 1) * HD] = head(proj, QH + KH + n)


def blend_kernel(
    owner, me, spots, kcos, ksin, fresh, q0, q1, q2, incoming,
    blended, num0, den0, p1, p2, kv, qs, sem, out_sem,
):
    blocks = owner.shape[1]
    tokens, width = kv.shape
    rows = tokens // blocks
    mine = me[0]
    own = [owner[mine, b] // blocks for b in range(blocks)]
    for b in range(blocks):
        rank = jnp.int32(0)
        for e in range(b):
            rank = rank + (own[e] == own[b]).astype(jnp.int32)
        pltpu.make_async_copy(
            incoming.at[own[b] * CAP + rank], kv.at[pl.ds(b * rows, rows)], sem.at[b]
        ).start()
    n_q = q0.shape[0]
    for k in range(KH):
        for i, q in enumerate((q0, q1, q2)):
            for g in range(GROUP):
                h = k * GROUP + g
                qs[k, pl.ds((i * GROUP + g) * n_q, n_q), :] = q[:, h * HD : (h + 1) * HD]
    ones = jnp.ones((n_q, HD), BF)
    for b in range(blocks):
        at = lax.broadcasted_iota(jnp.int32, (rows, n_q), 0) + b * rows
        hits = (at == spots[...]).astype(F32).astype(BF)
        chosen = jnp.dot(hits, ones, preferred_element_type=F32) > 0.5
        here = pl.ds(b * rows, rows)
        pltpu.make_async_copy(incoming.at[0], kv.at[here], sem.at[b]).wait()
        cos, sin = kcos[b : b + 1, :], ksin[b : b + 1, :]
        for n in range(2 * KH):
            cols = pl.ds(n * HD, HD)
            x = kv[here, cols]
            x = rotated(x, cos, sin) if n < KH else x.astype(F32)
            placed = jnp.dot(hits, fresh[:, cols], preferred_element_type=F32)
            kv[here, cols] = jnp.where(chosen, placed, x).astype(BF)
        pltpu.make_async_copy(kv.at[here], blended.at[here], out_sem.at[b]).start()

    spot_row = lax.broadcasted_iota(jnp.int32, (n_q, 1), 0) // 8 * rows

    def where_of(q):
        return spot_row + q[:, QH * HD : QH * HD + 1].astype(F32).astype(jnp.int32)

    key = lax.broadcasted_iota(jnp.int32, (n_q, tokens), 1)
    ok0 = key <= where_of(q0)
    ok2 = key > where_of(q2)
    lane = lax.broadcasted_iota(jnp.int32, (n_q, HD), 1)
    dens = [jnp.zeros((n_q, HD), F32) for _ in range(3)]
    for k in range(KH):
        keys = kv[:, k * HD : (k + 1) * HD]
        values = kv[:, (KH + k) * HD : (KH + k + 1) * HD]
        for i in range(3):
            part = qs[k, pl.ds(i * GROUP * n_q, GROUP * n_q), :]
            scores = lax.dot_general(
                part, keys, (((1,), (1,)), ((), ())), preferred_element_type=F32
            )
            w = jnp.exp(scores * HD ** (-0.5))
            if i != 1:
                w = jnp.where(
                    (ok0 if i == 0 else ok2)[None], w.reshape(GROUP, n_q, tokens), 0.0
                ).reshape(GROUP * n_q, tokens)
            total = jnp.sum(w, axis=1, keepdims=True)
            num = jnp.dot(w.astype(BF), values, preferred_element_type=F32)
            for g in range(GROUP):
                h = k * GROUP + g
                here = slice(g * n_q, (g + 1) * n_q)
                dens[i] = jnp.where(lane == h, total[here], dens[i])
                cols = pl.ds(h * HD, HD)
                if i == 0:
                    num0[:, cols] = num[here]
                elif i == 1:
                    p1[:, cols] = num[here].astype(BF)
                else:
                    p2[:, cols] = num[here].astype(BF)
    den0[...] = dens[0]
    for p, d in ((p1, dens[1]), (p2, dens[2])):
        high = d.astype(BF)
        low = d - high.astype(F32)
        p[:, QH * HD :] = jnp.where(
            lane < QH, high.astype(F32), pltpu.roll(low, QH, 1)
        ).astype(BF)
    for b in range(blocks):
        here = pl.ds(b * rows, rows)
        pltpu.make_async_copy(kv.at[here], blended.at[here], out_sem.at[b]).wait()


def merge_kernel(num0, den0, r1, r2, live, out):
    total = den0[...]
    for r in (r1, r2):
        d = r[:, QH * HD :].astype(F32)
        total = total + d + pltpu.roll(d, HD - QH, 1)
    alive = live[...] > 0
    for h in range(QH):
        cols = pl.ds(h * HD, HD)
        num = num0[:, cols] + r1[:, cols].astype(F32) + r2[:, cols].astype(F32)
        out[:, cols] = jnp.where(alive, num / total[:, h : h + 1], 0.0).astype(BF)


def half_turns(angles):
    cos, sin = jnp.cos(angles), jnp.sin(angles)
    return jnp.concatenate([cos, cos], -1), jnp.concatenate([-sin, sin], -1)


def on_device(sel_hidden, w_qkv, cache_pool, block_owner, doc_lengths, sel_index, sel_count):
    ny, nz = lax.axis_size("y"), lax.axis_size("z")
    y = lax.axis_index("y")
    shard = lax.axis_index(SEQ)
    group = NX * NC
    n_seq = nz * group
    _, blocks, slots, d = sel_hidden.shape
    rows = blocks * slots
    tokens, kvw = cache_pool.shape[1:]
    block_len = tokens // blocks
    cols = w_qkv.shape[1]
    me = y.reshape(1).astype(jnp.int32)

    outgoing = call(
        pick_kernel,
        jax.ShapeDtypeStruct((ny * CAP, block_len, kvw), BF),
        [SM, SM, ANY], ANY,
        [pltpu.SemaphoreType.DMA((blocks,))],
        moved=4 * tokens * kvw,
    )(block_owner, me, cache_pool[0])
    incoming = lax.all_to_all(outgoing, "y", 0, 0, tiled=True)

    flip = [(a * group + b, b * group + a) for a in range(ny) for b in range(group)]
    far = [(a * group + b, (b ^ 4) * group + a) for a in range(ny) for b in range(group)]
    over = ("y", "x", "c")
    w = (lax.ppermute(w_qkv, over, flip), lax.ppermute(w_qkv, over, far))

    def paired(mine, other, bit, axis):
        low = (y // bit) % 2 == 0
        return jnp.stack([jnp.where(low, mine, other), jnp.where(low, other, mine)], axis)

    w = paired(w[0], w[1], 4, 0)
    for axis, bit in ((1, 2), (2, 1)):
        other = lax.ppermute(w, "y", [(i, i ^ bit) for i in range(ny)])
        w = paired(w, other, bit, axis)
    w = lax.all_gather(w.reshape(-1, cols), "z", axis=0, tiled=True)
    hidden = lax.all_gather(sel_hidden.reshape(rows, d), XC, axis=0, tiled=True)
    projected = jnp.dot(hidden, w, preferred_element_type=F32).astype(BF)
    merged = lax.all_to_all(projected.reshape(group, rows, cols), XC, 0, 0, tiled=True)

    frequency = 1.0 / BASE ** (jnp.arange(HD // 2, dtype=F32) * 2.0 / HD)
    index = jnp.arange(blocks, dtype=jnp.int32)
    local = (index[:, None] * block_len + sel_index[0]).reshape(rows)
    live = (jnp.arange(slots, dtype=jnp.int32)[None, :] < sel_count[0][:, None]).reshape(rows)
    cos, sin = half_turns((shard * tokens + local).astype(F32)[:, None] * frequency)
    lengths = lax.dynamic_index_in_dim(doc_lengths, y, 0, keepdims=False)
    nth = jnp.arange(lengths.shape[0], dtype=jnp.int32)
    ends = jnp.sum(jnp.where(nth[None, :] <= nth[:, None], lengths[None, :], 0), axis=1)
    here = shard * blocks + index
    first = jnp.sum(jnp.where(ends[None, :] <= here[:, None], lengths[None, :], 0), axis=1)
    kcos, ksin = half_turns((first * block_len).astype(F32)[:, None] * frequency)
    spots = jnp.where(live, local, -1).reshape(1, rows)

    wide = QH * HD + HD
    queries, fresh = call(
        rope_kernel,
        (jax.ShapeDtypeStruct((rows, wide), BF), jax.ShapeDtypeStruct((rows, kvw), BF)),
        [VM] * 4, (VM, VM),
        moved=4 * rows * (wide + kvw),
    )(merged, cos, sin, sel_index.reshape(rows, 1))

    def along(array, by):
        pairs = [(i, i + by) for i in range(n_seq) if 0 <= i + by < n_seq]
        return lax.ppermute(array, SEQ, pairs)

    q1, q2 = along(queries, -1), along(queries, -2)
    blended, num0, den0, p1, p2 = call(
        blend_kernel,
        (
            jax.ShapeDtypeStruct((tokens, kvw), BF),
            jax.ShapeDtypeStruct((rows, QH * HD), F32),
            jax.ShapeDtypeStruct((rows, HD), F32),
            jax.ShapeDtypeStruct((rows, wide), BF),
            jax.ShapeDtypeStruct((rows, wide), BF),
        ),
        [SM, SM] + [VM] * 7 + [ANY], (ANY, VM, VM, VM, VM),
        [
            pltpu.VMEM((tokens, kvw), BF),
            pltpu.VMEM((KH, 3 * GROUP * rows, HD), BF),
            pltpu.SemaphoreType.DMA((blocks,)),
            pltpu.SemaphoreType.DMA((blocks,)),
        ],
        flops=12 * rows * QH * HD * tokens,
        moved=8 * tokens * kvw,
    )(block_owner, me, spots, kcos, ksin, fresh, queries, q1, q2, incoming)
    r1, r2 = along(p1, 1), along(p2, 2)
    attended = call(
        merge_kernel,
        jax.ShapeDtypeStruct((rows, QH * HD), BF),
        [VM] * 5, VM,
        moved=12 * rows * QH * HD,
    )(num0, den0, r1, r2, live.astype(jnp.int32).reshape(rows, 1))
    return attended.reshape(1, blocks, slots, QH * HD), blended[None]


def solution(mesh):
    ny, n_seq = mesh.devices.shape
    fine = Mesh(
        mesh.devices.reshape(ny, n_seq // (NX * NC), NX, NC), ("y", "z", "x", "c")
    )
    return jax.shard_map(
        on_device,
        mesh=fine,
        in_specs=(
            P("y", SEQ, None, None),
            P(SEQ, "y"),
            P("y", SEQ, None),
            P(None, SEQ),
            P(),
            P("y", SEQ, None),
            P("y", SEQ),
        ),
        out_specs=(P("y", SEQ, None, None), P("y", SEQ, None)),
        check_vma=False,
    )
```

time: 283 us -> 281 us (level)
  the two profiles are of different devices: /device:TPU:264 before, /device:TPU:65 now
where the time goes in v1:
time: 281 us
  waiting for transfers between devices  210 us (75%)
  starting transfers between devices  36.4 us (13%)
  between operations  14.4 us (5%)
  Pallas kernels  11.5 us (4%)
  matrix products  4.98 us (2%)
    all_to_all x1, waiting for transfers between devices, on_device(): incoming = lax.all_to_all(outgoing, 'y', 0, 0, tiled=True)  89.4 us
    all_gather x1, waiting for transfers between devices, on_device(): w = lax.all_gather(w.reshape(-1, cols), 'z', axis=0, tiled=True)  48.9 us
    all_gather x1, waiting for transfers between devices, on_device(): hidden = lax.all_gather(sel_hidden.reshape(rows, d), XC, axis=0, tiled=True)  39.5 us
    ppermute x2, waiting for transfers between devices, on_device(): other = lax.ppermute(w, 'y', [(i, i ^ bit) for i in range(ny)])  11.6 us
    ppermute x4, waiting for transfers between devices, along(): return lax.ppermute(array, SEQ, pairs)  11.2 us
    ppermute x2, starting transfers between devices, on_device(): w = (lax.ppermute(w_qkv, over, flip), lax.ppermute(w_qkv, over, far))  11 us
    ppermute x4, starting transfers between devices, along(): return lax.ppermute(array, SEQ, pairs)  10.2 us
    pallas_call x1, Pallas kernels, on_device(): call(blend_kernel, (jax.ShapeDtypeStruct((tokens, kvw), BF), jax.ShapeDty...  7.98 us
  transfers between devices with their start and end apart: 12, of which 9 were waited for; matrix products, arithmetic and copies ran while one was open for 1% of the time, Pallas kernels for 1%

profile of v1, /device:TPU:65, one launch (start us, length us, event | category | flops | bytes accessed | tf_op | source)
XLA Modules:
  0.0 280.8 jit_solution(2749063149565610089)
XLA Ops:
  7.2 3.8 %collective-permute-start = (bf16[64,384]{1,0:T(8,128)(2,1)}, bf16[64,384]{1,0:T(8,128)(2,1)S(1)}, u32[]{:S(2)}, u32[]{:S(2)}) collective-permute-start(bf16[64,384]{1,0:T(8,128)(2,1)} %param.8), channel_id=1, source_target_pairs={{0,0},{1,64},{2,128},{3,192},{4,256},{5,320},{6,384},{7,448},{64,1... | collective-permute-start | bytes 147464 | tf_op jit(solution)/shard_map/ppermute | solution.py:209
  11.0 7.3 %collective-permute-start.1 = (bf16[64,384]{1,0:T(8,128)(2,1)}, bf16[64,384]{1,0:T(8,128)(2,1)S(1)}, u32[]{:S(2)}, u32[]{:S(2)}) collective-permute-start(bf16[64,384]{1,0:T(8,128)(2,1)} %param.8), channel_id=1, source_target_pairs={{0,256},{1,320},{2,384},{3,448},{4,0},{5,64},{6,128},{7,192},{64,2... | collective-permute-start | bytes 147464 | tf_op jit(solution)/shard_map/ppermute | solution.py:209
  18.3 3.2 %collective-permute-done.1 = bf16[64,384]{1,0:T(8,128)(2,1)S(1)} collective-permute-done((bf16[64,384]{1,0:T(8,128)(2,1)}, bf16[64,384]{1,0:T(8,128)(2,1)S(1)}, u32[]{:S(2)}, u32[]{:S(2)}) %collective-permute-start.1) | collective-permute-done | bytes 49184 | tf_op jit(solution)/shard_map/ppermute | solution.py:209
  21.6 3.1 %collective-permute-start.2 = (bf16[2,64,384]{2,1,0:T(8,128)(2,1)S(1)}, bf16[2,64,384]{2,1,0:T(8,128)(2,1)S(1)}, u32[]{:S(2)}, u32[]{:S(2)}) collective-permute-start(bf16[2,64,384]{2,1,0:T(8,128)(2,1)S(1)} %pad_maximum_fusion.2), channel_id=1, source_target_pairs={{0,128},{64,192},{128,0},{192,64},{256,384},{320,448},{384,256},{4... | collective-permute-start | bytes 294920 | tf_op jit(solution)/shard_map/ppermute | solution.py:217
  24.7 6.0 %collective-permute-done.2 = bf16[2,64,384]{2,1,0:T(8,128)(2,1)S(1)} collective-permute-done((bf16[2,64,384]{2,1,0:T(8,128)(2,1)S(1)}, bf16[2,64,384]{2,1,0:T(8,128)(2,1)S(1)}, u32[]{:S(2)}, u32[]{:S(2)}) %collective-permute-start.2) | collective-permute-done | bytes 98336 | tf_op jit(solution)/shard_map/ppermute | solution.py:217
  30.8 1.9 collective-permute-start.3
  32.7 5.6 %collective-permute-done.3 = bf16[2,2,64,384]{3,2,1,0:T(8,128)(2,1)S(1)} collective-permute-done((bf16[2,2,64,384]{3,2,1,0:T(8,128)(2,1)S(1)}, bf16[2,2,64,384]{3,2,1,0:T(8,128)(2,1)S(1)}, u32[]{:S(2)}, u32[]{:S(2)}) %collective-permute-start.3) | collective-permute-done | bytes 196640 | tf_op jit(solution)/shard_map/ppermute | solution.py:217
  38.3 0.8 pad_maximum_fusion
  39.2 0.7 all-gather.5.cloned.1.call-update
  39.9 48.9 %all-gather.3.cloned.1.call-done = bf16[4096,384]{1,0:T(8,128)(2,1)} async-done(((bf16[512,384]{1,0:T(8,128)(2,1)}), bf16[4096,384]{1,0:T(8,128)(2,1)}) %all-gather.3.cloned.1.call-update) | async-done | bytes 3145744 | tf_op jit(solution)/shard_map/all_gather | solution.py:219
  88.8 39.5 %all-gather.5.cloned.1.call-done = bf16[512,4096]{1,0:T(8,128)(2,1)} async-done(((bf16[64,4096]{1,0:T(8,128)(2,1)}), bf16[512,4096]{1,0:T(8,128)(2,1)}) %all-gather.5.cloned.1.call-update) | async-done | bytes 4194320 | tf_op jit(solution)/shard_map/all_gather | solution.py:220
  128.2 5.0 %fusion = bf16[512,384]{0,1:T(8,128)(2,1)S(1)} fusion(bf16[4096,384]{1,0:T(8,128)(2,1)} %all-gather.3.cloned.1.call-done, bf16[512,4096]{1,0:T(8,128)(2,1)} %all-gather.5.cloned.1.call-done), kind=kOutput, calls=%fused_computation.1 | convolution fusion | flops 1610809344 | bytes 7733248 | tf_op jit(solution)/shard_map/dot_general | solution.py:221
  133.2 0.9 copy.19
  134.2 3.6 %all-to-all-start = ((bf16[8,64,384]{2,1,0:T(8,128)(2,1)}), bf16[8,64,384]{2,1,0:T(8,128)(2,1)S(1)}, u32[]{:S(2)}, u32[]{:S(2)}) async-start(bf16[8,64,384]{2,1,0:T(8,128)(2,1)} %bitcast.14), calls=%async_computation | async-start | bytes 786432 | tf_op jit(solution)/shard_map/all_to_all | solution.py:222
  137.8 2.2 shard_map.87
  140.1 5.8 %all-to-all-done.proj = bf16[8,64,384]{2,1,0:T(8,128)(2,1)S(1)} async-done(((bf16[8,64,384]{2,1,0:T(8,128)(2,1)}), bf16[8,64,384]{2,1,0:T(8,128)(2,1)S(1)}, u32[]{:S(2)}, u32[]{:S(2)}) %all-to-all-start) | async-done | bytes 393248 | tf_op jit(solution)/shard_map/all_to_all | solution.py:222
  145.9 6.5 %all-to-all-start.1 = ((bf16[16,128,1024]{2,1,0:T(8,128)(2,1)}), bf16[16,128,1024]{2,1,0:T(8,128)(2,1)}, u32[]{:S(2)}, u32[]{:S(2)}) async-start(bf16[16,128,1024]{2,1,0:T(8,128)(2,1)} %shard_map.87), calls=%async_computation.1 | async-start | bytes 8388608 | tf_op jit(solution)/shard_map/all_to_all | solution.py:204
  152.7 0.1 select_reduce_fusion
  152.8 0.2 select_reduce_fusion.1
  153.0 0.2 fusion.1
  153.4 0.1 fusion.2
  153.5 0.2 shard_map.86
  153.7 3.1 %collective-permute-start.4 = (bf16[64,2176]{1,0:T(8,128)(2,1)S(1)}, bf16[64,2176]{1,0:T(8,128)(2,1)S(1)}, u32[]{:S(2)}, u32[]{:S(2)}) collective-permute-start(bf16[64,2176]{1,0:T(8,128)(2,1)S(1)} %get-tuple-element.10.q0), channel_id=1, source_target_pairs={{1,0},{2,1},{3,2},{4,3},{5,4},{6,5},{7,6},{8,7},{9,8},{10,9},{11,1... | collective-permute-start | bytes 835592 | tf_op jit(solution)/shard_map/ppermute | solution.py:247
  156.8 2.6 collective-permute-start.5
  159.6 0.1 lt.56
  159.7 89.4 %all-to-all-done.1.incoming = bf16[16,128,1024]{2,1,0:T(8,128)(2,1)} async-done(((bf16[16,128,1024]{2,1,0:T(8,128)(2,1)}), bf16[16,128,1024]{2,1,0:T(8,128)(2,1)}, u32[]{:S(2)}, u32[]{:S(2)}) %all-to-all-start.1) | async-done | bytes 4194336 | tf_op jit(solution)/shard_map/all_to_all | solution.py:204
  249.2 8.0 %shard_map.88 = (bf16[1024,1024]{1,0:T(8,128)(2,1)}, f32[64,2048]{1,0:T(8,128)S(1)}, f32[64,128]{1,0:T(8,128)S(1)}, bf16[64,2176]{1,0:T(8,128)(2,1)S(1)}, bf16[64,2176]{1,0:T(8,128)(2,1)S(1)}) custom-call(s32[8,8]{1,0:T(8,128)S(1)} %copy-done.2, s32[1]{0:T(128)} %bitcast.me, s32[1,64]{1,0:T(1,128)S(1)} %add_select_fusion.spots, ...), custom_call_target="tpu_custom_call" | custom-call | flops 1610612736 | bytes 8388608 | tf_op jit(solution)/shard_map/pallas_call | solution.py:250
  257.2 2.6 collective-permute-start.6
  259.8 1.9 collective-permute-start.7
  261.8 1.9 collective-permute-done.6.r1
  263.7 9.3 %collective-permute-done.7.r2 = bf16[64,2176]{1,0:T(8,128)(2,1)S(1)} collective-permute-done((bf16[64,2176]{1,0:T(8,128)(2,1)S(1)}, bf16[64,2176]{1,0:T(8,128)(2,1)S(1)}, u32[]{:S(2)}, u32[]{:S(2)}) %collective-permute-start.7) | collective-permute-done | bytes 278560 | tf_op jit(solution)/shard_map/ppermute | solution.py:247
  272.9 1.0 shard_map.89
  (38 shorter events, 1.1 us)
Async XLA Ops:
  7.2 145.5 %copy-start = (s32[8,32]{1,0:T(8,128)S(1)}, s32[8,32]{1,0:T(8,128)}, u32[]{:S(2)}) copy-start(s32[8,32]{1,0:T(8,128)} %param.11) | copy-start | bytes 3076
  7.2 81.6 %all-gather.3.cloned.1.call-start = ((), (), s32[]{:S(2)}) async-start(), calls=%async_computation.2 | async-start | bytes 3538944 | tf_op jit(solution)/shard_map/all_gather | solution.py:219
  7.2 11.1 %collective-permute-start = (bf16[64,384]{1,0:T(8,128)(2,1)}, bf16[64,384]{1,0:T(8,128)(2,1)S(1)}, u32[]{:S(2)}, u32[]{:S(2)}) collective-permute-start(bf16[64,384]{1,0:T(8,128)(2,1)} %param.8), channel_id=1, source_target_pairs={{0,0},{1,64},{2,128},{3,192},{4,256},{5,320},{6,384},{7,448},{64,1... | collective-permute-start | bytes 147464 | tf_op jit(solution)/shard_map/ppermute | solution.py:209
  11.0 10.5 %collective-permute-start.1 = (bf16[64,384]{1,0:T(8,128)(2,1)}, bf16[64,384]{1,0:T(8,128)(2,1)S(1)}, u32[]{:S(2)}, u32[]{:S(2)}) collective-permute-start(bf16[64,384]{1,0:T(8,128)(2,1)} %param.8), channel_id=1, source_target_pairs={{0,256},{1,320},{2,384},{3,448},{4,0},{5,64},{6,128},{7,192},{64,2... | collective-permute-start | bytes 147464 | tf_op jit(solution)/shard_map/ppermute | solution.py:209
  21.6 9.1 %collective-permute-start.2 = (bf16[2,64,384]{2,1,0:T(8,128)(2,1)S(1)}, bf16[2,64,384]{2,1,0:T(8,128)(2,1)S(1)}, u32[]{:S(2)}, u32[]{:S(2)}) collective-permute-start(bf16[2,64,384]{2,1,0:T(8,128)(2,1)S(1)} %pad_maximum_fusion.2), channel_id=1, source_target_pairs={{0,128},{64,192},{128,0},{192,64},{256,384},{320,448},{384,256},{4... | collective-permute-start | bytes 294920 | tf_op jit(solution)/shard_map/ppermute | solution.py:217
  30.8 7.5 %collective-permute-start.3 = (bf16[2,2,64,384]{3,2,1,0:T(8,128)(2,1)S(1)}, bf16[2,2,64,384]{3,2,1,0:T(8,128)(2,1)S(1)}, u32[]{:S(2)}, u32[]{:S(2)}) collective-permute-start(bf16[2,2,64,384]{3,2,1,0:T(8,128)(2,1)S(1)} %pad_maximum_fusion.1), channel_id=1, source_target_pairs={{0,64},{64,0},{128,192},{192,128},{256,320},{320,256},{384,448},{4... | collective-permute-start | bytes 589832 | tf_op jit(solution)/shard_map/ppermute | solution.py:217
  39.1 89.1 %all-gather.5.cloned.1.call-start = ((), (), s32[]{:S(2)}) async-start(), calls=%async_computation.3 | async-start | bytes 4718592 | tf_op jit(solution)/shard_map/all_gather | solution.py:220
  39.9 97.9 %copy-start.1 = (bf16[1,1024,1024]{2,1,0:T(8,128)(2,1)S(1)}, bf16[1,1024,1024]{2,1,0:T(8,128)(2,1)}, u32[]{:S(2)}) copy-start(bf16[1,1024,1024]{2,1,0:T(8,128)(2,1)} %param.9) | copy-start | bytes 6291460
  39.9 97.9 %copy-start.2 = (s32[8,8]{1,0:T(8,128)S(1)}, s32[8,8]{1,0:T(8,128)}, u32[]{:S(2)}) copy-start(s32[8,8]{1,0:T(8,128)} %owner.3) | copy-start | bytes 772
  134.2 11.7 %all-to-all-start = ((bf16[8,64,384]{2,1,0:T(8,128)(2,1)}), bf16[8,64,384]{2,1,0:T(8,128)(2,1)S(1)}, u32[]{:S(2)}, u32[]{:S(2)}) async-start(bf16[8,64,384]{2,1,0:T(8,128)(2,1)} %bitcast.14), calls=%async_computation | async-start | bytes 786432 | tf_op jit(solution)/shard_map/all_to_all | solution.py:222
  140.0 12.3 %copy-start.3 = (s32[1,8,8]{2,1,0:T(8,128)S(1)}, s32[1,8,8]{2,1,0:T(8,128)}, u32[]{:S(2)}) copy-start(s32[1,8,8]{2,1,0:T(8,128)} %param.12) | copy-start | bytes 772
  140.0 13.3 %copy-start.4 = (s32[1,8]{1,0:T(1,128)S(1)}, s32[1,8]{1,0:T(1,128)}, u32[]{:S(2)}) copy-start(s32[1,8]{1,0:T(1,128)} %param.13) | copy-start | bytes 100
  145.9 103.3 %all-to-all-start.1 = ((bf16[16,128,1024]{2,1,0:T(8,128)(2,1)}), bf16[16,128,1024]{2,1,0:T(8,128)(2,1)}, u32[]{:S(2)}, u32[]{:S(2)}) async-start(bf16[16,128,1024]{2,1,0:T(8,128)(2,1)} %shard_map.87), calls=%async_computation.1 | async-start | bytes 8388608 | tf_op jit(solution)/shard_map/all_to_all | solution.py:204
  153.7 95.4 %collective-permute-start.4 = (bf16[64,2176]{1,0:T(8,128)(2,1)S(1)}, bf16[64,2176]{1,0:T(8,128)(2,1)S(1)}, u32[]{:S(2)}, u32[]{:S(2)}) collective-permute-start(bf16[64,2176]{1,0:T(8,128)(2,1)S(1)} %get-tuple-element.10.q0), channel_id=1, source_target_pairs={{1,0},{2,1},{3,2},{4,3},{5,4},{6,5},{7,6},{8,7},{9,8},{10,9},{11,1... | collective-permute-start | bytes 835592 | tf_op jit(solution)/shard_map/ppermute | solution.py:247
  156.8 92.4 %collective-permute-start.5 = (bf16[64,2176]{1,0:T(8,128)(2,1)S(1)}, bf16[64,2176]{1,0:T(8,128)(2,1)S(1)}, u32[]{:S(2)}, u32[]{:S(2)}) collective-permute-start(bf16[64,2176]{1,0:T(8,128)(2,1)S(1)} %get-tuple-element.10.q0), channel_id=1, source_target_pairs={{2,0},{3,1},{4,2},{5,3},{6,4},{7,5},{8,6},{9,7},{10,8},{11,9},{12,... | collective-permute-start | bytes 835592 | tf_op jit(solution)/shard_map/ppermute | solution.py:247
  257.2 6.5 %collective-permute-start.6 = (bf16[64,2176]{1,0:T(8,128)(2,1)S(1)}, bf16[64,2176]{1,0:T(8,128)(2,1)S(1)}, u32[]{:S(2)}, u32[]{:S(2)}) collective-permute-start(bf16[64,2176]{1,0:T(8,128)(2,1)S(1)} %get-tuple-element.13), channel_id=1, source_target_pairs={{0,1},{1,2},{2,3},{3,4},{4,5},{5,6},{6,7},{7,8},{8,9},{9,10},{10,1... | collective-permute-start | bytes 835592 | tf_op jit(solution)/shard_map/ppermute | solution.py:247
  259.8 13.1 %collective-permute-start.7 = (bf16[64,2176]{1,0:T(8,128)(2,1)S(1)}, bf16[64,2176]{1,0:T(8,128)(2,1)S(1)}, u32[]{:S(2)}, u32[]{:S(2)}) collective-permute-start(bf16[64,2176]{1,0:T(8,128)(2,1)S(1)} %get-tuple-element.14), channel_id=1, source_target_pairs={{0,2},{1,3},{2,4},{3,5},{4,6},{5,7},{6,8},{7,9},{8,10},{9,11},{10,... | collective-permute-start | bytes 835592 | tf_op jit(solution)/shard_map/ppermute | solution.py:247
Sparse Core Ops, SparseCore 0:
  39.3 49.4 all-gather.2
  90.9 37.2 all-gather.4

commit v2 on v1

v2 whole, which is shorter than its diff:
```python
import jax
import jax.numpy as jnp
from jax import lax
from jax.experimental import pallas as pl
from jax.experimental.pallas import tpu as pltpu
from jax.sharding import Mesh
from jax.sharding import PartitionSpec as P

QH = 16
KH = 4
HD = 128
GROUP = QH // KH
BLOCK = 128
BASE = 10000.0
NX, NC = 4, 2
CAP = 2
SEQ = ("z", "x", "c")
XC = ("x", "c")
F32 = jnp.float32
BF = jnp.bfloat16
VM = pl.BlockSpec(memory_space=pltpu.VMEM)
SM = pl.BlockSpec(memory_space=pltpu.SMEM)
ANY = pl.BlockSpec(memory_space=pl.ANY)


def call(kernel, out, ins, outs, scratch=(), flops=0, moved=0, vmem=8):
    return pl.pallas_call(
        kernel,
        out_shape=out,
        in_specs=ins,
        out_specs=outs,
        scratch_shapes=list(scratch),
        compiler_params=pltpu.CompilerParams(vmem_limit_bytes=vmem << 20),
        cost_estimate=pl.CostEstimate(flops=flops, bytes_accessed=moved, transcendentals=0),
    )


def pick_kernel(owner, me, pool, one_up, one_down, two_up, two_down, three_up, three_down, kept, sem):
    traces, blocks = owner.shape
    rows = pool.shape[0] // blocks
    mine = me[0]
    for slot in range(blocks):
        kept[slot] = 0
    slots = {
        1: (one_up.at[0], one_up.at[1]),
        2: (two_up.at[0], two_up.at[1]),
        3: (three_up.at[0], three_up.at[1]),
        4: (one_up.at[2], one_down.at[2]),
        5: (three_down.at[0], three_down.at[1]),
        6: (two_down.at[0], two_down.at[1]),
        7: (one_down.at[0], one_down.at[1]),
    }
    for d in range(traces):
        t = lax.rem(mine + d, traces)
        count = jnp.int32(0)
        for b in range(blocks):
            o = owner[t, b]
            slot = o % blocks
            hit = o // blocks == mine
            for nth in range(CAP if d else 0):

                @pl.when(hit & (count == nth))
                def _(slot=slot, out=slots[d][nth]):
                    start = pl.multiple_of(slot * rows, rows)
                    pltpu.make_async_copy(pool.at[pl.ds(start, rows)], out, sem.at[slot]).start()

            if d == 0:

                @pl.when(hit)
                def _(slot=slot):
                    kept[slot] = 1

            count = count + hit.astype(jnp.int32)
    for slot in range(blocks):

        @pl.when(kept[slot] == 0)
        def _(slot=slot):
            pltpu.make_async_copy(
                pool.at[pl.ds(slot * rows, rows)], two_up.at[0], sem.at[slot]
            ).wait()


def head(ref, n):
    per = ref.shape[2] // HD
    return ref[n // per, :, pl.ds((n % per) * HD, HD)]


def rotated(x, cos, sin):
    x = x.astype(F32)
    return x * cos + pltpu.roll(x, HD // 2, 1) * sin


def rope_kernel(proj, cos, sin, sel, q_out, fresh):
    for n in range(QH):
        q_out[:, n * HD : (n + 1) * HD] = rotated(head(proj, n), cos[...], sin[...]).astype(BF)
    rows = q_out.shape[0]
    q_out[:, QH * HD :] = jnp.broadcast_to(sel[...].astype(F32), (rows, HD)).astype(BF)
    for n in range(KH):
        k = rotated(head(proj, QH + n), cos[...], sin[...])
        fresh[:, n * HD : (n + 1) * HD] = k.astype(BF)
        fresh[:, (KH + n) * HD : (KH + n + 1) * HD] = head(proj, QH + KH + n)


def attend(queries, kv, stack, masks, put):
    n_q = queries[0].shape[0]
    tokens = kv.shape[0]
    size = GROUP * n_q
    lane = lax.broadcasted_iota(jnp.int32, (n_q, HD), 1)
    sums = [jnp.zeros((n_q, HD), F32) for _ in queries]
    for k in range(KH):
        keys = kv[:, k * HD : (k + 1) * HD]
        values = kv[:, (KH + k) * HD : (KH + k + 1) * HD]
        for i, q in enumerate(queries):
            for g in range(GROUP):
                h = k * GROUP + g
                stack[i, pl.ds(g * n_q, n_q), :] = q[:, h * HD : (h + 1) * HD]
            scores = lax.dot_general(
                stack[i], keys, (((1,), (1,)), ((), ())), preferred_element_type=F32
            )
            w = jnp.exp(scores * HD ** (-0.5))
            if masks[i] is not None:
                w = jnp.where(masks[i][None], w.reshape(GROUP, n_q, tokens), 0.0)
                w = w.reshape(size, tokens)
            total = jnp.sum(w, axis=1, keepdims=True)
            num = jnp.dot(w.astype(BF), values, preferred_element_type=F32)
            for g in range(GROUP):
                h = k * GROUP + g
                here = slice(g * n_q, (g + 1) * n_q)
                sums[i] = jnp.where(lane == h, total[here], sums[i])
                put(i, pl.ds(h * HD, HD), num[here])
    return sums


def token_of(q, tokens):
    n_q = q.shape[0]
    per = n_q // (tokens // BLOCK)
    block = lax.broadcasted_iota(jnp.int32, (n_q, 1), 0) // per
    return block * BLOCK + q[:, QH * HD : QH * HD + 1].astype(F32).astype(jnp.int32)


def blend_kernel(
    owner, me, kcos, ksin, spots, fresh, q0,
    pool, one_up, one_down, two_up, two_down, three_up, three_down,
    blended, kv, num0, den0, stack, sem, out_sem,
):
    traces, blocks = owner.shape
    rows = kv.shape[0] // blocks
    mine = me[0]
    own = [owner[mine, b] // blocks for b in range(blocks)]
    slots = {
        1: (one_up.at[0], one_up.at[1]),
        2: (two_up.at[0], two_up.at[1]),
        3: (three_up.at[0], three_up.at[1]),
        4: (three_up.at[2], three_down.at[2]),
        5: (three_down.at[0], three_down.at[1]),
        6: (two_down.at[0], two_down.at[1]),
        7: (one_down.at[0], one_down.at[1]),
    }
    for b in range(blocks):
        here = kv.at[pl.ds(b * rows, rows)]
        rank = jnp.int32(0)
        for e in range(b):
            rank = rank + (own[e] == own[b]).astype(jnp.int32)
        d = lax.rem(mine - own[b] + traces, traces)

        @pl.when(d == 0)
        def _(b=b, here=here):
            start = pl.multiple_of(owner[mine, b] % blocks * rows, rows)
            pltpu.make_async_copy(pool.at[pl.ds(start, rows)], here, sem.at[b]).start()

        for far in range(1, traces):
            for nth in range(CAP):

                @pl.when((d == far) & (rank == nth))
                def _(b=b, here=here, block=slots[far][nth]):
                    pltpu.make_async_copy(block, here, sem.at[b]).start()

    tokens, width = kv.shape
    n_q = q0.shape[0]
    ones = jnp.ones((n_q, HD), BF)
    for b in range(blocks):
        here = pl.ds(b * rows, rows)
        at = lax.broadcasted_iota(jnp.int32, (rows, n_q), 0) + b * rows
        hits = (at == spots[...]).astype(F32).astype(BF)
        chosen = jnp.dot(hits, ones, preferred_element_type=F32) > 0.5
        pltpu.make_async_copy(two_up.at[0], kv.at[here], sem.at[b]).wait()
        cos, sin = kcos[b : b + 1, :], ksin[b : b + 1, :]
        for n in range(width // HD):
            cols = pl.ds(n * HD, HD)
            x = kv[here, cols]
            x = rotated(x, cos, sin) if n < KH else x.astype(F32)
            placed = jnp.dot(hits, fresh[:, cols], preferred_element_type=F32)
            kv[here, cols] = jnp.where(chosen, placed, x).astype(BF)
        pltpu.make_async_copy(kv.at[here], blended.at[here], out_sem.at[b]).start()
    key = lax.broadcasted_iota(jnp.int32, (n_q, tokens), 1)

    def put(i, cols, num):
        num0[:, cols] = num

    (den0[...],) = attend([q0], kv, stack, [key <= token_of(q0, tokens)], put)
    for b in range(blocks):
        here = pl.ds(b * rows, rows)
        pltpu.make_async_copy(kv.at[here], blended.at[here], out_sem.at[b]).wait()


def remote_kernel(q1, q2, kv, p1, p2, stack):
    tokens = kv.shape[0]
    n_q = q1.shape[0]
    key = lax.broadcasted_iota(jnp.int32, (n_q, tokens), 1)

    def put(i, cols, num):
        (p1, p2)[i][:, cols] = num.astype(BF)

    sums = attend([q1, q2], kv, stack, [None, key > token_of(q2, tokens)], put)
    lane = lax.broadcasted_iota(jnp.int32, (n_q, HD), 1)
    for p, d in zip((p1, p2), sums):
        high = d.astype(BF)
        low = d - high.astype(F32)
        p[:, QH * HD :] = jnp.where(
            lane < QH, high.astype(F32), pltpu.roll(low, QH, 1)
        ).astype(BF)


def merge_kernel(num0, den0, r1, r2, live, out):
    total = den0[...]
    for r in (r1, r2):
        d = r[:, QH * HD :].astype(F32)
        total = total + d + pltpu.roll(d, HD - QH, 1)
    alive = live[...] > 0
    for h in range(QH):
        cols = pl.ds(h * HD, HD)
        num = num0[:, cols] + r1[:, cols].astype(F32) + r2[:, cols].astype(F32)
        out[:, cols] = jnp.where(alive, num / total[:, h : h + 1], 0.0).astype(BF)


def half_turns(angles):
    cos, sin = jnp.cos(angles), jnp.sin(angles)
    return jnp.concatenate([cos, cos], -1), jnp.concatenate([-sin, sin], -1)


def on_device(sel_hidden, w_qkv, cache_pool, block_owner, doc_lengths, sel_index, sel_count):
    ny, nz = lax.axis_size("y"), lax.axis_size("z")
    y = lax.axis_index("y")
    shard = lax.axis_index(SEQ)
    group = NX * NC
    n_seq = nz * group
    _, blocks, slots, d = sel_hidden.shape
    rows = blocks * slots
    tokens, kvw = cache_pool.shape[1:]
    block_len = tokens // blocks
    cols = w_qkv.shape[1]
    me = y.reshape(1).astype(jnp.int32)

    def turned(array, by):
        return lax.ppermute(array, "y", [(i, (i + by) % ny) for i in range(ny)])

    def room(n):
        return jax.ShapeDtypeStruct((n, block_len, kvw), BF)

    one_up, one_down, two_up, two_down, three_up, three_down = call(
        pick_kernel,
        (room(3), room(3), room(2), room(2), room(3), room(3)),
        [SM, SM, ANY], (ANY,) * 6,
        [pltpu.SMEM((blocks,), jnp.int32), pltpu.SemaphoreType.DMA((blocks,))],
        moved=4 * tokens * kvw,
    )(block_owner, me, cache_pool[0])
    one_up, w_qkv = lax.optimization_barrier((one_up, w_qkv))

    def crossed(m):
        pairs = [(a * group + b, (b ^ m) * group + a) for a in range(ny) for b in range(group)]
        return lax.ppermute(w_qkv, ("y", "x", "c"), pairs)

    def paired(mine, other, bit, axis):
        low = (y // bit) % 2 == 0
        return jnp.stack([jnp.where(low, mine, other), jnp.where(low, other, mine)], axis)

    w = paired(
        paired(crossed(0), crossed(4), 4, 0), paired(crossed(2), crossed(6), 4, 0), 2, 1
    )
    w = paired(w, lax.ppermute(w, "y", [(i, i ^ 1) for i in range(ny)]), 1, 2)
    w = w.reshape(-1, cols)
    w, one_up, one_down = lax.optimization_barrier((w, one_up, one_down))
    one_up, one_down = turned(one_up, 1), turned(one_down, -1)
    hidden = lax.all_gather(sel_hidden.reshape(rows, d), XC, axis=0, tiled=True)
    w, hidden, one_up, one_down = lax.optimization_barrier((w, hidden, one_up, one_down))
    w = lax.all_gather(w, "z", axis=0, tiled=True)
    two_up, two_down = turned(two_up, 2), turned(two_down, -2)
    three_up = turned(lax.dynamic_update_slice(three_up, one_up[2:], (2, 0, 0)), 3)
    three_down = turned(lax.dynamic_update_slice(three_down, one_down[2:], (2, 0, 0)), -3)
    projected = jnp.dot(hidden, w, preferred_element_type=F32).astype(BF)
    merged = lax.all_to_all(projected.reshape(group, rows, cols), XC, 0, 0, tiled=True)

    frequency = 1.0 / BASE ** (jnp.arange(HD // 2, dtype=F32) * 2.0 / HD)
    index = jnp.arange(blocks, dtype=jnp.int32)
    local = (index[:, None] * block_len + sel_index[0]).reshape(rows)
    live = (jnp.arange(slots, dtype=jnp.int32)[None, :] < sel_count[0][:, None]).reshape(rows)
    cos, sin = half_turns((shard * tokens + local).astype(F32)[:, None] * frequency)
    lengths = lax.dynamic_index_in_dim(doc_lengths, y, 0, keepdims=False)
    nth = jnp.arange(lengths.shape[0], dtype=jnp.int32)
    ends = jnp.sum(jnp.where(nth[None, :] <= nth[:, None], lengths[None, :], 0), axis=1)
    here = shard * blocks + index
    first = jnp.sum(jnp.where(ends[None, :] <= here[:, None], lengths[None, :], 0), axis=1)
    kcos, ksin = half_turns((first * block_len).astype(F32)[:, None] * frequency)
    spots = jnp.where(live, local, -1).reshape(1, rows)

    wide = QH * HD + HD
    queries, fresh = call(
        rope_kernel,
        (jax.ShapeDtypeStruct((rows, wide), BF), jax.ShapeDtypeStruct((rows, kvw), BF)),
        [VM] * 4, (VM, VM),
        moved=4 * rows * (wide + kvw),
    )(merged, cos, sin, sel_index.reshape(rows, 1))

    def along(array, by):
        pairs = [(i, i + by) for i in range(n_seq) if 0 <= i + by < n_seq]
        return lax.ppermute(array, SEQ, pairs)

    q1, q2 = along(queries, -1), along(queries, -2)
    blended, kv, num0, den0 = call(
        blend_kernel,
        (
            jax.ShapeDtypeStruct((tokens, kvw), BF),
            jax.ShapeDtypeStruct((tokens, kvw), BF),
            jax.ShapeDtypeStruct((rows, QH * HD), F32),
            jax.ShapeDtypeStruct((rows, HD), F32),
        ),
        [SM, SM] + [VM] * 5 + [ANY] * 7, (ANY, VM, VM, VM),
        [
            pltpu.VMEM((1, GROUP * rows, HD), BF),
            pltpu.SemaphoreType.DMA((blocks,)),
            pltpu.SemaphoreType.DMA((blocks,)),
        ],
        flops=4 * rows * QH * HD * tokens,
        moved=6 * tokens * kvw,
        vmem=20,
    )(
        block_owner, me, kcos, ksin, spots, fresh, queries, cache_pool[0],
        one_up, one_down, two_up, two_down, three_up, three_down,
    )
    p1, p2 = call(
        remote_kernel,
        (jax.ShapeDtypeStruct((rows, wide), BF),) * 2,
        [VM] * 3, (VM, VM),
        [pltpu.VMEM((2, GROUP * rows, HD), BF)],
        flops=8 * rows * QH * HD * tokens,
        moved=2 * tokens * kvw,
        vmem=20,
    )(q1, q2, kv)
    r1, r2 = along(p1, 1), along(p2, 2)
    attended = call(
        merge_kernel,
        jax.ShapeDtypeStruct((rows, QH * HD), BF),
        [VM] * 5, VM,
        moved=12 * rows * QH * HD,
    )(num0, den0, r1, r2, live.astype(jnp.int32).reshape(rows, 1))
    return attended.reshape(1, blocks, slots, QH * HD), blended[None]


def solution(mesh):
    ny, n_seq = mesh.devices.shape
    fine = Mesh(
        mesh.devices.reshape(ny, n_seq // (NX * NC), NX, NC), ("y", "z", "x", "c")
    )
    return jax.shard_map(
        on_device,
        mesh=fine,
        in_specs=(
            P("y", SEQ, None, None),
            P(SEQ, "y"),
            P("y", SEQ, None),
            P(None, SEQ),
            P(),
            P("y", SEQ, None),
            P("y", SEQ),
        ),
        out_specs=(P("y", SEQ, None, None), P("y", SEQ, None)),
        check_vma=False,
    )
```

time: 281 us -> 189 us (0.67)
  the two profiles are of different devices: /device:TPU:65 before, /device:TPU:257 now
where the time goes in v2:
time: 189 us; the launch traced here: 188 us
  waiting for transfers between devices  72.2 us (38%)
  starting transfers between devices  70.2 us (37%)
  between operations  14.5 us (8%)
  Pallas kernels  13.5 us (7%)
  local copies, waits for them, and re-layouts  7.9 us (4%)
  matrix products  6.25 us (3%)
  other arithmetic  3.81 us (2%)
    all_gather x1, waiting for transfers between devices, on_device(): w = lax.all_gather(w, 'z', axis=0, tiled=True)  31.5 us
    ppermute x4, starting transfers between devices, along(): return lax.ppermute(array, SEQ, pairs)  22.5 us
    ppermute x6, starting transfers between devices, turned(): return lax.ppermute(array, 'y', [(i, (i + by) % ny) for i in range(ny)])  21.1 us
    ppermute x4, starting transfers between devices, crossed(): return lax.ppermute(w_qkv, ('y', 'x', 'c'), pairs)  19.5 us
    ppermute x6, waiting for transfers between devices, turned(): return lax.ppermute(array, 'y', [(i, (i + by) % ny) for i in range(ny)])  15 us
    ppermute x4, waiting for transfers between devices, along(): return lax.ppermute(array, SEQ, pairs)  8.62 us
    all_to_all x1, waiting for transfers between devices, on_device(): lax.all_to_all(projected.reshape(group, rows, cols), XC, 0, 0, tiled=True)  7.22 us
    dot_general x1, matrix products, on_device(): projected = jnp.dot(hidden, w, preferred_element_type=F32).astype(BF)  6.25 us
  transfers between devices with their start and end apart: 18, of which 8 were waited for; matrix products, arithmetic and copies ran while one was open for 6% of the time, Pallas kernels for 4%

profile of v2, /device:TPU:257, one launch (start us, length us, event | category | flops | bytes accessed | tf_op | source)
XLA Modules:
  0.0 188.3 jit_solution(17603590765207903540)
XLA Ops:
  8.0 1.6 copy-done.1
  10.3 1.9 shard_map.86
  13.7 4.1 %collective-permute-start = (bf16[64,384]{1,0:T(8,128)(2,1)}, bf16[64,384]{1,0:T(8,128)(2,1)S(1)}, u32[]{:S(2)}, u32[]{:S(2)}) collective-permute-start(bf16[64,384]{1,0:T(8,128)(2,1)} %param.8), channel_id=1, source_target_pairs={{0,0},{1,64},{2,128},{3,192},{4,256},{5,320},{6,384},{7,448},{64,1... | collective-permute-start | bytes 147464 | tf_op jit(solution)/shard_map/ppermute | solution.py:271
  17.9 7.3 %collective-permute-start.1 = (bf16[64,384]{1,0:T(8,128)(2,1)}, bf16[64,384]{1,0:T(8,128)(2,1)S(1)}, u32[]{:S(2)}, u32[]{:S(2)}) collective-permute-start(bf16[64,384]{1,0:T(8,128)(2,1)} %param.8), channel_id=1, source_target_pairs={{0,256},{1,320},{2,384},{3,448},{4,0},{5,64},{6,128},{7,192},{64,2... | collective-permute-start | bytes 147464 | tf_op jit(solution)/shard_map/ppermute | solution.py:271
  25.1 3.4 %collective-permute-start.2 = (bf16[64,384]{1,0:T(8,128)(2,1)}, bf16[64,384]{1,0:T(8,128)(2,1)S(1)}, u32[]{:S(2)}, u32[]{:S(2)}) collective-permute-start(bf16[64,384]{1,0:T(8,128)(2,1)} %param.8), channel_id=1, source_target_pairs={{0,128},{1,192},{2,0},{3,64},{4,384},{5,448},{6,256},{7,320},{64,1... | collective-permute-start | bytes 147464 | tf_op jit(solution)/shard_map/ppermute | solution.py:271
  28.5 4.7 %collective-permute-start.3 = (bf16[64,384]{1,0:T(8,128)(2,1)}, bf16[64,384]{1,0:T(8,128)(2,1)S(1)}, u32[]{:S(2)}, u32[]{:S(2)}) collective-permute-start(bf16[64,384]{1,0:T(8,128)(2,1)} %param.8), channel_id=1, source_target_pairs={{0,384},{1,448},{2,256},{3,320},{4,128},{5,192},{6,0},{7,64},{64,3... | collective-permute-start | bytes 147464 | tf_op jit(solution)/shard_map/ppermute | solution.py:271
  33.4 3.5 %collective-permute-done.3 = bf16[64,384]{1,0:T(8,128)(2,1)S(1)} collective-permute-done((bf16[64,384]{1,0:T(8,128)(2,1)}, bf16[64,384]{1,0:T(8,128)(2,1)S(1)}, u32[]{:S(2)}, u32[]{:S(2)}) %collective-permute-start.3) | collective-permute-done | bytes 49184 | tf_op jit(solution)/shard_map/ppermute | solution.py:271
  37.0 2.1 %collective-permute-start.4 = (bf16[2,2,64,384]{3,2,1,0:T(8,128)(2,1)S(1)}, bf16[2,2,64,384]{3,2,1,0:T(8,128)(2,1)S(1)}, u32[]{:S(2)}, u32[]{:S(2)}) collective-permute-start(bf16[2,2,64,384]{3,2,1,0:T(8,128)(2,1)S(1)} %pad_maximum_fusion.1), channel_id=1, source_target_pairs={{0,64},{64,0},{128,192},{192,128},{256,320},{320,256},{384,448},{4... | collective-permute-start | bytes 589832 | tf_op jit(solution)/shard_map/ppermute | solution.py:280
  39.1 5.5 %collective-permute-done.4 = bf16[2,2,64,384]{3,2,1,0:T(8,128)(2,1)S(1)} collective-permute-done((bf16[2,2,64,384]{3,2,1,0:T(8,128)(2,1)S(1)}, bf16[2,2,64,384]{3,2,1,0:T(8,128)(2,1)S(1)}, u32[]{:S(2)}, u32[]{:S(2)}) %collective-permute-start.4) | collective-permute-done | bytes 196640 | tf_op jit(solution)/shard_map/ppermute | solution.py:280
  45.5 2.5 %collective-permute-start.5 = (bf16[3,128,1024]{2,1,0:T(8,128)(2,1)S(1)}, bf16[3,128,1024]{2,1,0:T(8,128)(2,1)S(1)}, u32[]{:S(2)}, u32[]{:S(2)}) collective-permute-start(bf16[3,128,1024]{2,1,0:T(8,128)(2,1)S(1)} %get-tuple-element.30), channel_id=1, source_target_pairs={{0,64},{64,128},{128,192},{192,256},{256,320},{320,384},{384,448},... | collective-permute-start | bytes 2359304 | tf_op jit(solution)/shard_map/ppermute | solution.py:255
  48.0 4.0 %collective-permute-start.6 = (bf16[3,128,1024]{2,1,0:T(8,128)(2,1)S(1)}, bf16[3,128,1024]{2,1,0:T(8,128)(2,1)S(1)}, u32[]{:S(2)}, u32[]{:S(2)}) collective-permute-start(bf16[3,128,1024]{2,1,0:T(8,128)(2,1)S(1)} %get-tuple-element.31), channel_id=1, source_target_pairs={{0,448},{64,0},{128,64},{192,128},{256,192},{320,256},{384,320},{4... | collective-permute-start | bytes 2359304 | tf_op jit(solution)/shard_map/ppermute | solution.py:255
  52.0 14.0 %collective-permute-done.5.one_up = bf16[3,128,1024]{2,1,0:T(8,128)(2,1)S(1)} collective-permute-done((bf16[3,128,1024]{2,1,0:T(8,128)(2,1)S(1)}, bf16[3,128,1024]{2,1,0:T(8,128)(2,1)S(1)}, u32[]{:S(2)}, u32[]{:S(2)}) %collective-permute-start.5) | collective-permute-done | bytes 786464 | tf_op jit(solution)/shard_map/ppermute | solution.py:255
  66.0 1.0 collective-permute-done.6.one_down
  67.0 3.3 %collective-permute-start.7 = (bf16[2,128,1024]{2,1,0:T(8,128)(2,1)}, bf16[2,128,1024]{2,1,0:T(8,128)(2,1)}, u32[]{:S(2)}, u32[]{:S(2)}) collective-permute-start(bf16[2,128,1024]{2,1,0:T(8,128)(2,1)} %copy-done.10), channel_id=1, source_target_pairs={{0,128},{64,192},{128,256},{192,320},{256,384},{320,448},{384,0},{... | collective-permute-start | bytes 1572872 | tf_op jit(solution)/shard_map/ppermute | solution.py:255
  70.3 4.1 %collective-permute-start.8 = (bf16[2,128,1024]{2,1,0:T(8,128)(2,1)}, bf16[2,128,1024]{2,1,0:T(8,128)(2,1)}, u32[]{:S(2)}, u32[]{:S(2)}) collective-permute-start(bf16[2,128,1024]{2,1,0:T(8,128)(2,1)} %copy-done.9), channel_id=1, source_target_pairs={{0,384},{64,448},{128,0},{192,64},{256,128},{320,192},{384,256},{4... | collective-permute-start | bytes 1572872 | tf_op jit(solution)/shard_map/ppermute | solution.py:255
  76.6 4.3 %collective-permute-start.10 = (bf16[3,128,1024]{2,1,0:T(8,128)(2,1)}, bf16[3,128,1024]{2,1,0:T(8,128)(2,1)}, u32[]{:S(2)}, u32[]{:S(2)}) collective-permute-start(bf16[3,128,1024]{2,1,0:T(8,128)(2,1)} %slice_dynamic-update-slice_fusion), channel_id=1, source_target_pairs={{0,320},{64,384},{128,448},{192,0},{256,64},{320,128},{384,192},{4... | collective-permute-start | bytes 2359304 | tf_op jit(solution)/shard_map/ppermute | solution.py:255
  81.7 2.9 %collective-permute-start.9 = (bf16[3,128,1024]{2,1,0:T(8,128)(2,1)}, bf16[3,128,1024]{2,1,0:T(8,128)(2,1)}, u32[]{:S(2)}, u32[]{:S(2)}) collective-permute-start(bf16[3,128,1024]{2,1,0:T(8,128)(2,1)} %slice_dynamic-update-slice_fusion.1), channel_id=1, source_target_pairs={{0,192},{64,256},{128,320},{192,384},{256,448},{320,0},{384,64},{4... | collective-permute-start | bytes 2359304 | tf_op jit(solution)/shard_map/ppermute | solution.py:255
  84.6 31.5 %all-gather.5.cloned.1.call-done = bf16[4096,384]{1,0:T(8,128)(2,1)} async-done(((bf16[512,384]{1,0:T(8,128)(2,1)}), bf16[4096,384]{1,0:T(8,128)(2,1)}) %all-gather.5.cloned.1.call-update) | async-done | bytes 3145744 | tf_op jit(solution)/shard_map/all_gather | solution.py:286
  116.1 6.3 %convolution_convert_fusion = bf16[512,384]{1,0:T(8,128)(2,1)} fusion(bf16[512,4096]{1,0:T(8,128)(2,1)} %all-gather.3.cloned.1.call-done, bf16[4096,384]{1,0:T(8,128)(2,1)} %all-gather.5.cloned.1.call-done), kind=kOutput, calls=%fused_computation | convolution fusion | flops 1610809344 | bytes 7733248 | tf_op jit(solution)/shard_map/dot_general | solution.py:290
  122.4 4.9 %all-to-all-start = ((bf16[8,64,384]{2,1,0:T(8,128)(2,1)}), bf16[8,64,384]{2,1,0:T(8,128)(2,1)S(1)}, u32[]{:S(2)}, u32[]{:S(2)}) async-start(bf16[8,64,384]{2,1,0:T(8,128)(2,1)} %bitcast.30), calls=%async_computation | async-start | bytes 786432 | tf_op jit(solution)/shard_map/all_to_all | solution.py:291
  128.3 7.2 %all-to-all-done.proj = bf16[8,64,384]{2,1,0:T(8,128)(2,1)S(1)} async-done(((bf16[8,64,384]{2,1,0:T(8,128)(2,1)}), bf16[8,64,384]{2,1,0:T(8,128)(2,1)S(1)}, u32[]{:S(2)}, u32[]{:S(2)}) %all-to-all-start) | async-done | bytes 393248 | tf_op jit(solution)/shard_map/all_to_all | solution.py:291
  135.5 0.9 shard_map.87
  136.4 2.7 %collective-permute-start.11 = (bf16[64,2176]{1,0:T(8,128)(2,1)}, bf16[64,2176]{1,0:T(8,128)(2,1)S(1)}, u32[]{:S(2)}, u32[]{:S(2)}) collective-permute-start(bf16[64,2176]{1,0:T(8,128)(2,1)} %get-tuple-element.35.q0), channel_id=1, source_target_pairs={{1,0},{2,1},{3,2},{4,3},{5,4},{6,5},{7,6},{8,7},{9,8},{10,9},{11,1... | collective-permute-start | bytes 835592 | tf_op jit(solution)/shard_map/ppermute | solution.py:316
  139.1 4.7 %collective-permute-start.12 = (bf16[64,2176]{1,0:T(8,128)(2,1)}, bf16[64,2176]{1,0:T(8,128)(2,1)}, u32[]{:S(2)}, u32[]{:S(2)}) collective-permute-start(bf16[64,2176]{1,0:T(8,128)(2,1)} %get-tuple-element.35.q0), channel_id=1, source_target_pairs={{2,0},{3,1},{4,2},{5,3},{6,4},{7,5},{8,6},{9,7},{10,8},{11,9},{12,... | collective-permute-start | bytes 835592 | tf_op jit(solution)/shard_map/ppermute | solution.py:316
  145.0 1.1 copy-done.4
  146.1 5.7 %shard_map.88 = (bf16[1024,1024]{1,0:T(8,128)(2,1)}, bf16[1024,1024]{1,0:T(8,128)(2,1)S(1)}, f32[64,2048]{1,0:T(8,128)S(1)}, f32[64,128]{1,0:T(8,128)S(1)}) custom-call(s32[8,8]{1,0:T(8,128)S(1)} %copy-done.8, s32[1]{0:T(128)} %bitcast.me, f32[8,128]{1,0:T(8,128)S(1)} %get-tuple-element.64.kcos, f32[8,128]{1,0:T(8,128)S(1)} %get-tuple-element.65.ksin, ...), custom_call_target="tpu_custom_call" | custom-call | flops 536870912 | bytes 6291456 | tf_op jit(solution)/shard_map/pallas_call | solution.py:319
  152.6 4.0 %shard_map.89 = (bf16[64,2176]{1,0:T(8,128)(2,1)S(1)}, bf16[64,2176]{1,0:T(8,128)(2,1)S(1)}) custom-call(bf16[64,2176]{1,0:T(8,128)(2,1)S(1)} %collective-permute-done.11.q1, bf16[64,2176]{1,0:T(8,128)(2,1)} %collective-permute-done.12.q2, bf16[1024,1024]{1,0:T(8,128)(2,1)S(1)} %get-tuple-element.44.kv), custom_call_target="tpu_custom_call" | custom-call | flops 1073741824 | bytes 2097152 | tf_op jit(solution)/shard_map/pallas_call | solution.py:340
  156.6 13.2 %collective-permute-start.13 = (bf16[64,2176]{1,0:T(8,128)(2,1)S(1)}, bf16[64,2176]{1,0:T(8,128)(2,1)S(1)}, u32[]{:S(2)}, u32[]{:S(2)}) collective-permute-start(bf16[64,2176]{1,0:T(8,128)(2,1)S(1)} %get-tuple-element.45), channel_id=1, source_target_pairs={{0,1},{1,2},{2,3},{3,4},{4,5},{5,6},{6,7},{7,8},{8,9},{9,10},{10,1... | collective-permute-start | bytes 835592 | tf_op jit(solution)/shard_map/ppermute | solution.py:316
  169.8 1.9 %collective-permute-start.14 = (bf16[64,2176]{1,0:T(8,128)(2,1)S(1)}, bf16[64,2176]{1,0:T(8,128)(2,1)S(1)}, u32[]{:S(2)}, u32[]{:S(2)}) collective-permute-start(bf16[64,2176]{1,0:T(8,128)(2,1)S(1)} %get-tuple-element.46), channel_id=1, source_target_pairs={{0,2},{1,3},{2,4},{3,5},{4,6},{5,7},{6,8},{7,9},{8,10},{9,11},{10,... | collective-permute-start | bytes 835592 | tf_op jit(solution)/shard_map/ppermute | solution.py:316
  171.8 1.9 collective-permute-done.13.r1
  173.7 6.8 %collective-permute-done.14.r2 = bf16[64,2176]{1,0:T(8,128)(2,1)S(1)} collective-permute-done((bf16[64,2176]{1,0:T(8,128)(2,1)S(1)}, bf16[64,2176]{1,0:T(8,128)(2,1)S(1)}, u32[]{:S(2)}, u32[]{:S(2)}) %collective-permute-start.14) | collective-permute-done | bytes 278560 | tf_op jit(solution)/shard_map/ppermute | solution.py:316
  180.5 1.0 shard_map.90
  (72 shorter events, 9.8 us)
Async XLA Ops:
  7.2 67.6 %copy-start = (s32[8,32]{1,0:T(8,128)S(1)}, s32[8,32]{1,0:T(8,128)}, u32[]{:S(2)}) copy-start(s32[8,32]{1,0:T(8,128)} %param.11) | copy-start | bytes 3076
  7.2 67.4 %copy-start.13 = (s32[1,8,8]{2,1,0:T(8,128)S(1)}, s32[1,8,8]{2,1,0:T(8,128)}, u32[]{:S(2)}) copy-start(s32[1,8,8]{2,1,0:T(8,128)} %param.12) | copy-start | bytes 772
  7.2 59.8 %all-gather.3.cloned.1.call-start = ((), (), s32[]{:S(2)}) async-start(), calls=%async_computation.1 | async-start | bytes 4718592 | tf_op jit(solution)/shard_map/all_gather | solution.py:284
  7.9 108.2 %all-gather.5.cloned.1.call-start = ((), (), s32[]{:S(2)}) async-start(), calls=%async_computation.2 | async-start | bytes 3538944 | tf_op jit(solution)/shard_map/all_gather | solution.py:286
  8.0 1.6 copy-start.1
  12.1 0.8 copy-start.9
  12.9 0.8 copy-start.10
  13.7 19.6 %collective-permute-start = (bf16[64,384]{1,0:T(8,128)(2,1)}, bf16[64,384]{1,0:T(8,128)(2,1)S(1)}, u32[]{:S(2)}, u32[]{:S(2)}) collective-permute-start(bf16[64,384]{1,0:T(8,128)(2,1)} %param.8), channel_id=1, source_target_pairs={{0,0},{1,64},{2,128},{3,192},{4,256},{5,320},{6,384},{7,448},{64,1... | collective-permute-start | bytes 147464 | tf_op jit(solution)/shard_map/ppermute | solution.py:271
  17.9 15.5 %collective-permute-start.1 = (bf16[64,384]{1,0:T(8,128)(2,1)}, bf16[64,384]{1,0:T(8,128)(2,1)S(1)}, u32[]{:S(2)}, u32[]{:S(2)}) collective-permute-start(bf16[64,384]{1,0:T(8,128)(2,1)} %param.8), channel_id=1, source_target_pairs={{0,256},{1,320},{2,384},{3,448},{4,0},{5,64},{6,128},{7,192},{64,2... | collective-permute-start | bytes 147464 | tf_op jit(solution)/shard_map/ppermute | solution.py:271
  25.1 8.2 %collective-permute-start.2 = (bf16[64,384]{1,0:T(8,128)(2,1)}, bf16[64,384]{1,0:T(8,128)(2,1)S(1)}, u32[]{:S(2)}, u32[]{:S(2)}) collective-permute-start(bf16[64,384]{1,0:T(8,128)(2,1)} %param.8), channel_id=1, source_target_pairs={{0,128},{1,192},{2,0},{3,64},{4,384},{5,448},{6,256},{7,320},{64,1... | collective-permute-start | bytes 147464 | tf_op jit(solution)/shard_map/ppermute | solution.py:271
  28.5 8.4 %collective-permute-start.3 = (bf16[64,384]{1,0:T(8,128)(2,1)}, bf16[64,384]{1,0:T(8,128)(2,1)S(1)}, u32[]{:S(2)}, u32[]{:S(2)}) collective-permute-start(bf16[64,384]{1,0:T(8,128)(2,1)} %param.8), channel_id=1, source_target_pairs={{0,384},{1,448},{2,256},{3,320},{4,128},{5,192},{6,0},{7,64},{64,3... | collective-permute-start | bytes 147464 | tf_op jit(solution)/shard_map/ppermute | solution.py:271
  37.0 7.6 %collective-permute-start.4 = (bf16[2,2,64,384]{3,2,1,0:T(8,128)(2,1)S(1)}, bf16[2,2,64,384]{3,2,1,0:T(8,128)(2,1)S(1)}, u32[]{:S(2)}, u32[]{:S(2)}) collective-permute-start(bf16[2,2,64,384]{3,2,1,0:T(8,128)(2,1)S(1)} %pad_maximum_fusion.1), channel_id=1, source_target_pairs={{0,64},{64,0},{128,192},{192,128},{256,320},{320,256},{384,448},{4... | collective-permute-start | bytes 589832 | tf_op jit(solution)/shard_map/ppermute | solution.py:280
  45.5 20.5 %collective-permute-start.5 = (bf16[3,128,1024]{2,1,0:T(8,128)(2,1)S(1)}, bf16[3,128,1024]{2,1,0:T(8,128)(2,1)S(1)}, u32[]{:S(2)}, u32[]{:S(2)}) collective-permute-start(bf16[3,128,1024]{2,1,0:T(8,128)(2,1)S(1)} %get-tuple-element.30), channel_id=1, source_target_pairs={{0,64},{64,128},{128,192},{192,256},{256,320},{320,384},{384,448},... | collective-permute-start | bytes 2359304 | tf_op jit(solution)/shard_map/ppermute | solution.py:255
  48.0 19.0 %collective-permute-start.6 = (bf16[3,128,1024]{2,1,0:T(8,128)(2,1)S(1)}, bf16[3,128,1024]{2,1,0:T(8,128)(2,1)S(1)}, u32[]{:S(2)}, u32[]{:S(2)}) collective-permute-start(bf16[3,128,1024]{2,1,0:T(8,128)(2,1)S(1)} %get-tuple-element.31), channel_id=1, source_target_pairs={{0,448},{64,0},{128,64},{192,128},{256,192},{320,256},{384,320},{4... | collective-permute-start | bytes 2359304 | tf_op jit(solution)/shard_map/ppermute | solution.py:255
  67.0 13.9 %copy-start.3 = (bf16[3,128,1024]{2,1,0:T(8,128)(2,1)}, bf16[3,128,1024]{2,1,0:T(8,128)(2,1)S(1)}, u32[]{:S(2)}) copy-start(bf16[3,128,1024]{2,1,0:T(8,128)(2,1)S(1)} %collective-permute-done.6.one_down) | copy-start | bytes 2359300
  67.0 72.1 %collective-permute-start.7 = (bf16[2,128,1024]{2,1,0:T(8,128)(2,1)}, bf16[2,128,1024]{2,1,0:T(8,128)(2,1)}, u32[]{:S(2)}, u32[]{:S(2)}) collective-permute-start(bf16[2,128,1024]{2,1,0:T(8,128)(2,1)} %copy-done.10), channel_id=1, source_target_pairs={{0,128},{64,192},{128,256},{192,320},{256,384},{320,448},{384,0},{... | collective-permute-start | bytes 1572872 | tf_op jit(solution)/shard_map/ppermute | solution.py:255
  70.3 74.6 %collective-permute-start.8 = (bf16[2,128,1024]{2,1,0:T(8,128)(2,1)}, bf16[2,128,1024]{2,1,0:T(8,128)(2,1)}, u32[]{:S(2)}, u32[]{:S(2)}) collective-permute-start(bf16[2,128,1024]{2,1,0:T(8,128)(2,1)} %copy-done.9), channel_id=1, source_target_pairs={{0,384},{64,448},{128,0},{192,64},{256,128},{320,192},{384,256},{4... | collective-permute-start | bytes 1572872 | tf_op jit(solution)/shard_map/ppermute | solution.py:255
  76.6 68.3 %collective-permute-start.10 = (bf16[3,128,1024]{2,1,0:T(8,128)(2,1)}, bf16[3,128,1024]{2,1,0:T(8,128)(2,1)}, u32[]{:S(2)}, u32[]{:S(2)}) collective-permute-start(bf16[3,128,1024]{2,1,0:T(8,128)(2,1)} %slice_dynamic-update-slice_fusion), channel_id=1, source_target_pairs={{0,320},{64,384},{128,448},{192,0},{256,64},{320,128},{384,192},{4... | collective-permute-start | bytes 2359304 | tf_op jit(solution)/shard_map/ppermute | solution.py:255
  81.7 46.4 %copy-start.11 = (f32[64,64]{1,0:T(8,128)S(1)}, f32[64,64]{1,0:T(8,128)}, u32[]{:S(2)}) copy-start(f32[64,64]{1,0:T(8,128)} %get-tuple-element.57) | copy-start | bytes 49156
  81.7 46.4 %copy-start.12 = (f32[64,64]{1,0:T(8,128)S(1)}, f32[64,64]{1,0:T(8,128)}, u32[]{:S(2)}) copy-start(f32[64,64]{1,0:T(8,128)} %get-tuple-element.58) | copy-start | bytes 49156
  81.7 46.5 %copy-start.14 = (s32[1,8]{1,0:T(1,128)S(1)}, s32[1,8]{1,0:T(1,128)}, u32[]{:S(2)}) copy-start(s32[1,8]{1,0:T(1,128)} %param.13) | copy-start | bytes 100
  81.7 63.3 %copy-start.2 = (bf16[1,1024,1024]{2,1,0:T(8,128)(2,1)S(1)}, bf16[1,1024,1024]{2,1,0:T(8,128)(2,1)}, u32[]{:S(2)}) copy-start(bf16[1,1024,1024]{2,1,0:T(8,128)(2,1)} %param.9) | copy-start | bytes 6291460
  81.7 63.3 %copy-start.8 = (s32[8,8]{1,0:T(8,128)S(1)}, s32[8,8]{1,0:T(8,128)}, u32[]{:S(2)}) copy-start(s32[8,8]{1,0:T(8,128)} %owner.3) | copy-start | bytes 772
  81.7 63.2 %collective-permute-start.9 = (bf16[3,128,1024]{2,1,0:T(8,128)(2,1)}, bf16[3,128,1024]{2,1,0:T(8,128)(2,1)}, u32[]{:S(2)}, u32[]{:S(2)}) collective-permute-start(bf16[3,128,1024]{2,1,0:T(8,128)(2,1)} %slice_dynamic-update-slice_fusion.1), channel_id=1, source_target_pairs={{0,192},{64,256},{128,320},{192,384},{256,448},{320,0},{384,64},{4... | collective-permute-start | bytes 2359304 | tf_op jit(solution)/shard_map/ppermute | solution.py:255
  122.4 13.1 %all-to-all-start = ((bf16[8,64,384]{2,1,0:T(8,128)(2,1)}), bf16[8,64,384]{2,1,0:T(8,128)(2,1)S(1)}, u32[]{:S(2)}, u32[]{:S(2)}) async-start(bf16[8,64,384]{2,1,0:T(8,128)(2,1)} %bitcast.30), calls=%async_computation | async-start | bytes 786432 | tf_op jit(solution)/shard_map/all_to_all | solution.py:291
  136.4 16.2 %collective-permute-start.11 = (bf16[64,2176]{1,0:T(8,128)(2,1)}, bf16[64,2176]{1,0:T(8,128)(2,1)S(1)}, u32[]{:S(2)}, u32[]{:S(2)}) collective-permute-start(bf16[64,2176]{1,0:T(8,128)(2,1)} %get-tuple-element.35.q0), channel_id=1, source_target_pairs={{1,0},{2,1},{3,2},{4,3},{5,4},{6,5},{7,6},{8,7},{9,8},{10,9},{11,1... | collective-permute-start | bytes 835592 | tf_op jit(solution)/shard_map/ppermute | solution.py:316
  139.1 13.5 %collective-permute-start.12 = (bf16[64,2176]{1,0:T(8,128)(2,1)}, bf16[64,2176]{1,0:T(8,128)(2,1)}, u32[]{:S(2)}, u32[]{:S(2)}) collective-permute-start(bf16[64,2176]{1,0:T(8,128)(2,1)} %get-tuple-element.35.q0), channel_id=1, source_target_pairs={{2,0},{3,1},{4,2},{5,3},{6,4},{7,5},{8,6},{9,7},{10,8},{11,9},{12,... | collective-permute-start | bytes 835592 | tf_op jit(solution)/shard_map/ppermute | solution.py:316
  145.0 1.1 copy-start.4
  151.8 0.8 copy-start.5
  152.6 27.9 %copy-start.6 = (f32[64,2048]{1,0:T(8,128)S(1)}, f32[64,2048]{1,0:T(8,128)}, u32[]{:S(2)}) copy-start(f32[64,2048]{1,0:T(8,128)} %copy-done.5) | copy-start | bytes 1572868
  156.6 17.1 %collective-permute-start.13 = (bf16[64,2176]{1,0:T(8,128)(2,1)S(1)}, bf16[64,2176]{1,0:T(8,128)(2,1)S(1)}, u32[]{:S(2)}, u32[]{:S(2)}) collective-permute-start(bf16[64,2176]{1,0:T(8,128)(2,1)S(1)} %get-tuple-element.45), channel_id=1, source_target_pairs={{0,1},{1,2},{2,3},{3,4},{4,5},{5,6},{6,7},{7,8},{8,9},{9,10},{10,1... | collective-permute-start | bytes 835592 | tf_op jit(solution)/shard_map/ppermute | solution.py:316
  169.8 10.6 %collective-permute-start.14 = (bf16[64,2176]{1,0:T(8,128)(2,1)S(1)}, bf16[64,2176]{1,0:T(8,128)(2,1)S(1)}, u32[]{:S(2)}, u32[]{:S(2)}) collective-permute-start(bf16[64,2176]{1,0:T(8,128)(2,1)S(1)} %get-tuple-element.46), channel_id=1, source_target_pairs={{0,2},{1,3},{2,4},{3,5},{4,6},{5,7},{6,8},{7,9},{8,10},{9,11},{10,... | collective-permute-start | bytes 835592 | tf_op jit(solution)/shard_map/ppermute | solution.py:316
  (1 other events, 0.7 us)
Sparse Core Ops, SparseCore 0:
  10.2 40.6 all-gather.2
  67.1 48.9 all-gather.4

commit v3 on v2

--- a/solution.py
+++ b/solution.py
@@ -20,7 +20,7 @@
 BF = jnp.bfloat16
 VM = pl.BlockSpec(memory_space=pltpu.VMEM)
 SM = pl.BlockSpec(memory_space=pltpu.SMEM)
-ANY = pl.BlockSpec(memory_space=pl.ANY)
+ANY = pl.BlockSpec(memory_space=pltpu.HBM)
 
 
 def call(kernel, out, ins, outs, scratch=(), flops=0, moved=0, vmem=8):
@@ -35,12 +35,16 @@
     )
 
 
-def pick_kernel(owner, me, pool, one_up, one_down, two_up, two_down, three_up, three_down, kept, sem):
+def kept(*arrays):
+    return [pltpu.with_memory_space_constraint(a, pltpu.HBM) for a in arrays]
+
+
+def pick_kernel(owner, me, pool, one_up, one_down, two_up, two_down, three_up, three_down, stays, sem):
     traces, blocks = owner.shape
     rows = pool.shape[0] // blocks
     mine = me[0]
     for slot in range(blocks):
-        kept[slot] = 0
+        stays[slot] = 0
     slots = {
         1: (one_up.at[0], one_up.at[1]),
         2: (two_up.at[0], two_up.at[1]),
@@ -68,16 +72,33 @@
 
                 @pl.when(hit)
                 def _(slot=slot):
-                    kept[slot] = 1
+                    stays[slot] = 1
 
             count = count + hit.astype(jnp.int32)
     for slot in range(blocks):
 
-        @pl.when(kept[slot] == 0)
+        @pl.when(stays[slot] == 0)
         def _(slot=slot):
             pltpu.make_async_copy(
                 pool.at[pl.ds(slot * rows, rows)], two_up.at[0], sem.at[slot]
             ).wait()
+
+
+def project_kernel(hidden, w, out, total):
+    step = pl.program_id(0)
+    product = jnp.dot(hidden[...], w[...], preferred_element_type=F32)
+
+    @pl.when(step == 0)
+    def _():
+        total[...] = product
+
+    @pl.when(step > 0)
+    def _():
+        total[...] += product
+
+    @pl.when(step == pl.num_programs(0) - 1)
+    def _():
+        out[...] = total[...].astype(BF).reshape(out.shape)
 
 
 def head(ref, n):
@@ -139,9 +160,9 @@
 
 
 def blend_kernel(
-    owner, me, kcos, ksin, spots, fresh, q0,
+    owner, me, kcos, ksin, spots, fresh,
     pool, one_up, one_down, two_up, two_down, three_up, three_down,
-    blended, kv, num0, den0, stack, sem, out_sem,
+    blended, kv, sem, out_sem,
 ):
     traces, blocks = owner.shape
     rows = kv.shape[0] // blocks
@@ -175,8 +196,8 @@
                 def _(b=b, here=here, block=slots[far][nth]):
                     pltpu.make_async_copy(block, here, sem.at[b]).start()
 
-    tokens, width = kv.shape
-    n_q = q0.shape[0]
+    width = kv.shape[1]
+    n_q = fresh.shape[0]
     ones = jnp.ones((n_q, HD), BF)
     for b in range(blocks):
         here = pl.ds(b * rows, rows)
@@ -192,15 +213,20 @@
             placed = jnp.dot(hits, fresh[:, cols], preferred_element_type=F32)
             kv[here, cols] = jnp.where(chosen, placed, x).astype(BF)
         pltpu.make_async_copy(kv.at[here], blended.at[here], out_sem.at[b]).start()
-    key = lax.broadcasted_iota(jnp.int32, (n_q, tokens), 1)
-
-    def put(i, cols, num):
-        num0[:, cols] = num
-
-    (den0[...],) = attend([q0], kv, stack, [key <= token_of(q0, tokens)], put)
     for b in range(blocks):
         here = pl.ds(b * rows, rows)
         pltpu.make_async_copy(kv.at[here], blended.at[here], out_sem.at[b]).wait()
+
+
+def own_kernel(q0, kv, num0, den0, stack):
+    tokens = kv.shape[0]
+    n_q = q0.shape[0]
+    key = lax.broadcasted_iota(jnp.int32, (n_q, tokens), 1)
+
+    def put(i, cols, num):
+        num0[:, cols] = num
+
+    (den0[...],) = attend([q0], kv, stack, [key <= token_of(q0, tokens)], put)
 
 
 def remote_kernel(q1, q2, kv, p1, p2, stack):
@@ -251,11 +277,15 @@
     cols = w_qkv.shape[1]
     me = y.reshape(1).astype(jnp.int32)
 
+    def around(array, axis, by):
+        n = lax.axis_size(axis)
+        return lax.ppermute(array, axis, [(i, (i + by) % n) for i in range(n)])
+
     def turned(array, by):
-        return lax.ppermute(array, "y", [(i, (i + by) % ny) for i in range(ny)])
+        return around(array, "y", by)
 
     def room(n):
-        return jax.ShapeDtypeStruct((n, block_len, kvw), BF)
+        return pltpu.HBM((n, block_len, kvw), BF)
 
     one_up, one_down, two_up, two_down, three_up, three_down = call(
         pick_kernel,
@@ -263,22 +293,13 @@
         [SM, SM, ANY], (ANY,) * 6,
         [pltpu.SMEM((blocks,), jnp.int32), pltpu.SemaphoreType.DMA((blocks,))],
         moved=4 * tokens * kvw,
-    )(block_owner, me, cache_pool[0])
+    )(block_owner, me, *kept(cache_pool[0]))
     one_up, w_qkv = lax.optimization_barrier((one_up, w_qkv))
 
-    def crossed(m):
-        pairs = [(a * group + b, (b ^ m) * group + a) for a in range(ny) for b in range(group)]
-        return lax.ppermute(w_qkv, ("y", "x", "c"), pairs)
-
-    def paired(mine, other, bit, axis):
-        low = (y // bit) % 2 == 0
-        return jnp.stack([jnp.where(low, mine, other), jnp.where(low, other, mine)], axis)
-
-    w = paired(
-        paired(crossed(0), crossed(4), 4, 0), paired(crossed(2), crossed(6), 4, 0), 2, 1
-    )
-    w = paired(w, lax.ppermute(w, "y", [(i, i ^ 1) for i in range(ny)]), 1, 2)
-    w = w.reshape(-1, cols)
+    pairs = [(a * group + b, b * group + a) for a in range(ny) for b in range(group)]
+    w = lax.ppermute(w_qkv, ("y", "x", "c"), pairs)
+    w = jnp.broadcast_to(w[None], (ny,) + w_qkv.shape)
+    w = lax.all_to_all(w, "y", 0, 0, tiled=True).reshape(-1, cols)
     w, one_up, one_down = lax.optimization_barrier((w, one_up, one_down))
     one_up, one_down = turned(one_up, 1), turned(one_down, -1)
     hidden = lax.all_gather(sel_hidden.reshape(rows, d), XC, axis=0, tiled=True)
@@ -287,8 +308,25 @@
     two_up, two_down = turned(two_up, 2), turned(two_down, -2)
     three_up = turned(lax.dynamic_update_slice(three_up, one_up[2:], (2, 0, 0)), 3)
     three_down = turned(lax.dynamic_update_slice(three_down, one_down[2:], (2, 0, 0)), -3)
-    projected = jnp.dot(hidden, w, preferred_element_type=F32).astype(BF)
-    merged = lax.all_to_all(projected.reshape(group, rows, cols), XC, 0, 0, tiled=True)
+    depth = 512
+    projected = pl.pallas_call(
+        project_kernel,
+        out_shape=jax.ShapeDtypeStruct((group, rows, cols), BF),
+        grid=(d // depth,),
+        in_specs=[
+            pl.BlockSpec((group * rows, depth), lambda i: (0, i)),
+            pl.BlockSpec((depth, cols), lambda i: (i, 0)),
+        ],
+        out_specs=pl.BlockSpec((group, rows, cols), lambda i: (0, 0, 0)),
+        scratch_shapes=[pltpu.VMEM((group * rows, cols), F32)],
+        compiler_params=pltpu.CompilerParams(vmem_limit_bytes=12 << 20),
+        cost_estimate=pl.CostEstimate(
+            flops=2 * group * rows * cols * d,
+            bytes_accessed=2 * d * (group * rows + cols),
+            transcendentals=0,
+        ),
+    )(*kept(hidden, w))
+    merged = lax.all_to_all(projected, XC, 0, 0, tiled=True)
 
     frequency = 1.0 / BASE ** (jnp.arange(HD // 2, dtype=F32) * 2.0 / HD)
     index = jnp.arange(blocks, dtype=jnp.int32)
@@ -316,26 +354,15 @@
         return lax.ppermute(array, SEQ, pairs)
 
     q1, q2 = along(queries, -1), along(queries, -2)
-    blended, kv, num0, den0 = call(
+    blended, kv = call(
         blend_kernel,
-        (
-            jax.ShapeDtypeStruct((tokens, kvw), BF),
-            jax.ShapeDtypeStruct((tokens, kvw), BF),
-            jax.ShapeDtypeStruct((rows, QH * HD), F32),
-            jax.ShapeDtypeStruct((rows, HD), F32),
-        ),
-        [SM, SM] + [VM] * 5 + [ANY] * 7, (ANY, VM, VM, VM),
-        [
-            pltpu.VMEM((1, GROUP * rows, HD), BF),
-            pltpu.SemaphoreType.DMA((blocks,)),
-            pltpu.SemaphoreType.DMA((blocks,)),
-        ],
-        flops=4 * rows * QH * HD * tokens,
+        (jax.ShapeDtypeStruct((tokens, kvw), BF),) * 2,
+        [SM, SM] + [VM] * 4 + [ANY] * 7, (ANY, VM),
+        [pltpu.SemaphoreType.DMA((blocks,)), pltpu.SemaphoreType.DMA((blocks,))],
         moved=6 * tokens * kvw,
-        vmem=20,
     )(
-        block_owner, me, kcos, ksin, spots, fresh, queries, cache_pool[0],
-        one_up, one_down, two_up, two_down, three_up, three_down,
+        block_owner, me, kcos, ksin, spots, fresh,
+        *kept(cache_pool[0], one_up, one_down, two_up, two_down, three_up, three_down),
     )
     p1, p2 = call(
         remote_kernel,
@@ -346,7 +373,17 @@
         moved=2 * tokens * kvw,
         vmem=20,
     )(q1, q2, kv)
+    whole, p1, p2 = lax.optimization_barrier((blended, p1, p2))
     r1, r2 = along(p1, 1), along(p2, 2)
+    num0, den0 = call(
+        own_kernel,
+        (jax.ShapeDtypeStruct((rows, QH * HD), F32), jax.ShapeDtypeStruct((rows, HD), F32)),
+        [VM] * 2, (VM, VM),
+        [pltpu.VMEM((1, GROUP * rows, HD), BF)],
+        flops=4 * rows * QH * HD * tokens,
+        moved=2 * tokens * kvw,
+        vmem=20,
+    )(queries, whole)
     attended = call(
         merge_kernel,
         jax.ShapeDtypeStruct((rows, QH * HD), BF),

time: 189 us -> 239 us (1.26)
  the two profiles are of different devices: /device:TPU:257 before, /device:TPU:112 now
where the time goes in v3:
time: 239 us; the launch traced here: 238 us
  waiting for transfers between devices  78.7 us (33%)
  Pallas kernels  68.1 us (28%)
  starting transfers between devices  56.1 us (23%)
  blocking collectives  17.3 us (7%)
  between operations  14.4 us (6%)
  local copies, waits for them, and re-layouts  2.84 us (1%)
    pallas_call x1, Pallas kernels, on_device(): call(pick_kernel, (room(3), room(3), room(2), room(2), room(3), room(3)),...  49.6 us
    all_gather x1, waiting for transfers between devices, on_device(): w = lax.all_gather(w, 'z', axis=0, tiled=True)  33.2 us
    ppermute x6, waiting for transfers between devices, around(): return lax.ppermute(array, axis, [(i, (i + by) % n) for i in range(n)])  23.8 us
    ppermute x6, starting transfers between devices, around(): return lax.ppermute(array, axis, [(i, (i + by) % n) for i in range(n)])  21.5 us
    ppermute x1, starting transfers between devices, on_device(): w = lax.ppermute(w_qkv, ('y', 'x', 'c'), pairs)  19.8 us
    all_to_all x1, blocking collectives, on_device(): w = lax.all_to_all(w, 'y', 0, 0, tiled=True).reshape(-1, cols)  17.3 us
    ppermute x4, starting transfers between devices, along(): return lax.ppermute(array, SEQ, pairs)  10.5 us
    ppermute x4, waiting for transfers between devices, along(): return lax.ppermute(array, SEQ, pairs)  8.65 us
  transfers between devices with their start and end apart: 14, of which 8 were waited for; matrix products, arithmetic and copies ran while one was open for 1% of the time, Pallas kernels for 27%

profile of v3, /device:TPU:112, one launch (start us, length us, event | category | flops | bytes accessed | tf_op | source)
XLA Modules:
  0.0 238.3 jit_solution(13607727920060282236)
XLA Ops:
  7.2 0.7 all-gather.3.cloned.1.call-update
  8.0 0.7 copy-done.2
  8.7 49.6 %shard_map.86 = (bf16[3,128,1024]{2,1,0:T(8,128)(2,1)}, bf16[3,128,1024]{2,1,0:T(8,128)(2,1)}, bf16[2,128,1024]{2,1,0:T(8,128)(2,1)}, bf16[2,128,1024]{2,1,0:T(8...) custom-call(s32[8,8]{1,0:T(8,128)S(1)} %copy-done.2, s32[1]{0:T(128)} %bitcast.me, ...), custom_call_target="tpu_custom_call" | custom-call | bytes 4194304 | tf_op jit(solution)/shard_map/pallas_call | solution.py:290
  58.3 19.8 %collective-permute-start = (bf16[64,384]{1,0:T(8,128)(2,1)S(1)}, bf16[64,384]{1,0:T(8,128)(2,1)S(1)}, u32[]{:S(2)}, u32[]{:S(2)}) collective-permute-start(bf16[64,384]{1,0:T(8,128)(2,1)S(1)} %copy-done.9), channel_id=1, source_target_pairs={{0,0},{1,64},{2,128},{3,192},{4,256},{5,320},{6,384},{7,448},{64,1... | collective-permute-start | bytes 147464 | tf_op jit(solution)/shard_map/ppermute | solution.py:300
  78.0 3.7 %collective-permute-done = bf16[64,384]{1,0:T(8,128)(2,1)S(1)} collective-permute-done((bf16[64,384]{1,0:T(8,128)(2,1)S(1)}, bf16[64,384]{1,0:T(8,128)(2,1)S(1)}, u32[]{:S(2)}, u32[]{:S(2)}) %collective-permute-start) | collective-permute-done | bytes 49184 | tf_op jit(solution)/shard_map/ppermute | solution.py:300
  81.8 17.3 %all_to_all.10 = bf16[8,64,384]{2,1,0:T(8,128)(2,1)} all-to-all(bf16[8,64,384]{2,1,0:T(8,128)(2,1)S(1)} %broadcast_in_dim.34), channel_id=1, replica_groups=mesh['y'=8,'z'=8,'x'=4,'c'=2] {'y'}, dimensions={0} | all-to-all | bytes 786432 | tf_op jit(solution)/shard_map/all_to_all | solution.py:302
  99.1 1.9 collective-permute-start.1
  101.0 3.9 %collective-permute-start.2 = (bf16[3,128,1024]{2,1,0:T(8,128)(2,1)}, bf16[3,128,1024]{2,1,0:T(8,128)(2,1)S(1)}, u32[]{:S(2)}, u32[]{:S(2)}) collective-permute-start(bf16[3,128,1024]{2,1,0:T(8,128)(2,1)} %get-tuple-element.34), channel_id=1, source_target_pairs={{0,448},{64,0},{128,64},{192,128},{256,192},{320,256},{384,320},{4... | collective-permute-start | bytes 2359304 | tf_op jit(solution)/shard_map/ppermute | solution.py:282
  104.9 15.2 %collective-permute-done.1.one_up = bf16[3,128,1024]{2,1,0:T(8,128)(2,1)S(1)} collective-permute-done((bf16[3,128,1024]{2,1,0:T(8,128)(2,1)}, bf16[3,128,1024]{2,1,0:T(8,128)(2,1)S(1)}, u32[]{:S(2)}, u32[]{:S(2)}) %collective-permute-start.1) | collective-permute-done | bytes 786464 | tf_op jit(solution)/shard_map/ppermute | solution.py:282
  120.1 4.8 %collective-permute-done.2.one_down = bf16[3,128,1024]{2,1,0:T(8,128)(2,1)S(1)} collective-permute-done((bf16[3,128,1024]{2,1,0:T(8,128)(2,1)}, bf16[3,128,1024]{2,1,0:T(8,128)(2,1)S(1)}, u32[]{:S(2)}, u32[]{:S(2)}) %collective-permute-start.2) | collective-permute-done | bytes 786464 | tf_op jit(solution)/shard_map/ppermute | solution.py:282
  124.9 3.9 %collective-permute-start.3 = (bf16[2,128,1024]{2,1,0:T(8,128)(2,1)}, bf16[2,128,1024]{2,1,0:T(8,128)(2,1)S(1)}, u32[]{:S(2)}, u32[]{:S(2)}) collective-permute-start(bf16[2,128,1024]{2,1,0:T(8,128)(2,1)} %get-tuple-element.41), channel_id=1, source_target_pairs={{0,128},{64,192},{128,256},{192,320},{256,384},{320,448},{384,0},{... | collective-permute-start | bytes 1572872 | tf_op jit(solution)/shard_map/ppermute | solution.py:282
  128.9 2.8 %collective-permute-start.4 = (bf16[2,128,1024]{2,1,0:T(8,128)(2,1)}, bf16[2,128,1024]{2,1,0:T(8,128)(2,1)}, u32[]{:S(2)}, u32[]{:S(2)}) collective-permute-start(bf16[2,128,1024]{2,1,0:T(8,128)(2,1)} %get-tuple-element.42), channel_id=1, source_target_pairs={{0,384},{64,448},{128,0},{192,64},{256,128},{320,192},{384,256},{4... | collective-permute-start | bytes 1572872 | tf_op jit(solution)/shard_map/ppermute | solution.py:282
  132.5 0.7 slice_dynamic-update-slice_fusion
  133.2 3.5 %collective-permute-start.6 = (bf16[3,128,1024]{2,1,0:T(8,128)(2,1)}, bf16[3,128,1024]{2,1,0:T(8,128)(2,1)}, u32[]{:S(2)}, u32[]{:S(2)}) collective-permute-start(bf16[3,128,1024]{2,1,0:T(8,128)(2,1)} %slice_dynamic-update-slice_fusion), channel_id=1, source_target_pairs={{0,320},{64,384},{128,448},{192,0},{256,64},{320,128},{384,192},{4... | collective-permute-start | bytes 2359304 | tf_op jit(solution)/shard_map/ppermute | solution.py:282
  136.7 0.7 slice_dynamic-update-slice_fusion.1
  137.4 5.5 %collective-permute-start.5 = (bf16[3,128,1024]{2,1,0:T(8,128)(2,1)}, bf16[3,128,1024]{2,1,0:T(8,128)(2,1)}, u32[]{:S(2)}, u32[]{:S(2)}) collective-permute-start(bf16[3,128,1024]{2,1,0:T(8,128)(2,1)} %slice_dynamic-update-slice_fusion.1), channel_id=1, source_target_pairs={{0,192},{64,256},{128,320},{192,384},{256,448},{320,0},{384,64},{4... | collective-permute-start | bytes 2359304 | tf_op jit(solution)/shard_map/ppermute | solution.py:282
  142.9 33.2 %all-gather.5.cloned.1.call-done.w = bf16[4096,384]{1,0:T(8,128)(2,1)} async-done(((bf16[512,384]{1,0:T(8,128)(2,1)}), bf16[4096,384]{1,0:T(8,128)(2,1)}) %all-gather.5.cloned.1.call-update) | async-done | bytes 3145744 | tf_op jit(solution)/shard_map/all_gather | solution.py:307
  176.2 8.2 %shard_map.87 = bf16[8,64,384]{2,1,0:T(8,128)(2,1)} custom-call(bf16[512,4096]{1,0:T(8,128)(2,1)} %all-gather.3.cloned.1.call-done.hidden, bf16[4096,384]{1,0:T(8,128)(2,1)} %all-gather.5.cloned.1.call-done.w), custom_call_target="tpu_custom_call" | custom-call | flops 1610612736 | bytes 7340032 | tf_op jit(solution)/shard_map/pallas_call | solution.py:312
  184.4 4.3 %all-to-all-start.1 = ((bf16[8,64,384]{2,1,0:T(8,128)(2,1)}), bf16[8,64,384]{2,1,0:T(8,128)(2,1)S(1)}, u32[]{:S(2)}, u32[]{:S(2)}) async-start(bf16[8,64,384]{2,1,0:T(8,128)(2,1)} %shard_map.87), calls=%async_computation.1 | async-start | bytes 786432 | tf_op jit(solution)/shard_map/all_to_all | solution.py:329
  189.0 8.6 %all-to-all-done.1.proj = bf16[8,64,384]{2,1,0:T(8,128)(2,1)S(1)} async-done(((bf16[8,64,384]{2,1,0:T(8,128)(2,1)}), bf16[8,64,384]{2,1,0:T(8,128)(2,1)S(1)}, u32[]{:S(2)}, u32[]{:S(2)}) %all-to-all-start.1) | async-done | bytes 393248 | tf_op jit(solution)/shard_map/all_to_all | solution.py:329
  197.6 0.2 shard_map.88
  197.8 2.8 %collective-permute-start.7 = (bf16[64,2176]{1,0:T(8,128)(2,1)S(1)}, bf16[64,2176]{1,0:T(8,128)(2,1)S(1)}, u32[]{:S(2)}, u32[]{:S(2)}) collective-permute-start(bf16[64,2176]{1,0:T(8,128)(2,1)S(1)} %get-tuple-element.37.q0), channel_id=1, source_target_pairs={{1,0},{2,1},{3,2},{4,3},{5,4},{6,5},{7,6},{8,7},{9,8},{10,9},{11,1... | collective-permute-start | bytes 835592 | tf_op jit(solution)/shard_map/ppermute | solution.py:354
  200.7 2.7 %collective-permute-start.8 = (bf16[64,2176]{1,0:T(8,128)(2,1)S(1)}, bf16[64,2176]{1,0:T(8,128)(2,1)S(1)}, u32[]{:S(2)}, u32[]{:S(2)}) collective-permute-start(bf16[64,2176]{1,0:T(8,128)(2,1)S(1)} %get-tuple-element.37.q0), channel_id=1, source_target_pairs={{2,0},{3,1},{4,2},{5,3},{6,4},{7,5},{8,6},{9,7},{10,8},{11,9},{12,... | collective-permute-start | bytes 835592 | tf_op jit(solution)/shard_map/ppermute | solution.py:354
  203.7 3.8 %collective-permute-done.6.three_down = bf16[3,128,1024]{2,1,0:T(8,128)(2,1)} collective-permute-done((bf16[3,128,1024]{2,1,0:T(8,128)(2,1)}, bf16[3,128,1024]{2,1,0:T(8,128)(2,1)}, u32[]{:S(2)}, u32[]{:S(2)}) %collective-permute-start.6) | collective-permute-done | bytes 786464 | tf_op jit(solution)/shard_map/ppermute | solution.py:282
  207.5 4.3 %shard_map.89 = (bf16[1024,1024]{1,0:T(8,128)(2,1)}, bf16[1024,1024]{1,0:T(8,128)(2,1)S(1)}) custom-call(s32[8,8]{1,0:T(8,128)S(1)} %copy-done.3, s32[1]{0:T(128)} %bitcast.me, f32[8,128]{1,0:T(8,128)S(1)} %get-tuple-element.64.kcos, f32[8,128]{1,0:T(8,128)S(1)} %get-tuple-element.65.ksin, s32[1,64]{1,0:T(1,128)S(1)} %add_select_fusion.spots, ...), custom_call_target="tpu_custom_call" | custom-call | bytes 6291456 | tf_op jit(solution)/shard_map/pallas_call | solution.py:357
  211.9 3.0 %shard_map.90 = (bf16[64,2176]{1,0:T(8,128)(2,1)S(1)}, bf16[64,2176]{1,0:T(8,128)(2,1)S(1)}) custom-call(bf16[64,2176]{1,0:T(8,128)(2,1)S(1)} %collective-permute-done.7.q1, bf16[64,2176]{1,0:T(8,128)(2,1)S(1)} %collective-permute-done.8.q2, bf16[1024,1024]{1,0:T(8,128)(2,1)S(1)} %get-tuple-element.46.kv), custom_call_target="tpu_custom_call" | custom-call | flops 1073741824 | bytes 2097152 | tf_op jit(solution)/shard_map/pallas_call | solution.py:367
  214.9 3.0 %collective-permute-start.10 = (bf16[64,2176]{1,0:T(8,128)(2,1)S(1)}, bf16[64,2176]{1,0:T(8,128)(2,1)S(1)}, u32[]{:S(2)}, u32[]{:S(2)}) collective-permute-start(bf16[64,2176]{1,0:T(8,128)(2,1)S(1)} %get-tuple-element.53), channel_id=1, source_target_pairs={{0,2},{1,3},{2,4},{3,5},{4,6},{5,7},{6,8},{7,9},{8,10},{9,11},{10,... | collective-permute-start | bytes 835592 | tf_op jit(solution)/shard_map/ppermute | solution.py:354
  217.9 1.9 collective-permute-start.9
  219.9 1.9 shard_map.91
  221.8 6.6 %collective-permute-done.10.r2 = bf16[64,2176]{1,0:T(8,128)(2,1)S(1)} collective-permute-done((bf16[64,2176]{1,0:T(8,128)(2,1)S(1)}, bf16[64,2176]{1,0:T(8,128)(2,1)S(1)}, u32[]{:S(2)}, u32[]{:S(2)}) %collective-permute-start.10) | collective-permute-done | bytes 278560 | tf_op jit(solution)/shard_map/ppermute | solution.py:354
  228.4 2.0 collective-permute-done.9.r1
  230.4 1.0 shard_map.92
  (51 shorter events, 1.7 us)
Async XLA Ops:
  7.2 124.8 %copy-start = (s32[8,32]{1,0:T(8,128)S(1)}, s32[8,32]{1,0:T(8,128)}, u32[]{:S(2)}) copy-start(s32[8,32]{1,0:T(8,128)} %param.11) | copy-start | bytes 3076
  7.2 51.1 %copy-start.9 = (bf16[64,384]{1,0:T(8,128)(2,1)S(1)}, bf16[64,384]{1,0:T(8,128)(2,1)}, u32[]{:S(2)}) copy-start(bf16[64,384]{1,0:T(8,128)(2,1)} %param.8) | copy-start | bytes 147460
  7.2 117.7 %all-gather.3.cloned.1.call-start = ((), (), s32[]{:S(2)}) async-start(), calls=%async_computation.2 | async-start | bytes 4718592 | tf_op jit(solution)/shard_map/all_gather | solution.py:305
  7.2 124.6 %copy-start.7 = (s32[1,8,8]{2,1,0:T(8,128)S(1)}, s32[1,8,8]{2,1,0:T(8,128)}, u32[]{:S(2)}) copy-start(s32[1,8,8]{2,1,0:T(8,128)} %param.12) | copy-start | bytes 772
  7.9 168.3 %all-gather.5.cloned.1.call-start = ((), (), s32[]{:S(2)}) async-start(), calls=%async_computation.3 | async-start | bytes 3538944 | tf_op jit(solution)/shard_map/all_gather | solution.py:307
  8.0 0.7 copy-start.2
  58.3 23.5 %collective-permute-start = (bf16[64,384]{1,0:T(8,128)(2,1)S(1)}, bf16[64,384]{1,0:T(8,128)(2,1)S(1)}, u32[]{:S(2)}, u32[]{:S(2)}) collective-permute-start(bf16[64,384]{1,0:T(8,128)(2,1)S(1)} %copy-done.9), channel_id=1, source_target_pairs={{0,0},{1,64},{2,128},{3,192},{4,256},{5,320},{6,384},{7,448},{64,1... | collective-permute-start | bytes 147464 | tf_op jit(solution)/shard_map/ppermute | solution.py:300
  99.1 21.0 %collective-permute-start.1 = (bf16[3,128,1024]{2,1,0:T(8,128)(2,1)}, bf16[3,128,1024]{2,1,0:T(8,128)(2,1)S(1)}, u32[]{:S(2)}, u32[]{:S(2)}) collective-permute-start(bf16[3,128,1024]{2,1,0:T(8,128)(2,1)} %get-tuple-element.33), channel_id=1, source_target_pairs={{0,64},{64,128},{128,192},{192,256},{256,320},{320,384},{384,448},... | collective-permute-start | bytes 2359304 | tf_op jit(solution)/shard_map/ppermute | solution.py:282
  101.0 23.9 %collective-permute-start.2 = (bf16[3,128,1024]{2,1,0:T(8,128)(2,1)}, bf16[3,128,1024]{2,1,0:T(8,128)(2,1)S(1)}, u32[]{:S(2)}, u32[]{:S(2)}) collective-permute-start(bf16[3,128,1024]{2,1,0:T(8,128)(2,1)} %get-tuple-element.34), channel_id=1, source_target_pairs={{0,448},{64,0},{128,64},{192,128},{256,192},{320,256},{384,320},{4... | collective-permute-start | bytes 2359304 | tf_op jit(solution)/shard_map/ppermute | solution.py:282
  120.1 64.3 %copy-start.4 = (bf16[3,128,1024]{2,1,0:T(8,128)(2,1)}, bf16[3,128,1024]{2,1,0:T(8,128)(2,1)S(1)}, u32[]{:S(2)}) copy-start(bf16[3,128,1024]{2,1,0:T(8,128)(2,1)S(1)} %collective-permute-done.1.one_up) | copy-start | bytes 2359300
  124.9 59.5 %copy-start.5 = (bf16[3,128,1024]{2,1,0:T(8,128)(2,1)}, bf16[3,128,1024]{2,1,0:T(8,128)(2,1)S(1)}, u32[]{:S(2)}) copy-start(bf16[3,128,1024]{2,1,0:T(8,128)(2,1)S(1)} %collective-permute-done.2.one_down) | copy-start | bytes 2359300
  124.9 75.8 %collective-permute-start.3 = (bf16[2,128,1024]{2,1,0:T(8,128)(2,1)}, bf16[2,128,1024]{2,1,0:T(8,128)(2,1)S(1)}, u32[]{:S(2)}, u32[]{:S(2)}) collective-permute-start(bf16[2,128,1024]{2,1,0:T(8,128)(2,1)} %get-tuple-element.41), channel_id=1, source_target_pairs={{0,128},{64,192},{128,256},{192,320},{256,384},{320,448},{384,0},{... | collective-permute-start | bytes 1572872 | tf_op jit(solution)/shard_map/ppermute | solution.py:282
  128.9 74.8 %collective-permute-start.4 = (bf16[2,128,1024]{2,1,0:T(8,128)(2,1)}, bf16[2,128,1024]{2,1,0:T(8,128)(2,1)}, u32[]{:S(2)}, u32[]{:S(2)}) collective-permute-start(bf16[2,128,1024]{2,1,0:T(8,128)(2,1)} %get-tuple-element.42), channel_id=1, source_target_pairs={{0,384},{64,448},{128,0},{192,64},{256,128},{320,192},{384,256},{4... | collective-permute-start | bytes 1572872 | tf_op jit(solution)/shard_map/ppermute | solution.py:282
  133.2 74.3 %collective-permute-start.6 = (bf16[3,128,1024]{2,1,0:T(8,128)(2,1)}, bf16[3,128,1024]{2,1,0:T(8,128)(2,1)}, u32[]{:S(2)}, u32[]{:S(2)}) collective-permute-start(bf16[3,128,1024]{2,1,0:T(8,128)(2,1)} %slice_dynamic-update-slice_fusion), channel_id=1, source_target_pairs={{0,320},{64,384},{128,448},{192,0},{256,64},{320,128},{384,192},{4... | collective-permute-start | bytes 2359304 | tf_op jit(solution)/shard_map/ppermute | solution.py:282
  137.4 51.5 %copy-start.8 = (s32[1,8]{1,0:T(1,128)S(1)}, s32[1,8]{1,0:T(1,128)}, u32[]{:S(2)}) copy-start(s32[1,8]{1,0:T(1,128)} %param.13) | copy-start | bytes 100
  137.4 70.1 %copy-start.3 = (s32[8,8]{1,0:T(8,128)S(1)}, s32[8,8]{1,0:T(8,128)}, u32[]{:S(2)}) copy-start(s32[8,8]{1,0:T(8,128)} %owner.3) | copy-start | bytes 772
  137.4 70.1 %collective-permute-start.5 = (bf16[3,128,1024]{2,1,0:T(8,128)(2,1)}, bf16[3,128,1024]{2,1,0:T(8,128)(2,1)}, u32[]{:S(2)}, u32[]{:S(2)}) collective-permute-start(bf16[3,128,1024]{2,1,0:T(8,128)(2,1)} %slice_dynamic-update-slice_fusion.1), channel_id=1, source_target_pairs={{0,192},{64,256},{128,320},{192,384},{256,448},{320,0},{384,64},{4... | collective-permute-start | bytes 2359304 | tf_op jit(solution)/shard_map/ppermute | solution.py:282
  184.4 13.2 %all-to-all-start.1 = ((bf16[8,64,384]{2,1,0:T(8,128)(2,1)}), bf16[8,64,384]{2,1,0:T(8,128)(2,1)S(1)}, u32[]{:S(2)}, u32[]{:S(2)}) async-start(bf16[8,64,384]{2,1,0:T(8,128)(2,1)} %shard_map.87), calls=%async_computation.1 | async-start | bytes 786432 | tf_op jit(solution)/shard_map/all_to_all | solution.py:329
  197.8 14.0 %collective-permute-start.7 = (bf16[64,2176]{1,0:T(8,128)(2,1)S(1)}, bf16[64,2176]{1,0:T(8,128)(2,1)S(1)}, u32[]{:S(2)}, u32[]{:S(2)}) collective-permute-start(bf16[64,2176]{1,0:T(8,128)(2,1)S(1)} %get-tuple-element.37.q0), channel_id=1, source_target_pairs={{1,0},{2,1},{3,2},{4,3},{5,4},{6,5},{7,6},{8,7},{9,8},{10,9},{11,1... | collective-permute-start | bytes 835592 | tf_op jit(solution)/shard_map/ppermute | solution.py:354
  200.7 6.9 %copy-start.6 = (bf16[2,128,1024]{2,1,0:T(8,128)(2,1)}, bf16[2,128,1024]{2,1,0:T(8,128)(2,1)S(1)}, u32[]{:S(2)}) copy-start(bf16[2,128,1024]{2,1,0:T(8,128)(2,1)S(1)} %collective-permute-done.3.two_up) | copy-start | bytes 1572868
  200.7 11.2 %collective-permute-start.8 = (bf16[64,2176]{1,0:T(8,128)(2,1)S(1)}, bf16[64,2176]{1,0:T(8,128)(2,1)S(1)}, u32[]{:S(2)}, u32[]{:S(2)}) collective-permute-start(bf16[64,2176]{1,0:T(8,128)(2,1)S(1)} %get-tuple-element.37.q0), channel_id=1, source_target_pairs={{2,0},{3,1},{4,2},{5,3},{6,4},{7,5},{8,6},{9,7},{10,8},{11,9},{12,... | collective-permute-start | bytes 835592 | tf_op jit(solution)/shard_map/ppermute | solution.py:354
  211.8 8.1 %copy-start.1 = (bf16[1024,1024]{1,0:T(8,128)(2,1)S(1)}, bf16[1024,1024]{1,0:T(8,128)(2,1)}, u32[]{:S(2)}) copy-start(bf16[1024,1024]{1,0:T(8,128)(2,1)} %get-tuple-element.49.kv) | copy-start | bytes 6291460
  214.9 13.5 %collective-permute-start.10 = (bf16[64,2176]{1,0:T(8,128)(2,1)S(1)}, bf16[64,2176]{1,0:T(8,128)(2,1)S(1)}, u32[]{:S(2)}, u32[]{:S(2)}) collective-permute-start(bf16[64,2176]{1,0:T(8,128)(2,1)S(1)} %get-tuple-element.53), channel_id=1, source_target_pairs={{0,2},{1,3},{2,4},{3,5},{4,6},{5,7},{6,8},{7,9},{8,10},{9,11},{10,... | collective-permute-start | bytes 835592 | tf_op jit(solution)/shard_map/ppermute | solution.py:354
  217.9 12.5 %collective-permute-start.9 = (bf16[64,2176]{1,0:T(8,128)(2,1)S(1)}, bf16[64,2176]{1,0:T(8,128)(2,1)S(1)}, u32[]{:S(2)}, u32[]{:S(2)}) collective-permute-start(bf16[64,2176]{1,0:T(8,128)(2,1)S(1)} %get-tuple-element.52), channel_id=1, source_target_pairs={{0,1},{1,2},{2,3},{3,4},{4,5},{5,6},{6,7},{7,8},{8,9},{9,10},{10,1... | collective-permute-start | bytes 835592 | tf_op jit(solution)/shard_map/ppermute | solution.py:354
Sparse Core Ops, SparseCore 0:
  10.2 40.8 all-gather.2
  125.0 51.0 all-gather.4

commit v4 on v3

--- a/solution.py
+++ b/solution.py
@@ -39,12 +39,17 @@
     return [pltpu.with_memory_space_constraint(a, pltpu.HBM) for a in arrays]
 
 
-def pick_kernel(owner, me, pool, one_up, one_down, two_up, two_down, three_up, three_down, stays, sem):
+def pick_kernel(owner, me, pool, one_up, one_down, two_up, two_down, three_up, three_down, stays, staged, sem, out_sem):
     traces, blocks = owner.shape
     rows = pool.shape[0] // blocks
     mine = me[0]
     for slot in range(blocks):
         stays[slot] = 0
+        here = pl.ds(slot * rows, rows)
+        pltpu.make_async_copy(pool.at[here], staged.at[here], sem.at[slot]).start()
+    for slot in range(blocks):
+        here = pl.ds(slot * rows, rows)
+        pltpu.make_async_copy(pool.at[here], staged.at[here], sem.at[slot]).wait()
     slots = {
         1: (one_up.at[0], one_up.at[1]),
         2: (two_up.at[0], two_up.at[1]),
@@ -66,7 +71,9 @@
                 @pl.when(hit & (count == nth))
                 def _(slot=slot, out=slots[d][nth]):
                     start = pl.multiple_of(slot * rows, rows)
-                    pltpu.make_async_copy(pool.at[pl.ds(start, rows)], out, sem.at[slot]).start()
+                    pltpu.make_async_copy(
+                        staged.at[pl.ds(start, rows)], out, out_sem.at[slot]
+                    ).start()
 
             if d == 0:
 
@@ -80,25 +87,8 @@
         @pl.when(stays[slot] == 0)
         def _(slot=slot):
             pltpu.make_async_copy(
-                pool.at[pl.ds(slot * rows, rows)], two_up.at[0], sem.at[slot]
+                staged.at[pl.ds(slot * rows, rows)], two_up.at[0], out_sem.at[slot]
             ).wait()
-
-
-def project_kernel(hidden, w, out, total):
-    step = pl.program_id(0)
-    product = jnp.dot(hidden[...], w[...], preferred_element_type=F32)
-
-    @pl.when(step == 0)
-    def _():
-        total[...] = product
-
-    @pl.when(step > 0)
-    def _():
-        total[...] += product
-
-    @pl.when(step == pl.num_programs(0) - 1)
-    def _():
-        out[...] = total[...].astype(BF).reshape(out.shape)
 
 
 def head(ref, n):
@@ -277,12 +267,8 @@
     cols = w_qkv.shape[1]
     me = y.reshape(1).astype(jnp.int32)
 
-    def around(array, axis, by):
-        n = lax.axis_size(axis)
-        return lax.ppermute(array, axis, [(i, (i + by) % n) for i in range(n)])
-
     def turned(array, by):
-        return around(array, "y", by)
+        return lax.ppermute(array, "y", [(i, (i + by) % ny) for i in range(ny)])
 
     def room(n):
         return pltpu.HBM((n, block_len, kvw), BF)
@@ -291,41 +277,44 @@
         pick_kernel,
         (room(3), room(3), room(2), room(2), room(3), room(3)),
         [SM, SM, ANY], (ANY,) * 6,
-        [pltpu.SMEM((blocks,), jnp.int32), pltpu.SemaphoreType.DMA((blocks,))],
+        [
+            pltpu.SMEM((blocks,), jnp.int32),
+            pltpu.VMEM((tokens, kvw), BF),
+            pltpu.SemaphoreType.DMA((blocks,)),
+            pltpu.SemaphoreType.DMA((blocks,)),
+        ],
         moved=4 * tokens * kvw,
     )(block_owner, me, *kept(cache_pool[0]))
     one_up, w_qkv = lax.optimization_barrier((one_up, w_qkv))
-
-    pairs = [(a * group + b, b * group + a) for a in range(ny) for b in range(group)]
-    w = lax.ppermute(w_qkv, ("y", "x", "c"), pairs)
-    w = jnp.broadcast_to(w[None], (ny,) + w_qkv.shape)
-    w = lax.all_to_all(w, "y", 0, 0, tiled=True).reshape(-1, cols)
+    one_up, one_down = turned(one_up, 1), turned(one_down, -1)
+
+    def crossed(m):
+        pairs = [(a * group + b, (b ^ m) * group + a) for a in range(ny) for b in range(group)]
+        return lax.ppermute(w_qkv, ("y", "x", "c"), pairs)
+
+    def paired(mine, other, bit, axis):
+        low = (y // bit) % 2 == 0
+        return jnp.stack([jnp.where(low, mine, other), jnp.where(low, other, mine)], axis)
+
+    w = paired(
+        paired(crossed(0), crossed(4), 4, 0), paired(crossed(2), crossed(6), 4, 0), 2, 1
+    )
     w, one_up, one_down = lax.optimization_barrier((w, one_up, one_down))
-    one_up, one_down = turned(one_up, 1), turned(one_down, -1)
+    w = paired(w, lax.ppermute(w, "y", [(i, i ^ 1) for i in range(ny)]), 1, 2).reshape(-1, cols)
+    w, two_up, two_down, one_up, one_down = lax.optimization_barrier(
+        (w, two_up, two_down, one_up, one_down)
+    )
     hidden = lax.all_gather(sel_hidden.reshape(rows, d), XC, axis=0, tiled=True)
-    w, hidden, one_up, one_down = lax.optimization_barrier((w, hidden, one_up, one_down))
+    w, hidden = lax.optimization_barrier((w, hidden))
     w = lax.all_gather(w, "z", axis=0, tiled=True)
     two_up, two_down = turned(two_up, 2), turned(two_down, -2)
+    two_up, two_down, three_up, three_down = lax.optimization_barrier(
+        (two_up, two_down, three_up, three_down)
+    )
     three_up = turned(lax.dynamic_update_slice(three_up, one_up[2:], (2, 0, 0)), 3)
     three_down = turned(lax.dynamic_update_slice(three_down, one_down[2:], (2, 0, 0)), -3)
-    depth = 512
-    projected = pl.pallas_call(
-        project_kernel,
-        out_shape=jax.ShapeDtypeStruct((group, rows, cols), BF),
-        grid=(d // depth,),
-        in_specs=[
-            pl.BlockSpec((group * rows, depth), lambda i: (0, i)),
-            pl.BlockSpec((depth, cols), lambda i: (i, 0)),
-        ],
-        out_specs=pl.BlockSpec((group, rows, cols), lambda i: (0, 0, 0)),
-        scratch_shapes=[pltpu.VMEM((group * rows, cols), F32)],
-        compiler_params=pltpu.CompilerParams(vmem_limit_bytes=12 << 20),
-        cost_estimate=pl.CostEstimate(
-            flops=2 * group * rows * cols * d,
-            bytes_accessed=2 * d * (group * rows + cols),
-            transcendentals=0,
-        ),
-    )(*kept(hidden, w))
+    projected = jnp.dot(hidden, w, preferred_element_type=F32).astype(BF)
+    projected = projected.reshape(group, rows, cols)
     merged = lax.all_to_all(projected, XC, 0, 0, tiled=True)
 
     frequency = 1.0 / BASE ** (jnp.arange(HD // 2, dtype=F32) * 2.0 / HD)

time: 239 us -> 186 us (0.78)
  the two profiles are of different devices: /device:TPU:112 before, /device:TPU:257 now
where the time goes in v4:
time: 186 us; the launch traced here: 185 us
  waiting for transfers between devices  77.7 us (42%)
  starting transfers between devices  68.4 us (37%)
  between operations  14.5 us (8%)
  Pallas kernels  13.9 us (7%)
  matrix products  6.24 us (3%)
  local copies, waits for them, and re-layouts  2.85 us (2%)
    ppermute x6, waiting for transfers between devices, turned(): return lax.ppermute(array, 'y', [(i, (i + by) % ny) for i in range(ny)])  43.8 us
    ppermute x6, starting transfers between devices, turned(): return lax.ppermute(array, 'y', [(i, (i + by) % ny) for i in range(ny)])  23.4 us
    ppermute x4, starting transfers between devices, crossed(): return lax.ppermute(w_qkv, ('y', 'x', 'c'), pairs)  22.8 us
    ppermute x4, starting transfers between devices, along(): return lax.ppermute(array, SEQ, pairs)  15.3 us
    all_to_all x1, waiting for transfers between devices, on_device(): merged = lax.all_to_all(projected, XC, 0, 0, tiled=True)  7.9 us
    ppermute x4, waiting for transfers between devices, along(): return lax.ppermute(array, SEQ, pairs)  7.48 us
    all_gather x1, waiting for transfers between devices, on_device(): w = lax.all_gather(w, 'z', axis=0, tiled=True)  6.77 us
    ppermute x4, waiting for transfers between devices, crossed(): return lax.ppermute(w_qkv, ('y', 'x', 'c'), pairs)  6.51 us
  transfers between devices with their start and end apart: 18, of which 10 were waited for; matrix products, arithmetic and copies ran while one was open for 5% of the time, Pallas kernels for 5%

profile of v4, /device:TPU:257, one launch (start us, length us, event | category | flops | bytes accessed | tf_op | source)
XLA Modules:
  0.0 185.4 jit_solution(5052807028001950393)
XLA Ops:
  8.7 3.6 %shard_map.86 = (bf16[3,128,1024]{2,1,0:T(8,128)(2,1)}, bf16[3,128,1024]{2,1,0:T(8,128)(2,1)}, bf16[2,128,1024]{2,1,0:T(8,128)(2,1)}, bf16[2,128,1024]{2,1,0:T(8...) custom-call(s32[8,8]{1,0:T(8,128)S(1)} %copy-done.2, s32[1]{0:T(128)} %bitcast.me, ...), custom_call_target="tpu_custom_call" | custom-call | bytes 4194304 | tf_op jit(solution)/shard_map/pallas_call | solution.py:276
  12.2 3.4 %collective-permute-start.4 = (bf16[3,128,1024]{2,1,0:T(8,128)(2,1)}, bf16[3,128,1024]{2,1,0:T(8,128)(2,1)S(1)}, u32[]{:S(2)}, u32[]{:S(2)}) collective-permute-start(bf16[3,128,1024]{2,1,0:T(8,128)(2,1)} %get-tuple-element.37), channel_id=1, source_target_pairs={{0,64},{64,128},{128,192},{192,256},{256,320},{320,384},{384,448},... | collective-permute-start | bytes 2359304 | tf_op jit(solution)/shard_map/ppermute | solution.py:271
  15.6 3.8 %collective-permute-start.5 = (bf16[3,128,1024]{2,1,0:T(8,128)(2,1)}, bf16[3,128,1024]{2,1,0:T(8,128)(2,1)S(1)}, u32[]{:S(2)}, u32[]{:S(2)}) collective-permute-start(bf16[3,128,1024]{2,1,0:T(8,128)(2,1)} %get-tuple-element.38), channel_id=1, source_target_pairs={{0,448},{64,0},{128,64},{192,128},{256,192},{320,256},{384,320},{4... | collective-permute-start | bytes 2359304 | tf_op jit(solution)/shard_map/ppermute | solution.py:271
  19.4 2.6 %collective-permute-start = (bf16[64,384]{1,0:T(8,128)(2,1)}, bf16[64,384]{1,0:T(8,128)(2,1)S(1)}, u32[]{:S(2)}, u32[]{:S(2)}) collective-permute-start(bf16[64,384]{1,0:T(8,128)(2,1)} %param.8), channel_id=1, source_target_pairs={{0,0},{1,64},{2,128},{3,192},{4,256},{5,320},{6,384},{7,448},{64,1... | collective-permute-start | bytes 147464 | tf_op jit(solution)/shard_map/ppermute | solution.py:293
  22.0 8.5 %collective-permute-start.1 = (bf16[64,384]{1,0:T(8,128)(2,1)}, bf16[64,384]{1,0:T(8,128)(2,1)S(1)}, u32[]{:S(2)}, u32[]{:S(2)}) collective-permute-start(bf16[64,384]{1,0:T(8,128)(2,1)} %param.8), channel_id=1, source_target_pairs={{0,256},{1,320},{2,384},{3,448},{4,0},{5,64},{6,128},{7,192},{64,2... | collective-permute-start | bytes 147464 | tf_op jit(solution)/shard_map/ppermute | solution.py:293
  30.5 2.8 %collective-permute-start.2 = (bf16[64,384]{1,0:T(8,128)(2,1)}, bf16[64,384]{1,0:T(8,128)(2,1)S(1)}, u32[]{:S(2)}, u32[]{:S(2)}) collective-permute-start(bf16[64,384]{1,0:T(8,128)(2,1)} %param.8), channel_id=1, source_target_pairs={{0,128},{1,192},{2,0},{3,64},{4,384},{5,448},{6,256},{7,320},{64,1... | collective-permute-start | bytes 147464 | tf_op jit(solution)/shard_map/ppermute | solution.py:293
  33.4 5.1 %collective-permute-done = bf16[64,384]{1,0:T(8,128)(2,1)S(1)} collective-permute-done((bf16[64,384]{1,0:T(8,128)(2,1)}, bf16[64,384]{1,0:T(8,128)(2,1)S(1)}, u32[]{:S(2)}, u32[]{:S(2)}) %collective-permute-start) | collective-permute-done | bytes 49184 | tf_op jit(solution)/shard_map/ppermute | solution.py:293
  38.4 9.0 %collective-permute-start.3 = (bf16[64,384]{1,0:T(8,128)(2,1)}, bf16[64,384]{1,0:T(8,128)(2,1)S(1)}, u32[]{:S(2)}, u32[]{:S(2)}) collective-permute-start(bf16[64,384]{1,0:T(8,128)(2,1)} %param.8), channel_id=1, source_target_pairs={{0,384},{1,448},{2,256},{3,320},{4,128},{5,192},{6,0},{7,64},{64,3... | collective-permute-start | bytes 147464 | tf_op jit(solution)/shard_map/ppermute | solution.py:293
  47.5 1.4 collective-permute-done.3
  49.0 1.9 %collective-permute-start.6 = (bf16[2,2,64,384]{3,2,1,0:T(8,128)(2,1)S(1)}, bf16[2,2,64,384]{3,2,1,0:T(8,128)(2,1)S(1)}, u32[]{:S(2)}, u32[]{:S(2)}) collective-permute-start(bf16[2,2,64,384]{3,2,1,0:T(8,128)(2,1)S(1)} %pad_maximum_fusion.1), channel_id=1, source_target_pairs={{0,64},{64,0},{128,192},{192,128},{256,320},{320,256},{384,448},{4... | collective-permute-start | bytes 589832 | tf_op jit(solution)/shard_map/ppermute | solution.py:303
  51.0 4.5 %collective-permute-done.6 = bf16[2,2,64,384]{3,2,1,0:T(8,128)(2,1)S(1)} collective-permute-done((bf16[2,2,64,384]{3,2,1,0:T(8,128)(2,1)S(1)}, bf16[2,2,64,384]{3,2,1,0:T(8,128)(2,1)S(1)}, u32[]{:S(2)}, u32[]{:S(2)}) %collective-permute-start.6) | collective-permute-done | bytes 196640 | tf_op jit(solution)/shard_map/ppermute | solution.py:303
  56.9 7.1 %collective-permute-start.7 = (bf16[2,128,1024]{2,1,0:T(8,128)(2,1)}, bf16[2,128,1024]{2,1,0:T(8,128)(2,1)S(1)}, u32[]{:S(2)}, u32[]{:S(2)}) collective-permute-start(bf16[2,128,1024]{2,1,0:T(8,128)(2,1)} %get-tuple-element.51), channel_id=1, source_target_pairs={{0,128},{64,192},{128,256},{192,320},{256,384},{320,448},{384,0},{... | collective-permute-start | bytes 1572872 | tf_op jit(solution)/shard_map/ppermute | solution.py:271
  64.0 1.9 %collective-permute-start.8 = (bf16[2,128,1024]{2,1,0:T(8,128)(2,1)S(1)}, bf16[2,128,1024]{2,1,0:T(8,128)(2,1)S(1)}, u32[]{:S(2)}, u32[]{:S(2)}) collective-permute-start(bf16[2,128,1024]{2,1,0:T(8,128)(2,1)S(1)} %copy-done.10), channel_id=1, source_target_pairs={{0,384},{64,448},{128,0},{192,64},{256,128},{320,192},{384,256},{4... | collective-permute-start | bytes 1572872 | tf_op jit(solution)/shard_map/ppermute | solution.py:271
  66.3 19.6 %collective-permute-done.7.two_up = bf16[2,128,1024]{2,1,0:T(8,128)(2,1)S(1)} collective-permute-done((bf16[2,128,1024]{2,1,0:T(8,128)(2,1)}, bf16[2,128,1024]{2,1,0:T(8,128)(2,1)S(1)}, u32[]{:S(2)}, u32[]{:S(2)}) %collective-permute-start.7) | collective-permute-done | bytes 524320 | tf_op jit(solution)/shard_map/ppermute | solution.py:271
  85.8 4.5 %collective-permute-done.8.two_down = bf16[2,128,1024]{2,1,0:T(8,128)(2,1)S(1)} collective-permute-done((bf16[2,128,1024]{2,1,0:T(8,128)(2,1)S(1)}, bf16[2,128,1024]{2,1,0:T(8,128)(2,1)S(1)}, u32[]{:S(2)}, u32[]{:S(2)}) %collective-permute-start.8) | collective-permute-done | bytes 524320 | tf_op jit(solution)/shard_map/ppermute | solution.py:271
  91.1 1.9 %collective-permute-start.10 = (bf16[3,128,1024]{2,1,0:T(8,128)(2,1)}, bf16[3,128,1024]{2,1,0:T(8,128)(2,1)}, u32[]{:S(2)}, u32[]{:S(2)}) collective-permute-start(bf16[3,128,1024]{2,1,0:T(8,128)(2,1)} %slice_dynamic-update-slice_fusion), channel_id=1, source_target_pairs={{0,320},{64,384},{128,448},{192,0},{256,64},{320,128},{384,192},{4... | collective-permute-start | bytes 2359304 | tf_op jit(solution)/shard_map/ppermute | solution.py:271
  93.8 5.3 %collective-permute-start.9 = (bf16[3,128,1024]{2,1,0:T(8,128)(2,1)}, bf16[3,128,1024]{2,1,0:T(8,128)(2,1)}, u32[]{:S(2)}, u32[]{:S(2)}) collective-permute-start(bf16[3,128,1024]{2,1,0:T(8,128)(2,1)} %slice_dynamic-update-slice_fusion.1), channel_id=1, source_target_pairs={{0,192},{64,256},{128,320},{192,384},{256,448},{320,0},{384,64},{4... | collective-permute-start | bytes 2359304 | tf_op jit(solution)/shard_map/ppermute | solution.py:271
  99.1 6.8 %all-gather.5.cloned.1.call-done = bf16[4096,384]{1,0:T(8,128)(2,1)} async-done(((bf16[512,384]{1,0:T(8,128)(2,1)}), bf16[4096,384]{1,0:T(8,128)(2,1)}) %all-gather.5.cloned.1.call-update) | async-done | bytes 3145744 | tf_op jit(solution)/shard_map/all_gather | solution.py:309
  105.8 6.2 %convolution_convert_fusion = bf16[512,384]{1,0:T(8,128)(2,1)} fusion(bf16[512,4096]{1,0:T(8,128)(2,1)} %all-gather.3.cloned.1.call-done, bf16[4096,384]{1,0:T(8,128)(2,1)} %all-gather.5.cloned.1.call-done), kind=kOutput, calls=%fused_computation | convolution fusion | flops 1610809344 | bytes 7733248 | tf_op jit(solution)/shard_map/dot_general | solution.py:316
  112.1 5.0 %all-to-all-start = ((bf16[8,64,384]{2,1,0:T(8,128)(2,1)}), bf16[8,64,384]{2,1,0:T(8,128)(2,1)S(1)}, u32[]{:S(2)}, u32[]{:S(2)}) async-start(bf16[8,64,384]{2,1,0:T(8,128)(2,1)} %bitcast.11), calls=%async_computation | async-start | bytes 786432 | tf_op jit(solution)/shard_map/all_to_all | solution.py:318
  117.3 7.9 %all-to-all-done.proj = bf16[8,64,384]{2,1,0:T(8,128)(2,1)S(1)} async-done(((bf16[8,64,384]{2,1,0:T(8,128)(2,1)}), bf16[8,64,384]{2,1,0:T(8,128)(2,1)S(1)}, u32[]{:S(2)}, u32[]{:S(2)}) %all-to-all-start) | async-done | bytes 393248 | tf_op jit(solution)/shard_map/all_to_all | solution.py:318
  125.5 2.7 %collective-permute-start.11 = (bf16[64,2176]{1,0:T(8,128)(2,1)S(1)}, bf16[64,2176]{1,0:T(8,128)(2,1)S(1)}, u32[]{:S(2)}, u32[]{:S(2)}) collective-permute-start(bf16[64,2176]{1,0:T(8,128)(2,1)S(1)} %get-tuple-element.47.q0), channel_id=1, source_target_pairs={{1,0},{2,1},{3,2},{4,3},{5,4},{6,5},{7,6},{8,7},{9,8},{10,9},{11,1... | collective-permute-start | bytes 835592 | tf_op jit(solution)/shard_map/ppermute | solution.py:343
  128.1 4.7 %collective-permute-start.12 = (bf16[64,2176]{1,0:T(8,128)(2,1)S(1)}, bf16[64,2176]{1,0:T(8,128)(2,1)S(1)}, u32[]{:S(2)}, u32[]{:S(2)}) collective-permute-start(bf16[64,2176]{1,0:T(8,128)(2,1)S(1)} %get-tuple-element.47.q0), channel_id=1, source_target_pairs={{2,0},{3,1},{4,2},{5,3},{6,4},{7,5},{8,6},{9,7},{10,8},{11,9},{12,... | collective-permute-start | bytes 835592 | tf_op jit(solution)/shard_map/ppermute | solution.py:343
  133.2 9.1 %collective-permute-done.10.three_down = bf16[3,128,1024]{2,1,0:T(8,128)(2,1)} collective-permute-done((bf16[3,128,1024]{2,1,0:T(8,128)(2,1)}, bf16[3,128,1024]{2,1,0:T(8,128)(2,1)}, u32[]{:S(2)}, u32[]{:S(2)}) %collective-permute-start.10) | collective-permute-done | bytes 786464 | tf_op jit(solution)/shard_map/ppermute | solution.py:271
  142.3 10.7 %collective-permute-done.9.three_up = bf16[3,128,1024]{2,1,0:T(8,128)(2,1)} collective-permute-done((bf16[3,128,1024]{2,1,0:T(8,128)(2,1)}, bf16[3,128,1024]{2,1,0:T(8,128)(2,1)}, u32[]{:S(2)}, u32[]{:S(2)}) %collective-permute-start.9) | collective-permute-done | bytes 786464 | tf_op jit(solution)/shard_map/ppermute | solution.py:271
  152.9 4.3 %shard_map.88 = (bf16[1024,1024]{1,0:T(8,128)(2,1)}, bf16[1024,1024]{1,0:T(8,128)(2,1)S(1)}) custom-call(s32[8,8]{1,0:T(8,128)S(1)} %copy-done.3, s32[1]{0:T(128)} %bitcast.me, f32[8,128]{1,0:T(8,128)S(1)} %get-tuple-element.86.kcos, f32[8,128]{1,0:T(8,128)S(1)} %get-tuple-element.87.ksin, s32[1,64]{1,0:T(1,128)S(1)} %add_select_fusion.spots, ...), custom_call_target="tpu_custom_call" | custom-call | bytes 6291456 | tf_op jit(solution)/shard_map/pallas_call | solution.py:346
  157.2 3.0 %shard_map.89 = (bf16[64,2176]{1,0:T(8,128)(2,1)S(1)}, bf16[64,2176]{1,0:T(8,128)(2,1)S(1)}) custom-call(bf16[64,2176]{1,0:T(8,128)(2,1)S(1)} %collective-permute-done.11.q1, bf16[64,2176]{1,0:T(8,128)(2,1)S(1)} %collective-permute-done.12.q2, bf16[1024,1024]{1,0:T(8,128)(2,1)S(1)} %get-tuple-element.60.kv), custom_call_target="tpu_custom_call" | custom-call | flops 1073741824 | bytes 2097152 | tf_op jit(solution)/shard_map/pallas_call | solution.py:356
  160.2 6.0 %collective-permute-start.13 = (bf16[64,2176]{1,0:T(8,128)(2,1)S(1)}, bf16[64,2176]{1,0:T(8,128)(2,1)S(1)}, u32[]{:S(2)}, u32[]{:S(2)}) collective-permute-start(bf16[64,2176]{1,0:T(8,128)(2,1)S(1)} %get-tuple-element.66), channel_id=1, source_target_pairs={{0,1},{1,2},{2,3},{3,4},{4,5},{5,6},{6,7},{7,8},{8,9},{9,10},{10,1... | collective-permute-start | bytes 835592 | tf_op jit(solution)/shard_map/ppermute | solution.py:343
  166.2 1.9 %collective-permute-start.14 = (bf16[64,2176]{1,0:T(8,128)(2,1)S(1)}, bf16[64,2176]{1,0:T(8,128)(2,1)S(1)}, u32[]{:S(2)}, u32[]{:S(2)}) collective-permute-start(bf16[64,2176]{1,0:T(8,128)(2,1)S(1)} %get-tuple-element.67), channel_id=1, source_target_pairs={{0,2},{1,3},{2,4},{3,5},{4,6},{5,7},{6,8},{7,9},{8,10},{9,11},{10,... | collective-permute-start | bytes 835592 | tf_op jit(solution)/shard_map/ppermute | solution.py:343
  168.2 1.9 shard_map.90
  170.1 7.5 %collective-permute-done.14.r2 = bf16[64,2176]{1,0:T(8,128)(2,1)S(1)} collective-permute-done((bf16[64,2176]{1,0:T(8,128)(2,1)S(1)}, bf16[64,2176]{1,0:T(8,128)(2,1)S(1)}, u32[]{:S(2)}, u32[]{:S(2)}) %collective-permute-start.14) | collective-permute-done | bytes 278560 | tf_op jit(solution)/shard_map/ppermute | solution.py:343
  177.6 1.0 shard_map.91
  (65 shorter events, 5.7 us)
Async XLA Ops:
  7.2 49.4 %copy-start = (s32[8,32]{1,0:T(8,128)S(1)}, s32[8,32]{1,0:T(8,128)}, u32[]{:S(2)}) copy-start(s32[8,32]{1,0:T(8,128)} %param.11) | copy-start | bytes 3076
  7.2 49.3 %copy-start.8 = (s32[1,8,8]{2,1,0:T(8,128)S(1)}, s32[1,8,8]{2,1,0:T(8,128)}, u32[]{:S(2)}) copy-start(s32[1,8,8]{2,1,0:T(8,128)} %param.12) | copy-start | bytes 772
  7.2 58.8 %copy-start.9 = (s32[1,8]{1,0:T(1,128)S(1)}, s32[1,8]{1,0:T(1,128)}, u32[]{:S(2)}) copy-start(s32[1,8]{1,0:T(1,128)} %param.13) | copy-start | bytes 100
  7.2 49.1 %all-gather.3.cloned.1.call-start = ((), (), s32[]{:S(2)}) async-start(), calls=%async_computation.1 | async-start | bytes 4718592 | tf_op jit(solution)/shard_map/all_gather | solution.py:307
  7.9 97.9 %all-gather.5.cloned.1.call-start = ((), (), s32[]{:S(2)}) async-start(), calls=%async_computation.2 | async-start | bytes 3538944 | tf_op jit(solution)/shard_map/all_gather | solution.py:309
  8.0 0.7 copy-start.2
  12.2 51.8 %copy-start.10 = (bf16[2,128,1024]{2,1,0:T(8,128)(2,1)S(1)}, bf16[2,128,1024]{2,1,0:T(8,128)(2,1)}, u32[]{:S(2)}) copy-start(bf16[2,128,1024]{2,1,0:T(8,128)(2,1)} %get-tuple-element.52) | copy-start | bytes 1572868
  12.2 36.7 %collective-permute-start.4 = (bf16[3,128,1024]{2,1,0:T(8,128)(2,1)}, bf16[3,128,1024]{2,1,0:T(8,128)(2,1)S(1)}, u32[]{:S(2)}, u32[]{:S(2)}) collective-permute-start(bf16[3,128,1024]{2,1,0:T(8,128)(2,1)} %get-tuple-element.37), channel_id=1, source_target_pairs={{0,64},{64,128},{128,192},{192,256},{256,320},{320,384},{384,448},... | collective-permute-start | bytes 2359304 | tf_op jit(solution)/shard_map/ppermute | solution.py:271
  15.6 33.4 %collective-permute-start.5 = (bf16[3,128,1024]{2,1,0:T(8,128)(2,1)}, bf16[3,128,1024]{2,1,0:T(8,128)(2,1)S(1)}, u32[]{:S(2)}, u32[]{:S(2)}) collective-permute-start(bf16[3,128,1024]{2,1,0:T(8,128)(2,1)} %get-tuple-element.38), channel_id=1, source_target_pairs={{0,448},{64,0},{128,64},{192,128},{256,192},{320,256},{384,320},{4... | collective-permute-start | bytes 2359304 | tf_op jit(solution)/shard_map/ppermute | solution.py:271
  19.4 19.0 %collective-permute-start = (bf16[64,384]{1,0:T(8,128)(2,1)}, bf16[64,384]{1,0:T(8,128)(2,1)S(1)}, u32[]{:S(2)}, u32[]{:S(2)}) collective-permute-start(bf16[64,384]{1,0:T(8,128)(2,1)} %param.8), channel_id=1, source_target_pairs={{0,0},{1,64},{2,128},{3,192},{4,256},{5,320},{6,384},{7,448},{64,1... | collective-permute-start | bytes 147464 | tf_op jit(solution)/shard_map/ppermute | solution.py:293
  22.0 25.4 %collective-permute-start.1 = (bf16[64,384]{1,0:T(8,128)(2,1)}, bf16[64,384]{1,0:T(8,128)(2,1)S(1)}, u32[]{:S(2)}, u32[]{:S(2)}) collective-permute-start(bf16[64,384]{1,0:T(8,128)(2,1)} %param.8), channel_id=1, source_target_pairs={{0,256},{1,320},{2,384},{3,448},{4,0},{5,64},{6,128},{7,192},{64,2... | collective-permute-start | bytes 147464 | tf_op jit(solution)/shard_map/ppermute | solution.py:293
  30.5 17.0 %collective-permute-start.2 = (bf16[64,384]{1,0:T(8,128)(2,1)}, bf16[64,384]{1,0:T(8,128)(2,1)S(1)}, u32[]{:S(2)}, u32[]{:S(2)}) collective-permute-start(bf16[64,384]{1,0:T(8,128)(2,1)} %param.8), channel_id=1, source_target_pairs={{0,128},{1,192},{2,0},{3,64},{4,384},{5,448},{6,256},{7,320},{64,1... | collective-permute-start | bytes 147464 | tf_op jit(solution)/shard_map/ppermute | solution.py:293
  38.4 10.5 %collective-permute-start.3 = (bf16[64,384]{1,0:T(8,128)(2,1)}, bf16[64,384]{1,0:T(8,128)(2,1)S(1)}, u32[]{:S(2)}, u32[]{:S(2)}) collective-permute-start(bf16[64,384]{1,0:T(8,128)(2,1)} %param.8), channel_id=1, source_target_pairs={{0,384},{1,448},{2,256},{3,320},{4,128},{5,192},{6,0},{7,64},{64,3... | collective-permute-start | bytes 147464 | tf_op jit(solution)/shard_map/ppermute | solution.py:293
  49.0 63.1 %copy-start.4 = (bf16[3,128,1024]{2,1,0:T(8,128)(2,1)}, bf16[3,128,1024]{2,1,0:T(8,128)(2,1)S(1)}, u32[]{:S(2)}) copy-start(bf16[3,128,1024]{2,1,0:T(8,128)(2,1)S(1)} %collective-permute-done.4.one_up) | copy-start | bytes 2359300
  49.0 63.1 %copy-start.5 = (bf16[3,128,1024]{2,1,0:T(8,128)(2,1)}, bf16[3,128,1024]{2,1,0:T(8,128)(2,1)S(1)}, u32[]{:S(2)}) copy-start(bf16[3,128,1024]{2,1,0:T(8,128)(2,1)S(1)} %collective-permute-done.5.one_down) | copy-start | bytes 2359300
  49.0 6.4 %collective-permute-start.6 = (bf16[2,2,64,384]{3,2,1,0:T(8,128)(2,1)S(1)}, bf16[2,2,64,384]{3,2,1,0:T(8,128)(2,1)S(1)}, u32[]{:S(2)}, u32[]{:S(2)}) collective-permute-start(bf16[2,2,64,384]{3,2,1,0:T(8,128)(2,1)S(1)} %pad_maximum_fusion.1), channel_id=1, source_target_pairs={{0,64},{64,0},{128,192},{192,128},{256,320},{320,256},{384,448},{4... | collective-permute-start | bytes 589832 | tf_op jit(solution)/shard_map/ppermute | solution.py:303
  56.9 28.9 %collective-permute-start.7 = (bf16[2,128,1024]{2,1,0:T(8,128)(2,1)}, bf16[2,128,1024]{2,1,0:T(8,128)(2,1)S(1)}, u32[]{:S(2)}, u32[]{:S(2)}) collective-permute-start(bf16[2,128,1024]{2,1,0:T(8,128)(2,1)} %get-tuple-element.51), channel_id=1, source_target_pairs={{0,128},{64,192},{128,256},{192,320},{256,384},{320,448},{384,0},{... | collective-permute-start | bytes 1572872 | tf_op jit(solution)/shard_map/ppermute | solution.py:271
  64.0 26.3 %collective-permute-start.8 = (bf16[2,128,1024]{2,1,0:T(8,128)(2,1)S(1)}, bf16[2,128,1024]{2,1,0:T(8,128)(2,1)S(1)}, u32[]{:S(2)}, u32[]{:S(2)}) collective-permute-start(bf16[2,128,1024]{2,1,0:T(8,128)(2,1)S(1)} %copy-done.10), channel_id=1, source_target_pairs={{0,384},{64,448},{128,0},{192,64},{256,128},{320,192},{384,256},{4... | collective-permute-start | bytes 1572872 | tf_op jit(solution)/shard_map/ppermute | solution.py:271
  85.8 26.3 %copy-start.6 = (bf16[2,128,1024]{2,1,0:T(8,128)(2,1)}, bf16[2,128,1024]{2,1,0:T(8,128)(2,1)S(1)}, u32[]{:S(2)}) copy-start(bf16[2,128,1024]{2,1,0:T(8,128)(2,1)S(1)} %collective-permute-done.7.two_up) | copy-start | bytes 1572868
  90.4 21.7 %copy-start.7 = (bf16[2,128,1024]{2,1,0:T(8,128)(2,1)}, bf16[2,128,1024]{2,1,0:T(8,128)(2,1)S(1)}, u32[]{:S(2)}) copy-start(bf16[2,128,1024]{2,1,0:T(8,128)(2,1)S(1)} %collective-permute-done.8.two_down) | copy-start | bytes 1572868
  91.1 51.2 %collective-permute-start.10 = (bf16[3,128,1024]{2,1,0:T(8,128)(2,1)}, bf16[3,128,1024]{2,1,0:T(8,128)(2,1)}, u32[]{:S(2)}, u32[]{:S(2)}) collective-permute-start(bf16[3,128,1024]{2,1,0:T(8,128)(2,1)} %slice_dynamic-update-slice_fusion), channel_id=1, source_target_pairs={{0,320},{64,384},{128,448},{192,0},{256,64},{320,128},{384,192},{4... | collective-permute-start | bytes 2359304 | tf_op jit(solution)/shard_map/ppermute | solution.py:271
  93.8 59.2 %copy-start.3 = (s32[8,8]{1,0:T(8,128)S(1)}, s32[8,8]{1,0:T(8,128)}, u32[]{:S(2)}) copy-start(s32[8,8]{1,0:T(8,128)} %owner.3) | copy-start | bytes 772
  93.8 59.2 %collective-permute-start.9 = (bf16[3,128,1024]{2,1,0:T(8,128)(2,1)}, bf16[3,128,1024]{2,1,0:T(8,128)(2,1)}, u32[]{:S(2)}, u32[]{:S(2)}) collective-permute-start(bf16[3,128,1024]{2,1,0:T(8,128)(2,1)} %slice_dynamic-update-slice_fusion.1), channel_id=1, source_target_pairs={{0,192},{64,256},{128,320},{192,384},{256,448},{320,0},{384,64},{4... | collective-permute-start | bytes 2359304 | tf_op jit(solution)/shard_map/ppermute | solution.py:271
  112.1 13.1 %all-to-all-start = ((bf16[8,64,384]{2,1,0:T(8,128)(2,1)}), bf16[8,64,384]{2,1,0:T(8,128)(2,1)S(1)}, u32[]{:S(2)}, u32[]{:S(2)}) async-start(bf16[8,64,384]{2,1,0:T(8,128)(2,1)} %bitcast.11), calls=%async_computation | async-start | bytes 786432 | tf_op jit(solution)/shard_map/all_to_all | solution.py:318
  125.5 31.8 %collective-permute-start.11 = (bf16[64,2176]{1,0:T(8,128)(2,1)S(1)}, bf16[64,2176]{1,0:T(8,128)(2,1)S(1)}, u32[]{:S(2)}, u32[]{:S(2)}) collective-permute-start(bf16[64,2176]{1,0:T(8,128)(2,1)S(1)} %get-tuple-element.47.q0), channel_id=1, source_target_pairs={{1,0},{2,1},{3,2},{4,3},{5,4},{6,5},{7,6},{8,7},{9,8},{10,9},{11,1... | collective-permute-start | bytes 835592 | tf_op jit(solution)/shard_map/ppermute | solution.py:343
  128.1 29.1 %collective-permute-start.12 = (bf16[64,2176]{1,0:T(8,128)(2,1)S(1)}, bf16[64,2176]{1,0:T(8,128)(2,1)S(1)}, u32[]{:S(2)}, u32[]{:S(2)}) collective-permute-start(bf16[64,2176]{1,0:T(8,128)(2,1)S(1)} %get-tuple-element.47.q0), channel_id=1, source_target_pairs={{2,0},{3,1},{4,2},{5,3},{6,4},{7,5},{8,6},{9,7},{10,8},{11,9},{12,... | collective-permute-start | bytes 835592 | tf_op jit(solution)/shard_map/ppermute | solution.py:343
  157.2 11.0 %copy-start.1 = (bf16[1024,1024]{1,0:T(8,128)(2,1)S(1)}, bf16[1024,1024]{1,0:T(8,128)(2,1)}, u32[]{:S(2)}) copy-start(bf16[1024,1024]{1,0:T(8,128)(2,1)} %get-tuple-element.63.kv) | copy-start | bytes 6291460
  160.2 9.9 %collective-permute-start.13 = (bf16[64,2176]{1,0:T(8,128)(2,1)S(1)}, bf16[64,2176]{1,0:T(8,128)(2,1)S(1)}, u32[]{:S(2)}, u32[]{:S(2)}) collective-permute-start(bf16[64,2176]{1,0:T(8,128)(2,1)S(1)} %get-tuple-element.66), channel_id=1, source_target_pairs={{0,1},{1,2},{2,3},{3,4},{4,5},{5,6},{6,7},{7,8},{8,9},{9,10},{10,1... | collective-permute-start | bytes 835592 | tf_op jit(solution)/shard_map/ppermute | solution.py:343
  166.2 11.3 %collective-permute-start.14 = (bf16[64,2176]{1,0:T(8,128)(2,1)S(1)}, bf16[64,2176]{1,0:T(8,128)(2,1)S(1)}, u32[]{:S(2)}, u32[]{:S(2)}) collective-permute-start(bf16[64,2176]{1,0:T(8,128)(2,1)S(1)} %get-tuple-element.67), channel_id=1, source_target_pairs={{0,2},{1,3},{2,4},{3,5},{4,6},{5,7},{6,8},{7,9},{8,10},{9,11},{10,... | collective-permute-start | bytes 835592 | tf_op jit(solution)/shard_map/ppermute | solution.py:343
Sparse Core Ops, SparseCore 0:
  10.2 41.6 all-gather.2
  56.4 49.3 all-gather.4

commit v5 on v4

--- a/solution.py
+++ b/solution.py
@@ -150,9 +150,9 @@
 
 
 def blend_kernel(
-    owner, me, kcos, ksin, spots, fresh,
+    owner, me, kcos, ksin, spots, fresh, q1, q2,
     pool, one_up, one_down, two_up, two_down, three_up, three_down,
-    blended, kv, sem, out_sem,
+    blended, p1, p2, kv, stack, sem, out_sem,
 ):
     traces, blocks = owner.shape
     rows = kv.shape[0] // blocks
@@ -203,25 +203,7 @@
             placed = jnp.dot(hits, fresh[:, cols], preferred_element_type=F32)
             kv[here, cols] = jnp.where(chosen, placed, x).astype(BF)
         pltpu.make_async_copy(kv.at[here], blended.at[here], out_sem.at[b]).start()
-    for b in range(blocks):
-        here = pl.ds(b * rows, rows)
-        pltpu.make_async_copy(kv.at[here], blended.at[here], out_sem.at[b]).wait()
-
-
-def own_kernel(q0, kv, num0, den0, stack):
     tokens = kv.shape[0]
-    n_q = q0.shape[0]
-    key = lax.broadcasted_iota(jnp.int32, (n_q, tokens), 1)
-
-    def put(i, cols, num):
-        num0[:, cols] = num
-
-    (den0[...],) = attend([q0], kv, stack, [key <= token_of(q0, tokens)], put)
-
-
-def remote_kernel(q1, q2, kv, p1, p2, stack):
-    tokens = kv.shape[0]
-    n_q = q1.shape[0]
     key = lax.broadcasted_iota(jnp.int32, (n_q, tokens), 1)
 
     def put(i, cols, num):
@@ -235,6 +217,20 @@
         p[:, QH * HD :] = jnp.where(
             lane < QH, high.astype(F32), pltpu.roll(low, QH, 1)
         ).astype(BF)
+    for b in range(blocks):
+        here = pl.ds(b * rows, rows)
+        pltpu.make_async_copy(kv.at[here], blended.at[here], out_sem.at[b]).wait()
+
+
+def own_kernel(q0, kv, num0, den0, stack):
+    tokens = kv.shape[0]
+    n_q = q0.shape[0]
+    key = lax.broadcasted_iota(jnp.int32, (n_q, tokens), 1)
+
+    def put(i, cols, num):
+        num0[:, cols] = num
+
+    (den0[...],) = attend([q0], kv, stack, [key <= token_of(q0, tokens)], put)
 
 
 def merge_kernel(num0, den0, r1, r2, live, out):
@@ -285,9 +281,6 @@
         ],
         moved=4 * tokens * kvw,
     )(block_owner, me, *kept(cache_pool[0]))
-    one_up, w_qkv = lax.optimization_barrier((one_up, w_qkv))
-    one_up, one_down = turned(one_up, 1), turned(one_down, -1)
-
     def crossed(m):
         pairs = [(a * group + b, (b ^ m) * group + a) for a in range(ny) for b in range(group)]
         return lax.ppermute(w_qkv, ("y", "x", "c"), pairs)
@@ -299,20 +292,18 @@
     w = paired(
         paired(crossed(0), crossed(4), 4, 0), paired(crossed(2), crossed(6), 4, 0), 2, 1
     )
-    w, one_up, one_down = lax.optimization_barrier((w, one_up, one_down))
     w = paired(w, lax.ppermute(w, "y", [(i, i ^ 1) for i in range(ny)]), 1, 2).reshape(-1, cols)
-    w, two_up, two_down, one_up, one_down = lax.optimization_barrier(
-        (w, two_up, two_down, one_up, one_down)
-    )
+    w, one_up, one_down, two_up, two_down = lax.optimization_barrier(
+        (w, one_up, one_down, two_up, two_down)
+    )
+    one_up, one_down = turned(one_up, 1), turned(one_down, -1)
+    two_up, two_down = turned(two_up, 2), turned(two_down, -2)
     hidden = lax.all_gather(sel_hidden.reshape(rows, d), XC, axis=0, tiled=True)
-    w, hidden = lax.optimization_barrier((w, hidden))
+    w, hidden, one_up, one_down = lax.optimization_barrier((w, hidden, one_up, one_down))
     w = lax.all_gather(w, "z", axis=0, tiled=True)
-    two_up, two_down = turned(two_up, 2), turned(two_down, -2)
-    two_up, two_down, three_up, three_down = lax.optimization_barrier(
-        (two_up, two_down, three_up, three_down)
-    )
     three_up = turned(lax.dynamic_update_slice(three_up, one_up[2:], (2, 0, 0)), 3)
     three_down = turned(lax.dynamic_update_slice(three_down, one_down[2:], (2, 0, 0)), -3)
+    hidden, w, two_up, two_down = lax.optimization_barrier((hidden, w, two_up, two_down))
     projected = jnp.dot(hidden, w, preferred_element_type=F32).astype(BF)
     projected = projected.reshape(group, rows, cols)
     merged = lax.all_to_all(projected, XC, 0, 0, tiled=True)
@@ -343,25 +334,24 @@
         return lax.ppermute(array, SEQ, pairs)
 
     q1, q2 = along(queries, -1), along(queries, -2)
-    blended, kv = call(
+    partial = jax.ShapeDtypeStruct((rows, wide), BF)
+    blended, p1, p2 = call(
         blend_kernel,
-        (jax.ShapeDtypeStruct((tokens, kvw), BF),) * 2,
-        [SM, SM] + [VM] * 4 + [ANY] * 7, (ANY, VM),
-        [pltpu.SemaphoreType.DMA((blocks,)), pltpu.SemaphoreType.DMA((blocks,))],
-        moved=6 * tokens * kvw,
+        (pltpu.HBM((tokens, kvw), BF), partial, partial),
+        [SM, SM] + [VM] * 6 + [ANY] * 7, (ANY, VM, VM),
+        [
+            pltpu.VMEM((tokens, kvw), BF),
+            pltpu.VMEM((2, GROUP * rows, HD), BF),
+            pltpu.SemaphoreType.DMA((blocks,)),
+            pltpu.SemaphoreType.DMA((blocks,)),
+        ],
+        flops=8 * rows * QH * HD * tokens,
+        moved=4 * tokens * kvw,
+        vmem=24,
     )(
-        block_owner, me, kcos, ksin, spots, fresh,
+        block_owner, me, kcos, ksin, spots, fresh, q1, q2,
         *kept(cache_pool[0], one_up, one_down, two_up, two_down, three_up, three_down),
     )
-    p1, p2 = call(
-        remote_kernel,
-        (jax.ShapeDtypeStruct((rows, wide), BF),) * 2,
-        [VM] * 3, (VM, VM),
-        [pltpu.VMEM((2, GROUP * rows, HD), BF)],
-        flops=8 * rows * QH * HD * tokens,
-        moved=2 * tokens * kvw,
-        vmem=20,
-    )(q1, q2, kv)
     whole, p1, p2 = lax.optimization_barrier((blended, p1, p2))
     r1, r2 = along(p1, 1), along(p2, 2)
     num0, den0 = call(

time: 186 us -> 182 us (0.978)
  the two profiles are of different devices: /device:TPU:257 before, /device:TPU:273 now
where the time goes in v5:
time: 182 us; the launch traced here: 181 us
  waiting for transfers between devices  83.5 us (46%)
  starting transfers between devices  57.3 us (31%)
  between operations  14.5 us (8%)
  Pallas kernels  13.1 us (7%)
  matrix products  6.24 us (3%)
  local copies, waits for them, and re-layouts  4.39 us (2%)
    ppermute x6, waiting for transfers between devices, turned(): return lax.ppermute(array, 'y', [(i, (i + by) % ny) for i in range(ny)])  35.4 us
    all_gather x1, waiting for transfers between devices, on_device(): w = lax.all_gather(w, 'z', axis=0, tiled=True)  25.3 us
    ppermute x6, starting transfers between devices, turned(): return lax.ppermute(array, 'y', [(i, (i + by) % ny) for i in range(ny)])  20.4 us
    ppermute x4, starting transfers between devices, crossed(): return lax.ppermute(w_qkv, ('y', 'x', 'c'), pairs)  17.6 us
    ppermute x4, starting transfers between devices, along(): return lax.ppermute(array, SEQ, pairs)  11.5 us
    ppermute x4, waiting for transfers between devices, along(): return lax.ppermute(array, SEQ, pairs)  10 us
    all_to_all x1, waiting for transfers between devices, on_device(): merged = lax.all_to_all(projected, XC, 0, 0, tiled=True)  7.9 us
    pallas_call x1, Pallas kernels, on_device(): call(blend_kernel, (pltpu.HBM((tokens, kvw), BF), partial, partial), [SM,...  6.43 us
  transfers between devices with their start and end apart: 18, of which 9 were waited for; matrix products, arithmetic and copies ran while one was open for 6% of the time, Pallas kernels for 3%

profile of v5, /device:TPU:273, one launch (start us, length us, event | category | flops | bytes accessed | tf_op | source)
XLA Modules:
  0.0 180.9 jit_solution(7897224153544050119)
XLA Ops:
  8.0 7.0 %collective-permute-start.1 = (bf16[64,384]{1,0:T(8,128)(2,1)}, bf16[64,384]{1,0:T(8,128)(2,1)S(1)}, u32[]{:S(2)}, u32[]{:S(2)}) collective-permute-start(bf16[64,384]{1,0:T(8,128)(2,1)} %param.8), channel_id=1, source_target_pairs={{0,256},{1,320},{2,384},{3,448},{4,0},{5,64},{6,128},{7,192},{64,2... | collective-permute-start | bytes 147464 | tf_op jit(solution)/shard_map/ppermute | solution.py:286
  15.0 2.0 %collective-permute-start = (bf16[64,384]{1,0:T(8,128)(2,1)}, bf16[64,384]{1,0:T(8,128)(2,1)S(1)}, u32[]{:S(2)}, u32[]{:S(2)}) collective-permute-start(bf16[64,384]{1,0:T(8,128)(2,1)} %param.8), channel_id=1, source_target_pairs={{0,0},{1,64},{2,128},{3,192},{4,256},{5,320},{6,384},{7,448},{64,1... | collective-permute-start | bytes 147464 | tf_op jit(solution)/shard_map/ppermute | solution.py:286
  17.0 6.6 %collective-permute-start.3 = (bf16[64,384]{1,0:T(8,128)(2,1)}, bf16[64,384]{1,0:T(8,128)(2,1)S(1)}, u32[]{:S(2)}, u32[]{:S(2)}) collective-permute-start(bf16[64,384]{1,0:T(8,128)(2,1)} %param.8), channel_id=1, source_target_pairs={{0,384},{1,448},{2,256},{3,320},{4,128},{5,192},{6,0},{7,64},{64,3... | collective-permute-start | bytes 147464 | tf_op jit(solution)/shard_map/ppermute | solution.py:286
  23.7 1.9 %collective-permute-start.2 = (bf16[64,384]{1,0:T(8,128)(2,1)}, bf16[64,384]{1,0:T(8,128)(2,1)S(1)}, u32[]{:S(2)}, u32[]{:S(2)}) collective-permute-start(bf16[64,384]{1,0:T(8,128)(2,1)} %param.8), channel_id=1, source_target_pairs={{0,128},{1,192},{2,0},{3,64},{4,384},{5,448},{6,256},{7,320},{64,1... | collective-permute-start | bytes 147464 | tf_op jit(solution)/shard_map/ppermute | solution.py:286
  25.7 1.3 collective-permute-done.3
  27.0 2.9 %collective-permute-done.2 = bf16[64,384]{1,0:T(8,128)(2,1)S(1)} collective-permute-done((bf16[64,384]{1,0:T(8,128)(2,1)}, bf16[64,384]{1,0:T(8,128)(2,1)S(1)}, u32[]{:S(2)}, u32[]{:S(2)}) %collective-permute-start.2) | collective-permute-done | bytes 49184 | tf_op jit(solution)/shard_map/ppermute | solution.py:286
  29.9 2.8 %collective-permute-start.4 = (bf16[2,2,64,384]{3,2,1,0:T(8,128)(2,1)S(1)}, bf16[2,2,64,384]{3,2,1,0:T(8,128)(2,1)S(1)}, u32[]{:S(2)}, u32[]{:S(2)}) collective-permute-start(bf16[2,2,64,384]{3,2,1,0:T(8,128)(2,1)S(1)} %pad_maximum_fusion.1), channel_id=1, source_target_pairs={{0,64},{64,0},{128,192},{192,128},{256,320},{320,256},{384,448},{4... | collective-permute-start | bytes 589832 | tf_op jit(solution)/shard_map/ppermute | solution.py:295
  33.4 3.6 %shard_map.86 = (bf16[3,128,1024]{2,1,0:T(8,128)(2,1)}, bf16[3,128,1024]{2,1,0:T(8,128)(2,1)}, bf16[2,128,1024]{2,1,0:T(8,128)(2,1)}, bf16[2,128,1024]{2,1,0:T(8...) custom-call(s32[8,8]{1,0:T(8,128)S(1)} %copy-done.2, s32[1]{0:T(128)} %bitcast.8.me, ...), custom_call_target="tpu_custom_call" | custom-call | bytes 4194304 | tf_op jit(solution)/shard_map/pallas_call | solution.py:272
  37.1 0.8 pad_maximum_fusion
  37.9 3.6 %collective-permute-start.5 = (bf16[3,128,1024]{2,1,0:T(8,128)(2,1)}, bf16[3,128,1024]{2,1,0:T(8,128)(2,1)S(1)}, u32[]{:S(2)}, u32[]{:S(2)}) collective-permute-start(bf16[3,128,1024]{2,1,0:T(8,128)(2,1)} %get-tuple-element.34), channel_id=1, source_target_pairs={{0,64},{64,128},{128,192},{192,256},{256,320},{320,384},{384,448},... | collective-permute-start | bytes 2359304 | tf_op jit(solution)/shard_map/ppermute | solution.py:267
  41.5 1.9 %collective-permute-start.6 = (bf16[3,128,1024]{2,1,0:T(8,128)(2,1)}, bf16[3,128,1024]{2,1,0:T(8,128)(2,1)S(1)}, u32[]{:S(2)}, u32[]{:S(2)}) collective-permute-start(bf16[3,128,1024]{2,1,0:T(8,128)(2,1)} %get-tuple-element.35), channel_id=1, source_target_pairs={{0,448},{64,0},{128,64},{192,128},{256,192},{320,256},{384,320},{4... | collective-permute-start | bytes 2359304 | tf_op jit(solution)/shard_map/ppermute | solution.py:267
  43.4 14.0 %collective-permute-done.5.one_up = bf16[3,128,1024]{2,1,0:T(8,128)(2,1)S(1)} collective-permute-done((bf16[3,128,1024]{2,1,0:T(8,128)(2,1)}, bf16[3,128,1024]{2,1,0:T(8,128)(2,1)S(1)}, u32[]{:S(2)}, u32[]{:S(2)}) %collective-permute-start.5) | collective-permute-done | bytes 786464 | tf_op jit(solution)/shard_map/ppermute | solution.py:267
  57.4 6.9 %collective-permute-done.6.one_down = bf16[3,128,1024]{2,1,0:T(8,128)(2,1)S(1)} collective-permute-done((bf16[3,128,1024]{2,1,0:T(8,128)(2,1)}, bf16[3,128,1024]{2,1,0:T(8,128)(2,1)S(1)}, u32[]{:S(2)}, u32[]{:S(2)}) %collective-permute-start.6) | collective-permute-done | bytes 786464 | tf_op jit(solution)/shard_map/ppermute | solution.py:267
  65.0 3.5 %collective-permute-start.7 = (bf16[2,128,1024]{2,1,0:T(8,128)(2,1)}, bf16[2,128,1024]{2,1,0:T(8,128)(2,1)S(1)}, u32[]{:S(2)}, u32[]{:S(2)}) collective-permute-start(bf16[2,128,1024]{2,1,0:T(8,128)(2,1)} %get-tuple-element.38), channel_id=1, source_target_pairs={{0,128},{64,192},{128,256},{192,320},{256,384},{320,448},{384,0},{... | collective-permute-start | bytes 1572872 | tf_op jit(solution)/shard_map/ppermute | solution.py:267
  68.5 2.7 %collective-permute-start.8 = (bf16[2,128,1024]{2,1,0:T(8,128)(2,1)}, bf16[2,128,1024]{2,1,0:T(8,128)(2,1)S(1)}, u32[]{:S(2)}, u32[]{:S(2)}) collective-permute-start(bf16[2,128,1024]{2,1,0:T(8,128)(2,1)} %get-tuple-element.39), channel_id=1, source_target_pairs={{0,384},{64,448},{128,0},{192,64},{256,128},{320,192},{384,256},{4... | collective-permute-start | bytes 1572872 | tf_op jit(solution)/shard_map/ppermute | solution.py:267
  72.1 5.7 %collective-permute-start.12 = (bf16[3,128,1024]{2,1,0:T(8,128)(2,1)}, bf16[3,128,1024]{2,1,0:T(8,128)(2,1)}, u32[]{:S(2)}, u32[]{:S(2)}) collective-permute-start(bf16[3,128,1024]{2,1,0:T(8,128)(2,1)} %slice_dynamic-update-slice_fusion), channel_id=1, source_target_pairs={{0,320},{64,384},{128,448},{192,0},{256,64},{320,128},{384,192},{4... | collective-permute-start | bytes 2359304 | tf_op jit(solution)/shard_map/ppermute | solution.py:267
  78.5 3.0 %collective-permute-start.11 = (bf16[3,128,1024]{2,1,0:T(8,128)(2,1)}, bf16[3,128,1024]{2,1,0:T(8,128)(2,1)}, u32[]{:S(2)}, u32[]{:S(2)}) collective-permute-start(bf16[3,128,1024]{2,1,0:T(8,128)(2,1)} %slice_dynamic-update-slice_fusion.1), channel_id=1, source_target_pairs={{0,192},{64,256},{128,320},{192,384},{256,448},{320,0},{384,64},{4... | collective-permute-start | bytes 2359304 | tf_op jit(solution)/shard_map/ppermute | solution.py:267
  81.6 3.0 %collective-permute-done.8.two_down = bf16[2,128,1024]{2,1,0:T(8,128)(2,1)S(1)} collective-permute-done((bf16[2,128,1024]{2,1,0:T(8,128)(2,1)}, bf16[2,128,1024]{2,1,0:T(8,128)(2,1)S(1)}, u32[]{:S(2)}, u32[]{:S(2)}) %collective-permute-start.8) | collective-permute-done | bytes 524320 | tf_op jit(solution)/shard_map/ppermute | solution.py:267
  84.6 25.3 %all-gather.5.cloned.1.call-done = bf16[4096,384]{1,0:T(8,128)(2,1)} async-done(((bf16[512,384]{1,0:T(8,128)(2,1)}), bf16[4096,384]{1,0:T(8,128)(2,1)}) %all-gather.5.cloned.1.call-update) | async-done | bytes 3145744 | tf_op jit(solution)/shard_map/all_gather | solution.py:303
  110.0 6.2 %convolution_convert_fusion = bf16[512,384]{1,0:T(8,128)(2,1)} fusion(bf16[512,4096]{1,0:T(8,128)(2,1)} %all-gather.3.cloned.1.call-done, bf16[4096,384]{1,0:T(8,128)(2,1)} %all-gather.5.cloned.1.call-done), kind=kOutput, calls=%fused_computation | convolution fusion | flops 1610809344 | bytes 7733248 | tf_op jit(solution)/shard_map/dot_general | solution.py:307
  116.2 5.0 %all-to-all-start = ((bf16[8,64,384]{2,1,0:T(8,128)(2,1)}), bf16[8,64,384]{2,1,0:T(8,128)(2,1)S(1)}, u32[]{:S(2)}, u32[]{:S(2)}) async-start(bf16[8,64,384]{2,1,0:T(8,128)(2,1)} %bitcast.11), calls=%async_computation | async-start | bytes 786432 | tf_op jit(solution)/shard_map/all_to_all | solution.py:309
  121.5 7.9 %all-to-all-done.proj = bf16[8,64,384]{2,1,0:T(8,128)(2,1)S(1)} async-done(((bf16[8,64,384]{2,1,0:T(8,128)(2,1)}), bf16[8,64,384]{2,1,0:T(8,128)(2,1)S(1)}, u32[]{:S(2)}, u32[]{:S(2)}) %all-to-all-start) | async-done | bytes 393248 | tf_op jit(solution)/shard_map/all_to_all | solution.py:309
  129.6 4.7 %collective-permute-start.10 = (bf16[64,2176]{1,0:T(8,128)(2,1)S(1)}, bf16[64,2176]{1,0:T(8,128)(2,1)S(1)}, u32[]{:S(2)}, u32[]{:S(2)}) collective-permute-start(bf16[64,2176]{1,0:T(8,128)(2,1)S(1)} %get-tuple-element.42.q0), channel_id=1, source_target_pairs={{2,0},{3,1},{4,2},{5,3},{6,4},{7,5},{8,6},{9,7},{10,8},{11,9},{12,... | collective-permute-start | bytes 835592 | tf_op jit(solution)/shard_map/ppermute | solution.py:334
  134.3 3.0 %collective-permute-start.9 = (bf16[64,2176]{1,0:T(8,128)(2,1)S(1)}, bf16[64,2176]{1,0:T(8,128)(2,1)S(1)}, u32[]{:S(2)}, u32[]{:S(2)}) collective-permute-start(bf16[64,2176]{1,0:T(8,128)(2,1)S(1)} %get-tuple-element.42.q0), channel_id=1, source_target_pairs={{1,0},{2,1},{3,2},{4,3},{5,4},{6,5},{7,6},{8,7},{9,8},{10,9},{11,1... | collective-permute-start | bytes 835592 | tf_op jit(solution)/shard_map/ppermute | solution.py:334
  137.6 11.5 %collective-permute-done.12.three_down = bf16[3,128,1024]{2,1,0:T(8,128)(2,1)} collective-permute-done((bf16[3,128,1024]{2,1,0:T(8,128)(2,1)}, bf16[3,128,1024]{2,1,0:T(8,128)(2,1)}, u32[]{:S(2)}, u32[]{:S(2)}) %collective-permute-start.12) | collective-permute-done | bytes 786464 | tf_op jit(solution)/shard_map/ppermute | solution.py:267
  149.2 6.4 %shard_map.88 = (bf16[1024,1024]{1,0:T(8,128)(2,1)}, bf16[64,2176]{1,0:T(8,128)(2,1)S(1)}, bf16[64,2176]{1,0:T(8,128)(2,1)S(1)}) custom-call(s32[8,8]{1,0:T(8,128)S(1)} %copy-done.3, s32[1]{0:T(128)} %bitcast.8.me, f32[8,128]{1,0:T(8,128)S(1)} %get-tuple-element.74.kcos, f32[8,128]{1,0:T(8,128)S(1)} %get-tuple-element.75.ksin, ...), custom_call_target="tpu_custom_call" | custom-call | flops 1073741824 | bytes 4194304 | tf_op jit(solution)/shard_map/pallas_call | solution.py:338
  155.6 1.9 %collective-permute-start.13 = (bf16[64,2176]{1,0:T(8,128)(2,1)S(1)}, bf16[64,2176]{1,0:T(8,128)(2,1)S(1)}, u32[]{:S(2)}, u32[]{:S(2)}) collective-permute-start(bf16[64,2176]{1,0:T(8,128)(2,1)S(1)} %get-tuple-element.53), channel_id=1, source_target_pairs={{0,1},{1,2},{2,3},{3,4},{4,5},{5,6},{6,7},{7,8},{8,9},{9,10},{10,1... | collective-permute-start | bytes 835592 | tf_op jit(solution)/shard_map/ppermute | solution.py:334
  157.5 1.9 %collective-permute-start.14 = (bf16[64,2176]{1,0:T(8,128)(2,1)S(1)}, bf16[64,2176]{1,0:T(8,128)(2,1)S(1)}, u32[]{:S(2)}, u32[]{:S(2)}) collective-permute-start(bf16[64,2176]{1,0:T(8,128)(2,1)S(1)} %get-tuple-element.54), channel_id=1, source_target_pairs={{0,2},{1,3},{2,4},{3,5},{4,6},{5,7},{6,8},{7,9},{8,10},{9,11},{10,... | collective-permute-start | bytes 835592 | tf_op jit(solution)/shard_map/ppermute | solution.py:334
  159.5 1.6 copy-done.1
  161.1 1.8 %shard_map.89 = (f32[64,2048]{1,0:T(8,128)S(1)}, f32[64,128]{1,0:T(8,128)S(1)}) custom-call(bf16[64,2176]{1,0:T(8,128)(2,1)S(1)} %get-tuple-element.42.q0, bf16[1024,1024]{1,0:T(8,128)(2,1)S(1)} %copy-done.1), custom_call_target="tpu_custom_call" | custom-call | flops 536870912 | bytes 2097152 | tf_op jit(solution)/shard_map/pallas_call | solution.py:357
  163.0 10.0 %collective-permute-done.14.r2 = bf16[64,2176]{1,0:T(8,128)(2,1)S(1)} collective-permute-done((bf16[64,2176]{1,0:T(8,128)(2,1)S(1)}, bf16[64,2176]{1,0:T(8,128)(2,1)S(1)}, u32[]{:S(2)}, u32[]{:S(2)}) %collective-permute-start.14) | collective-permute-done | bytes 278560 | tf_op jit(solution)/shard_map/ppermute | solution.py:334
  173.0 1.0 shard_map.90
  (62 shorter events, 4.8 us)
Async XLA Ops:
  7.2 57.4 %copy-start = (s32[8,32]{1,0:T(8,128)S(1)}, s32[8,32]{1,0:T(8,128)}, u32[]{:S(2)}) copy-start(s32[8,32]{1,0:T(8,128)} %param.11) | copy-start | bytes 3076
  7.2 57.1 %copy-start.8 = (s32[1,8,8]{2,1,0:T(8,128)S(1)}, s32[1,8,8]{2,1,0:T(8,128)}, u32[]{:S(2)}) copy-start(s32[1,8,8]{2,1,0:T(8,128)} %param.12) | copy-start | bytes 772
  7.2 57.5 %copy-start.9 = (s32[1,8]{1,0:T(1,128)S(1)}, s32[1,8]{1,0:T(1,128)}, u32[]{:S(2)}) copy-start(s32[1,8]{1,0:T(1,128)} %param.13) | copy-start | bytes 100
  7.2 57.1 %all-gather.3.cloned.1.call-start = ((), (), s32[]{:S(2)}) async-start(), calls=%async_computation.1 | async-start | bytes 4718592 | tf_op jit(solution)/shard_map/all_gather | solution.py:301
  7.9 102.0 %all-gather.5.cloned.1.call-start = ((), (), s32[]{:S(2)}) async-start(), calls=%async_computation.2 | async-start | bytes 3538944 | tf_op jit(solution)/shard_map/all_gather | solution.py:303
  8.0 17.7 %collective-permute-start.1 = (bf16[64,384]{1,0:T(8,128)(2,1)}, bf16[64,384]{1,0:T(8,128)(2,1)S(1)}, u32[]{:S(2)}, u32[]{:S(2)}) collective-permute-start(bf16[64,384]{1,0:T(8,128)(2,1)} %param.8), channel_id=1, source_target_pairs={{0,256},{1,320},{2,384},{3,448},{4,0},{5,64},{6,128},{7,192},{64,2... | collective-permute-start | bytes 147464 | tf_op jit(solution)/shard_map/ppermute | solution.py:286
  15.0 10.6 %collective-permute-start = (bf16[64,384]{1,0:T(8,128)(2,1)}, bf16[64,384]{1,0:T(8,128)(2,1)S(1)}, u32[]{:S(2)}, u32[]{:S(2)}) collective-permute-start(bf16[64,384]{1,0:T(8,128)(2,1)} %param.8), channel_id=1, source_target_pairs={{0,0},{1,64},{2,128},{3,192},{4,256},{5,320},{6,384},{7,448},{64,1... | collective-permute-start | bytes 147464 | tf_op jit(solution)/shard_map/ppermute | solution.py:286
  17.0 9.9 %collective-permute-start.3 = (bf16[64,384]{1,0:T(8,128)(2,1)}, bf16[64,384]{1,0:T(8,128)(2,1)S(1)}, u32[]{:S(2)}, u32[]{:S(2)}) collective-permute-start(bf16[64,384]{1,0:T(8,128)(2,1)} %param.8), channel_id=1, source_target_pairs={{0,384},{1,448},{2,256},{3,320},{4,128},{5,192},{6,0},{7,64},{64,3... | collective-permute-start | bytes 147464 | tf_op jit(solution)/shard_map/ppermute | solution.py:286
  23.7 6.2 %collective-permute-start.2 = (bf16[64,384]{1,0:T(8,128)(2,1)}, bf16[64,384]{1,0:T(8,128)(2,1)S(1)}, u32[]{:S(2)}, u32[]{:S(2)}) collective-permute-start(bf16[64,384]{1,0:T(8,128)(2,1)} %param.8), channel_id=1, source_target_pairs={{0,128},{1,192},{2,0},{3,64},{4,384},{5,448},{6,256},{7,320},{64,1... | collective-permute-start | bytes 147464 | tf_op jit(solution)/shard_map/ppermute | solution.py:286
  29.9 7.1 %collective-permute-start.4 = (bf16[2,2,64,384]{3,2,1,0:T(8,128)(2,1)S(1)}, bf16[2,2,64,384]{3,2,1,0:T(8,128)(2,1)S(1)}, u32[]{:S(2)}, u32[]{:S(2)}) collective-permute-start(bf16[2,2,64,384]{3,2,1,0:T(8,128)(2,1)S(1)} %pad_maximum_fusion.1), channel_id=1, source_target_pairs={{0,64},{64,0},{128,192},{192,128},{256,320},{320,256},{384,448},{4... | collective-permute-start | bytes 589832 | tf_op jit(solution)/shard_map/ppermute | solution.py:295
  32.7 0.7 copy-start.2
  37.9 19.5 %collective-permute-start.5 = (bf16[3,128,1024]{2,1,0:T(8,128)(2,1)}, bf16[3,128,1024]{2,1,0:T(8,128)(2,1)S(1)}, u32[]{:S(2)}, u32[]{:S(2)}) collective-permute-start(bf16[3,128,1024]{2,1,0:T(8,128)(2,1)} %get-tuple-element.34), channel_id=1, source_target_pairs={{0,64},{64,128},{128,192},{192,256},{256,320},{320,384},{384,448},... | collective-permute-start | bytes 2359304 | tf_op jit(solution)/shard_map/ppermute | solution.py:267
  41.5 22.8 %collective-permute-start.6 = (bf16[3,128,1024]{2,1,0:T(8,128)(2,1)}, bf16[3,128,1024]{2,1,0:T(8,128)(2,1)S(1)}, u32[]{:S(2)}, u32[]{:S(2)}) collective-permute-start(bf16[3,128,1024]{2,1,0:T(8,128)(2,1)} %get-tuple-element.35), channel_id=1, source_target_pairs={{0,448},{64,0},{128,64},{192,128},{256,192},{320,256},{384,320},{4... | collective-permute-start | bytes 2359304 | tf_op jit(solution)/shard_map/ppermute | solution.py:267
  57.4 58.8 %copy-start.4 = (bf16[3,128,1024]{2,1,0:T(8,128)(2,1)}, bf16[3,128,1024]{2,1,0:T(8,128)(2,1)S(1)}, u32[]{:S(2)}) copy-start(bf16[3,128,1024]{2,1,0:T(8,128)(2,1)S(1)} %collective-permute-done.5.one_up) | copy-start | bytes 2359300
  64.3 51.9 %copy-start.5 = (bf16[3,128,1024]{2,1,0:T(8,128)(2,1)}, bf16[3,128,1024]{2,1,0:T(8,128)(2,1)S(1)}, u32[]{:S(2)}) copy-start(bf16[3,128,1024]{2,1,0:T(8,128)(2,1)S(1)} %collective-permute-done.6.one_down) | copy-start | bytes 2359300
  65.0 16.6 %collective-permute-start.7 = (bf16[2,128,1024]{2,1,0:T(8,128)(2,1)}, bf16[2,128,1024]{2,1,0:T(8,128)(2,1)S(1)}, u32[]{:S(2)}, u32[]{:S(2)}) collective-permute-start(bf16[2,128,1024]{2,1,0:T(8,128)(2,1)} %get-tuple-element.38), channel_id=1, source_target_pairs={{0,128},{64,192},{128,256},{192,320},{256,384},{320,448},{384,0},{... | collective-permute-start | bytes 1572872 | tf_op jit(solution)/shard_map/ppermute | solution.py:267
  68.5 16.1 %collective-permute-start.8 = (bf16[2,128,1024]{2,1,0:T(8,128)(2,1)}, bf16[2,128,1024]{2,1,0:T(8,128)(2,1)S(1)}, u32[]{:S(2)}, u32[]{:S(2)}) collective-permute-start(bf16[2,128,1024]{2,1,0:T(8,128)(2,1)} %get-tuple-element.39), channel_id=1, source_target_pairs={{0,384},{64,448},{128,0},{192,64},{256,128},{320,192},{384,256},{4... | collective-permute-start | bytes 1572872 | tf_op jit(solution)/shard_map/ppermute | solution.py:267
  72.1 77.0 %collective-permute-start.12 = (bf16[3,128,1024]{2,1,0:T(8,128)(2,1)}, bf16[3,128,1024]{2,1,0:T(8,128)(2,1)}, u32[]{:S(2)}, u32[]{:S(2)}) collective-permute-start(bf16[3,128,1024]{2,1,0:T(8,128)(2,1)} %slice_dynamic-update-slice_fusion), channel_id=1, source_target_pairs={{0,320},{64,384},{128,448},{192,0},{256,64},{320,128},{384,192},{4... | collective-permute-start | bytes 2359304 | tf_op jit(solution)/shard_map/ppermute | solution.py:267
  78.5 70.6 %copy-start.3 = (s32[8,8]{1,0:T(8,128)S(1)}, s32[8,8]{1,0:T(8,128)}, u32[]{:S(2)}) copy-start(s32[8,8]{1,0:T(8,128)} %owner.3) | copy-start | bytes 772
  78.5 70.6 %collective-permute-start.11 = (bf16[3,128,1024]{2,1,0:T(8,128)(2,1)}, bf16[3,128,1024]{2,1,0:T(8,128)(2,1)}, u32[]{:S(2)}, u32[]{:S(2)}) collective-permute-start(bf16[3,128,1024]{2,1,0:T(8,128)(2,1)} %slice_dynamic-update-slice_fusion.1), channel_id=1, source_target_pairs={{0,192},{64,256},{128,320},{192,384},{256,448},{320,0},{384,64},{4... | collective-permute-start | bytes 2359304 | tf_op jit(solution)/shard_map/ppermute | solution.py:267
  81.6 34.6 %copy-start.6 = (bf16[2,128,1024]{2,1,0:T(8,128)(2,1)}, bf16[2,128,1024]{2,1,0:T(8,128)(2,1)S(1)}, u32[]{:S(2)}) copy-start(bf16[2,128,1024]{2,1,0:T(8,128)(2,1)S(1)} %collective-permute-done.7.two_up) | copy-start | bytes 1572868
  84.6 31.6 %copy-start.7 = (bf16[2,128,1024]{2,1,0:T(8,128)(2,1)}, bf16[2,128,1024]{2,1,0:T(8,128)(2,1)S(1)}, u32[]{:S(2)}) copy-start(bf16[2,128,1024]{2,1,0:T(8,128)(2,1)S(1)} %collective-permute-done.8.two_down) | copy-start | bytes 1572868
  116.2 13.1 %all-to-all-start = ((bf16[8,64,384]{2,1,0:T(8,128)(2,1)}), bf16[8,64,384]{2,1,0:T(8,128)(2,1)S(1)}, u32[]{:S(2)}, u32[]{:S(2)}) async-start(bf16[8,64,384]{2,1,0:T(8,128)(2,1)} %bitcast.11), calls=%async_computation | async-start | bytes 786432 | tf_op jit(solution)/shard_map/all_to_all | solution.py:309
  129.6 19.6 %collective-permute-start.10 = (bf16[64,2176]{1,0:T(8,128)(2,1)S(1)}, bf16[64,2176]{1,0:T(8,128)(2,1)S(1)}, u32[]{:S(2)}, u32[]{:S(2)}) collective-permute-start(bf16[64,2176]{1,0:T(8,128)(2,1)S(1)} %get-tuple-element.42.q0), channel_id=1, source_target_pairs={{2,0},{3,1},{4,2},{5,3},{6,4},{7,5},{8,6},{9,7},{10,8},{11,9},{12,... | collective-permute-start | bytes 835592 | tf_op jit(solution)/shard_map/ppermute | solution.py:334
  134.3 14.8 %collective-permute-start.9 = (bf16[64,2176]{1,0:T(8,128)(2,1)S(1)}, bf16[64,2176]{1,0:T(8,128)(2,1)S(1)}, u32[]{:S(2)}, u32[]{:S(2)}) collective-permute-start(bf16[64,2176]{1,0:T(8,128)(2,1)S(1)} %get-tuple-element.42.q0), channel_id=1, source_target_pairs={{1,0},{2,1},{3,2},{4,3},{5,4},{6,5},{7,6},{8,7},{9,8},{10,9},{11,1... | collective-permute-start | bytes 835592 | tf_op jit(solution)/shard_map/ppermute | solution.py:334
  155.6 7.4 %collective-permute-start.13 = (bf16[64,2176]{1,0:T(8,128)(2,1)S(1)}, bf16[64,2176]{1,0:T(8,128)(2,1)S(1)}, u32[]{:S(2)}, u32[]{:S(2)}) collective-permute-start(bf16[64,2176]{1,0:T(8,128)(2,1)S(1)} %get-tuple-element.53), channel_id=1, source_target_pairs={{0,1},{1,2},{2,3},{3,4},{4,5},{5,6},{6,7},{7,8},{8,9},{9,10},{10,1... | collective-permute-start | bytes 835592 | tf_op jit(solution)/shard_map/ppermute | solution.py:334
  157.5 15.5 %collective-permute-start.14 = (bf16[64,2176]{1,0:T(8,128)(2,1)S(1)}, bf16[64,2176]{1,0:T(8,128)(2,1)S(1)}, u32[]{:S(2)}, u32[]{:S(2)}) collective-permute-start(bf16[64,2176]{1,0:T(8,128)(2,1)S(1)} %get-tuple-element.54), channel_id=1, source_target_pairs={{0,2},{1,3},{2,4},{3,5},{4,6},{5,7},{6,8},{7,9},{8,10},{9,11},{10,... | collective-permute-start | bytes 835592 | tf_op jit(solution)/shard_map/ppermute | solution.py:334
  159.5 1.6 copy-start.1
Sparse Core Ops, SparseCore 0:
  10.2 39.4 all-gather.2
  64.4 45.4 all-gather.4

commit v6 on v5

--- a/solution.py
+++ b/solution.py
@@ -11,6 +11,7 @@
 HD = 128
 GROUP = QH // KH
 BLOCK = 128
+WIDE = 1024
 BASE = 10000.0
 NX, NC = 4, 2
 CAP = 2
@@ -51,13 +52,13 @@
         here = pl.ds(slot * rows, rows)
         pltpu.make_async_copy(pool.at[here], staged.at[here], sem.at[slot]).wait()
     slots = {
-        1: (one_up.at[0], one_up.at[1]),
+        1: (one_up.at[pl.ds(0, rows)], one_up.at[pl.ds(rows, rows)]),
         2: (two_up.at[0], two_up.at[1]),
         3: (three_up.at[0], three_up.at[1]),
-        4: (one_up.at[2], one_down.at[2]),
+        4: (one_up.at[pl.ds(2 * rows, rows)], one_down.at[pl.ds(2 * rows, rows)]),
         5: (three_down.at[0], three_down.at[1]),
         6: (two_down.at[0], two_down.at[1]),
-        7: (one_down.at[0], one_down.at[1]),
+        7: (one_down.at[pl.ds(0, rows)], one_down.at[pl.ds(rows, rows)]),
     }
     for d in range(traces):
         t = lax.rem(mine + d, traces)
@@ -89,6 +90,55 @@
             pltpu.make_async_copy(
                 staged.at[pl.ds(slot * rows, rows)], two_up.at[0], out_sem.at[slot]
             ).wait()
+
+
+def tiles(w):
+    n = 0
+    for part in range(w.shape[0]):
+        for r in range(0, w.shape[1], 16):
+            for c in range(0, w.shape[2], HD):
+                at = (pl.ds(n * HD // WIDE * 16, 16), pl.ds(n * HD % WIDE, HD))
+                yield at, (part, pl.ds(r, 16), pl.ds(c, HD))
+                n += 1
+
+
+def pack_kernel(y, e0, e2, e4, e6, up_in, down_in, up, down, w, all_w, packed, sem):
+    for k, e in enumerate((e0, e2, e4, e6)):
+        all_w[k] = e[...]
+    for n in range(w.shape[0]):
+        w[n] = all_w[n ^ (y[0] // 2)]
+    for at, place in tiles(w):
+        packed[at] = w[place]
+    size = packed.shape[0]
+    copies = [
+        pltpu.make_async_copy(packed, to.at[pl.ds(to.shape[0] - size, size)], sem.at[i])
+        for i, to in enumerate((up, down))
+    ]
+    for copy in copies:
+        copy.start()
+    for copy in copies:
+        copy.wait()
+
+
+def unpack_kernel(y, w, up, down, out, other, packed, sem):
+    tail = pl.ds(up.shape[0] - packed.shape[0], packed.shape[0])
+    odd = lax.rem(y[0], 2)
+
+    @pl.when(odd == 1)
+    def _():
+        pltpu.make_async_copy(up.at[tail], packed, sem).start()
+
+    @pl.when(odd == 0)
+    def _():
+        pltpu.make_async_copy(down.at[tail], packed, sem).start()
+
+    for n in range(w.shape[0]):
+        out[2 * n + odd] = w[n]
+    pltpu.make_async_copy(up.at[tail], packed, sem).wait()
+    for at, place in tiles(w):
+        other[place] = packed[at]
+    for n in range(w.shape[0]):
+        out[2 * n + 1 - odd] = other[n]
 
 
 def head(ref, n):
@@ -159,13 +209,13 @@
     mine = me[0]
     own = [owner[mine, b] // blocks for b in range(blocks)]
     slots = {
-        1: (one_up.at[0], one_up.at[1]),
+        1: (one_up.at[pl.ds(0, rows)], one_up.at[pl.ds(rows, rows)]),
         2: (two_up.at[0], two_up.at[1]),
         3: (three_up.at[0], three_up.at[1]),
         4: (three_up.at[2], three_down.at[2]),
         5: (three_down.at[0], three_down.at[1]),
         6: (two_down.at[0], two_down.at[1]),
-        7: (one_down.at[0], one_down.at[1]),
+        7: (one_down.at[pl.ds(0, rows)], one_down.at[pl.ds(rows, rows)]),
     }
     for b in range(blocks):
         here = kv.at[pl.ds(b * rows, rows)]
@@ -266,12 +316,15 @@
     def turned(array, by):
         return lax.ppermute(array, "y", [(i, (i + by) % ny) for i in range(ny)])
 
+    tail = 4 * w_qkv.size // kvw
+    tall = 3 * block_len + tail
+
     def room(n):
         return pltpu.HBM((n, block_len, kvw), BF)
 
     one_up, one_down, two_up, two_down, three_up, three_down = call(
         pick_kernel,
-        (room(3), room(3), room(2), room(2), room(3), room(3)),
+        (pltpu.HBM((tall, kvw), BF),) * 2 + (room(2), room(2), room(3), room(3)),
         [SM, SM, ANY], (ANY,) * 6,
         [
             pltpu.SMEM((blocks,), jnp.int32),
@@ -285,24 +338,42 @@
         pairs = [(a * group + b, (b ^ m) * group + a) for a in range(ny) for b in range(group)]
         return lax.ppermute(w_qkv, ("y", "x", "c"), pairs)
 
-    def paired(mine, other, bit, axis):
-        low = (y // bit) % 2 == 0
-        return jnp.stack([jnp.where(low, mine, other), jnp.where(low, other, mine)], axis)
-
-    w = paired(
-        paired(crossed(0), crossed(4), 4, 0), paired(crossed(2), crossed(6), 4, 0), 2, 1
-    )
-    w = paired(w, lax.ppermute(w, "y", [(i, i ^ 1) for i in range(ny)]), 1, 2).reshape(-1, cols)
-    w, one_up, one_down, two_up, two_down = lax.optimization_barrier(
-        (w, one_up, one_down, two_up, two_down)
-    )
+    one_up, one_down, w = pl.pallas_call(
+        pack_kernel,
+        out_shape=(
+            pltpu.HBM((tall, kvw), BF),
+            pltpu.HBM((tall, kvw), BF),
+            jax.ShapeDtypeStruct((4,) + w_qkv.shape, BF),
+        ),
+        in_specs=[SM] + [VM] * 4 + [ANY] * 2,
+        out_specs=(ANY, ANY, VM),
+        scratch_shapes=[
+            pltpu.VMEM((4,) + w_qkv.shape, BF),
+            pltpu.VMEM((tail, kvw), BF),
+            pltpu.SemaphoreType.DMA((2,)),
+        ],
+        input_output_aliases={5: 0, 6: 1},
+        compiler_params=pltpu.CompilerParams(vmem_limit_bytes=8 << 20),
+    )(me, crossed(0), crossed(2), crossed(4), crossed(6), *kept(one_up, one_down))
     one_up, one_down = turned(one_up, 1), turned(one_down, -1)
+    w = call(
+        unpack_kernel,
+        jax.ShapeDtypeStruct((8,) + w_qkv.shape, BF),
+        [SM, VM] + [pl.BlockSpec(memory_space=pl.ANY)] * 2, VM,
+        [
+            pltpu.VMEM((4,) + w_qkv.shape, BF),
+            pltpu.VMEM((tail, kvw), BF),
+            pltpu.SemaphoreType.DMA,
+        ],
+        moved=8 * w_qkv.size,
+    )(me, w, one_up, one_down).reshape(-1, cols)
+    w, two_up, two_down = lax.optimization_barrier((w, two_up, two_down))
     two_up, two_down = turned(two_up, 2), turned(two_down, -2)
     hidden = lax.all_gather(sel_hidden.reshape(rows, d), XC, axis=0, tiled=True)
-    w, hidden, one_up, one_down = lax.optimization_barrier((w, hidden, one_up, one_down))
+    w, hidden = lax.optimization_barrier((w, hidden))
     w = lax.all_gather(w, "z", axis=0, tiled=True)
-    three_up = turned(lax.dynamic_update_slice(three_up, one_up[2:], (2, 0, 0)), 3)
-    three_down = turned(lax.dynamic_update_slice(three_down, one_down[2:], (2, 0, 0)), -3)
+    three_up = turned(lax.dynamic_update_slice(three_up, one_up[2 * block_len : 3 * block_len][None], (2, 0, 0)), 3)
+    three_down = turned(lax.dynamic_update_slice(three_down, one_down[2 * block_len : 3 * block_len][None], (2, 0, 0)), -3)
     hidden, w, two_up, two_down = lax.optimization_barrier((hidden, w, two_up, two_down))
     projected = jnp.dot(hidden, w, preferred_element_type=F32).astype(BF)
     projected = projected.reshape(group, rows, cols)

time: 182 us -> 182 us (level)
  the two profiles are of different devices: /device:TPU:273 before, /device:TPU:265 now
where the time goes in v6:
time: 182 us; the launch traced here: 181 us
  waiting for transfers between devices  75.8 us (42%)
  starting transfers between devices  59.2 us (33%)
  Pallas kernels  14.8 us (8%)
  between operations  14.4 us (8%)
  local copies, waits for them, and re-layouts  6.25 us (3%)
  matrix products  6.24 us (3%)
  other arithmetic  4.66 us (3%)
    ppermute x6, waiting for transfers between devices, turned(): return lax.ppermute(array, 'y', [(i, (i + by) % ny) for i in range(ny)])  36.3 us
    ppermute x6, starting transfers between devices, turned(): return lax.ppermute(array, 'y', [(i, (i + by) % ny) for i in range(ny)])  23.7 us
    all_gather x1, waiting for transfers between devices, on_device(): w = lax.all_gather(w, 'z', axis=0, tiled=True)  22.6 us
    ppermute x4, starting transfers between devices, crossed(): return lax.ppermute(w_qkv, ('y', 'x', 'c'), pairs)  19.1 us
    ppermute x4, starting transfers between devices, along(): return lax.ppermute(array, SEQ, pairs)  11.3 us
    ppermute x4, waiting for transfers between devices, along(): return lax.ppermute(array, SEQ, pairs)  10.4 us
    pallas_call x1, Pallas kernels, on_device(): call(blend_kernel, (pltpu.HBM((tokens, kvw), BF), partial, partial), [SM,...  6.46 us
    dot_general x1, matrix products, on_device(): projected = jnp.dot(hidden, w, preferred_element_type=F32).astype(BF)  6.24 us
  transfers between devices with their start and end apart: 17, of which 8 were waited for; matrix products, arithmetic and copies ran while one was open for 8% of the time, Pallas kernels for 4%

profile of v6, /device:TPU:265, one launch (start us, length us, event | category | flops | bytes accessed | tf_op | source)
XLA Modules:
  0.0 181.3 jit_solution(13681524948433354631)
XLA Ops:
  8.0 1.5 collective-permute-start
  9.4 5.7 %collective-permute-start.1 = (bf16[64,384]{1,0:T(8,128)(2,1)}, bf16[64,384]{1,0:T(8,128)(2,1)S(1)}, u32[]{:S(2)}, u32[]{:S(2)}) collective-permute-start(bf16[64,384]{1,0:T(8,128)(2,1)} %param.8), channel_id=1, source_target_pairs={{0,128},{1,192},{2,0},{3,64},{4,384},{5,448},{6,256},{7,320},{64,1... | collective-permute-start | bytes 147464 | tf_op jit(solution)/shard_map/ppermute | solution.py:339
  15.1 9.3 %collective-permute-start.2 = (bf16[64,384]{1,0:T(8,128)(2,1)}, bf16[64,384]{1,0:T(8,128)(2,1)S(1)}, u32[]{:S(2)}, u32[]{:S(2)}) collective-permute-start(bf16[64,384]{1,0:T(8,128)(2,1)} %param.8), channel_id=1, source_target_pairs={{0,256},{1,320},{2,384},{3,448},{4,0},{5,64},{6,128},{7,192},{64,2... | collective-permute-start | bytes 147464 | tf_op jit(solution)/shard_map/ppermute | solution.py:339
  24.4 2.8 %collective-permute-start.3 = (bf16[64,384]{1,0:T(8,128)(2,1)}, bf16[64,384]{1,0:T(8,128)(2,1)S(1)}, u32[]{:S(2)}, u32[]{:S(2)}) collective-permute-start(bf16[64,384]{1,0:T(8,128)(2,1)} %param.8), channel_id=1, source_target_pairs={{0,384},{1,448},{2,256},{3,320},{4,128},{5,192},{6,0},{7,64},{64,3... | collective-permute-start | bytes 147464 | tf_op jit(solution)/shard_map/ppermute | solution.py:339
  27.8 3.4 %shard_map.86 = (bf16[480,1024]{1,0:T(8,128)(2,1)}, bf16[480,1024]{1,0:T(8,128)(2,1)}, bf16[2,128,1024]{2,1,0:T(8,128)(2,1)}, bf16[2,128,1024]{2,1,0:T(8,128)(2,...) custom-call(s32[8,8]{1,0:T(8,128)S(1)} %copy-done.4, s32[1]{0:T(128)} %bitcast.me.y, ...), custom_call_target="tpu_custom_call" | custom-call | bytes 4194304 | tf_op jit(solution)/shard_map/pallas_call | solution.py:325
  32.1 6.0 %collective-permute-start.4 = (bf16[480,1024]{1,0:T(8,128)(2,1)}, bf16[480,1024]{1,0:T(8,128)(2,1)S(1)}, u32[]{:S(2)}, u32[]{:S(2)}) collective-permute-start(bf16[480,1024]{1,0:T(8,128)(2,1)} %get-tuple-element.31), channel_id=1, source_target_pairs={{0,64},{64,128},{128,192},{192,256},{256,320},{320,384},{384,448},... | collective-permute-start | bytes 2949128 | tf_op jit(solution)/shard_map/ppermute | solution.py:317
  38.1 1.9 %collective-permute-start.5 = (bf16[480,1024]{1,0:T(8,128)(2,1)}, bf16[480,1024]{1,0:T(8,128)(2,1)S(1)}, u32[]{:S(2)}, u32[]{:S(2)}) collective-permute-start(bf16[480,1024]{1,0:T(8,128)(2,1)} %get-tuple-element.32), channel_id=1, source_target_pairs={{0,448},{64,0},{128,64},{192,128},{256,192},{320,256},{384,320},{4... | collective-permute-start | bytes 2949128 | tf_op jit(solution)/shard_map/ppermute | solution.py:317
  40.1 18.0 %collective-permute-done.4.up.one_up = bf16[480,1024]{1,0:T(8,128)(2,1)S(1)} collective-permute-done((bf16[480,1024]{1,0:T(8,128)(2,1)}, bf16[480,1024]{1,0:T(8,128)(2,1)S(1)}, u32[]{:S(2)}, u32[]{:S(2)}) %collective-permute-start.4) | collective-permute-done | bytes 983072 | tf_op jit(solution)/shard_map/ppermute | solution.py:317
  58.1 3.7 %collective-permute-done.5.down.one_down = bf16[480,1024]{1,0:T(8,128)(2,1)S(1)} collective-permute-done((bf16[480,1024]{1,0:T(8,128)(2,1)}, bf16[480,1024]{1,0:T(8,128)(2,1)S(1)}, u32[]{:S(2)}, u32[]{:S(2)}) %collective-permute-start.5) | collective-permute-done | bytes 983072 | tf_op jit(solution)/shard_map/ppermute | solution.py:317
  61.8 1.1 shard_map.88
  64.9 3.6 %collective-permute-start.6 = (bf16[2,128,1024]{2,1,0:T(8,128)(2,1)}, bf16[2,128,1024]{2,1,0:T(8,128)(2,1)}, u32[]{:S(2)}, u32[]{:S(2)}) collective-permute-start(bf16[2,128,1024]{2,1,0:T(8,128)(2,1)} %get-tuple-element.38), channel_id=1, source_target_pairs={{0,128},{64,192},{128,256},{192,320},{256,384},{320,448},{384,0},{... | collective-permute-start | bytes 1572872 | tf_op jit(solution)/shard_map/ppermute | solution.py:317
  68.5 3.8 %collective-permute-start.7 = (bf16[2,128,1024]{2,1,0:T(8,128)(2,1)}, bf16[2,128,1024]{2,1,0:T(8,128)(2,1)}, u32[]{:S(2)}, u32[]{:S(2)}) collective-permute-start(bf16[2,128,1024]{2,1,0:T(8,128)(2,1)} %get-tuple-element.39), channel_id=1, source_target_pairs={{0,384},{64,448},{128,0},{192,64},{256,128},{320,192},{384,256},{4... | collective-permute-start | bytes 1572872 | tf_op jit(solution)/shard_map/ppermute | solution.py:317
  73.7 1.9 %collective-permute-start.11 = (bf16[3,128,1024]{2,1,0:T(8,128)(2,1)}, bf16[3,128,1024]{2,1,0:T(8,128)(2,1)S(1)}, u32[]{:S(2)}, u32[]{:S(2)}) collective-permute-start(bf16[3,128,1024]{2,1,0:T(8,128)(2,1)} %fusion), channel_id=1, source_target_pairs={{0,320},{64,384},{128,448},{192,0},{256,64},{320,128},{384,192},{4... | collective-permute-start | bytes 2359304 | tf_op jit(solution)/shard_map/ppermute | solution.py:317
  76.4 6.5 %collective-permute-start.10 = (bf16[3,128,1024]{2,1,0:T(8,128)(2,1)}, bf16[3,128,1024]{2,1,0:T(8,128)(2,1)S(1)}, u32[]{:S(2)}, u32[]{:S(2)}) collective-permute-start(bf16[3,128,1024]{2,1,0:T(8,128)(2,1)} %fusion.1), channel_id=1, source_target_pairs={{0,192},{64,256},{128,320},{192,384},{256,448},{320,0},{384,64},{4... | collective-permute-start | bytes 2359304 | tf_op jit(solution)/shard_map/ppermute | solution.py:317
  82.8 2.8 %collective-permute-done.6.two_up = bf16[2,128,1024]{2,1,0:T(8,128)(2,1)} collective-permute-done((bf16[2,128,1024]{2,1,0:T(8,128)(2,1)}, bf16[2,128,1024]{2,1,0:T(8,128)(2,1)}, u32[]{:S(2)}, u32[]{:S(2)}) %collective-permute-start.6) | collective-permute-done | bytes 524320 | tf_op jit(solution)/shard_map/ppermute | solution.py:317
  85.7 1.8 collective-permute-done.7.two_down
  87.5 22.6 %all-gather.5.cloned.1.call-done = bf16[4096,384]{1,0:T(8,128)(2,1)} async-done(((bf16[512,384]{1,0:T(8,128)(2,1)}), bf16[4096,384]{1,0:T(8,128)(2,1)}) %all-gather.5.cloned.1.call-update) | async-done | bytes 3145744 | tf_op jit(solution)/shard_map/all_gather | solution.py:374
  110.1 6.2 %convolution_convert_fusion = bf16[512,384]{1,0:T(8,128)(2,1)} fusion(bf16[512,4096]{1,0:T(8,128)(2,1)} %all-gather.3.cloned.1.call-done, bf16[4096,384]{1,0:T(8,128)(2,1)} %all-gather.5.cloned.1.call-done), kind=kOutput, calls=%fused_computation | convolution fusion | flops 1610809344 | bytes 7733248 | tf_op jit(solution)/shard_map/dot_general | solution.py:378
  116.4 5.0 %all-to-all-start = ((bf16[8,64,384]{2,1,0:T(8,128)(2,1)}), bf16[8,64,384]{2,1,0:T(8,128)(2,1)S(1)}, u32[]{:S(2)}, u32[]{:S(2)}) async-start(bf16[8,64,384]{2,1,0:T(8,128)(2,1)} %bitcast.24), calls=%async_computation | async-start | bytes 786432 | tf_op jit(solution)/shard_map/all_to_all | solution.py:380
  122.0 0.9 pad_maximum_fusion
  123.7 5.7 %all-to-all-done.proj = bf16[8,64,384]{2,1,0:T(8,128)(2,1)S(1)} async-done(((bf16[8,64,384]{2,1,0:T(8,128)(2,1)}), bf16[8,64,384]{2,1,0:T(8,128)(2,1)S(1)}, u32[]{:S(2)}, u32[]{:S(2)}) %all-to-all-start) | async-done | bytes 393248 | tf_op jit(solution)/shard_map/all_to_all | solution.py:380
  129.6 2.8 %collective-permute-start.8 = (bf16[64,2176]{1,0:T(8,128)(2,1)S(1)}, bf16[64,2176]{1,0:T(8,128)(2,1)S(1)}, u32[]{:S(2)}, u32[]{:S(2)}) collective-permute-start(bf16[64,2176]{1,0:T(8,128)(2,1)S(1)} %get-tuple-element.42.q0), channel_id=1, source_target_pairs={{1,0},{2,1},{3,2},{4,3},{5,4},{6,5},{7,6},{8,7},{9,8},{10,9},{11,1... | collective-permute-start | bytes 835592 | tf_op jit(solution)/shard_map/ppermute | solution.py:405
  132.4 4.7 %collective-permute-start.9 = (bf16[64,2176]{1,0:T(8,128)(2,1)S(1)}, bf16[64,2176]{1,0:T(8,128)(2,1)S(1)}, u32[]{:S(2)}, u32[]{:S(2)}) collective-permute-start(bf16[64,2176]{1,0:T(8,128)(2,1)S(1)} %get-tuple-element.42.q0), channel_id=1, source_target_pairs={{2,0},{3,1},{4,2},{5,3},{6,4},{7,5},{8,6},{9,7},{10,8},{11,9},{12,... | collective-permute-start | bytes 835592 | tf_op jit(solution)/shard_map/ppermute | solution.py:405
  138.1 9.9 %collective-permute-done.11.three_down = bf16[3,128,1024]{2,1,0:T(8,128)(2,1)S(1)} collective-permute-done((bf16[3,128,1024]{2,1,0:T(8,128)(2,1)}, bf16[3,128,1024]{2,1,0:T(8,128)(2,1)S(1)}, u32[]{:S(2)}, u32[]{:S(2)}) %collective-permute-start.11) | collective-permute-done | bytes 786464 | tf_op jit(solution)/shard_map/ppermute | solution.py:317
  148.1 0.9 copy-done.6
  149.2 6.5 %shard_map.90 = (bf16[1024,1024]{1,0:T(8,128)(2,1)}, bf16[64,2176]{1,0:T(8,128)(2,1)S(1)}, bf16[64,2176]{1,0:T(8,128)(2,1)S(1)}) custom-call(s32[8,8]{1,0:T(8,128)S(1)} %copy-done.5, s32[1]{0:T(128)} %bitcast.me.y, f32[8,128]{1,0:T(8,128)S(1)} %get-tuple-element.64.kcos, f32[8,128]{1,0:T(8,128)S(1)} %get-tuple-element.65.ksin, ...), custom_call_target="tpu_custom_call" | custom-call | flops 1073741824 | bytes 4194304 | tf_op jit(solution)/shard_map/pallas_call | solution.py:409
  155.7 1.9 %collective-permute-start.12 = (bf16[64,2176]{1,0:T(8,128)(2,1)S(1)}, bf16[64,2176]{1,0:T(8,128)(2,1)S(1)}, u32[]{:S(2)}, u32[]{:S(2)}) collective-permute-start(bf16[64,2176]{1,0:T(8,128)(2,1)S(1)} %get-tuple-element.51), channel_id=1, source_target_pairs={{0,1},{1,2},{2,3},{3,4},{4,5},{5,6},{6,7},{7,8},{8,9},{9,10},{10,1... | collective-permute-start | bytes 835592 | tf_op jit(solution)/shard_map/ppermute | solution.py:405
  157.6 1.9 %collective-permute-start.13 = (bf16[64,2176]{1,0:T(8,128)(2,1)S(1)}, bf16[64,2176]{1,0:T(8,128)(2,1)S(1)}, u32[]{:S(2)}, u32[]{:S(2)}) collective-permute-start(bf16[64,2176]{1,0:T(8,128)(2,1)S(1)} %get-tuple-element.52), channel_id=1, source_target_pairs={{0,2},{1,3},{2,4},{3,5},{4,6},{5,7},{6,8},{7,9},{8,10},{9,11},{10,... | collective-permute-start | bytes 835592 | tf_op jit(solution)/shard_map/ppermute | solution.py:405
  159.7 1.6 copy-done.3
  161.2 1.8 %shard_map.91 = (f32[64,2048]{1,0:T(8,128)S(1)}, f32[64,128]{1,0:T(8,128)S(1)}) custom-call(bf16[64,2176]{1,0:T(8,128)(2,1)S(1)} %get-tuple-element.42.q0, bf16[1024,1024]{1,0:T(8,128)(2,1)S(1)} %copy-done.3), custom_call_target="tpu_custom_call" | custom-call | flops 536870912 | bytes 2097152 | tf_op jit(solution)/shard_map/pallas_call | solution.py:428
  163.1 10.4 %collective-permute-done.13.r2 = bf16[64,2176]{1,0:T(8,128)(2,1)S(1)} collective-permute-done((bf16[64,2176]{1,0:T(8,128)(2,1)S(1)}, bf16[64,2176]{1,0:T(8,128)(2,1)S(1)}, u32[]{:S(2)}, u32[]{:S(2)}) %collective-permute-start.13) | collective-permute-done | bytes 278560 | tf_op jit(solution)/shard_map/ppermute | solution.py:405
  173.4 1.0 shard_map.92
  (60 shorter events, 9.4 us)
Async XLA Ops:
  7.2 56.1 %copy-start = (s32[8,32]{1,0:T(8,128)S(1)}, s32[8,32]{1,0:T(8,128)}, u32[]{:S(2)}) copy-start(s32[8,32]{1,0:T(8,128)} %param.11) | copy-start | bytes 3076
  7.2 55.7 %all-gather.3.cloned.1.call-start = ((), (), s32[]{:S(2)}) async-start(), calls=%async_computation.1 | async-start | bytes 4718592 | tf_op jit(solution)/shard_map/all_gather | solution.py:372
  7.9 102.2 %all-gather.5.cloned.1.call-start = ((), (), s32[]{:S(2)}) async-start(), calls=%async_computation.2 | async-start | bytes 3538944 | tf_op jit(solution)/shard_map/all_gather | solution.py:374
  8.0 23.3 %collective-permute-start = (bf16[64,384]{1,0:T(8,128)(2,1)}, bf16[64,384]{1,0:T(8,128)(2,1)S(1)}, u32[]{:S(2)}, u32[]{:S(2)}) collective-permute-start(bf16[64,384]{1,0:T(8,128)(2,1)} %param.8), channel_id=1, source_target_pairs={{0,0},{1,64},{2,128},{3,192},{4,256},{5,320},{6,384},{7,448},{64,1... | collective-permute-start | bytes 147464 | tf_op jit(solution)/shard_map/ppermute | solution.py:339
  9.4 21.8 %collective-permute-start.1 = (bf16[64,384]{1,0:T(8,128)(2,1)}, bf16[64,384]{1,0:T(8,128)(2,1)S(1)}, u32[]{:S(2)}, u32[]{:S(2)}) collective-permute-start(bf16[64,384]{1,0:T(8,128)(2,1)} %param.8), channel_id=1, source_target_pairs={{0,128},{1,192},{2,0},{3,64},{4,384},{5,448},{6,256},{7,320},{64,1... | collective-permute-start | bytes 147464 | tf_op jit(solution)/shard_map/ppermute | solution.py:339
  15.1 16.2 %collective-permute-start.2 = (bf16[64,384]{1,0:T(8,128)(2,1)}, bf16[64,384]{1,0:T(8,128)(2,1)S(1)}, u32[]{:S(2)}, u32[]{:S(2)}) collective-permute-start(bf16[64,384]{1,0:T(8,128)(2,1)} %param.8), channel_id=1, source_target_pairs={{0,256},{1,320},{2,384},{3,448},{4,0},{5,64},{6,128},{7,192},{64,2... | collective-permute-start | bytes 147464 | tf_op jit(solution)/shard_map/ppermute | solution.py:339
  24.4 6.9 %collective-permute-start.3 = (bf16[64,384]{1,0:T(8,128)(2,1)}, bf16[64,384]{1,0:T(8,128)(2,1)S(1)}, u32[]{:S(2)}, u32[]{:S(2)}) collective-permute-start(bf16[64,384]{1,0:T(8,128)(2,1)} %param.8), channel_id=1, source_target_pairs={{0,384},{1,448},{2,256},{3,320},{4,128},{5,192},{6,0},{7,64},{64,3... | collective-permute-start | bytes 147464 | tf_op jit(solution)/shard_map/ppermute | solution.py:339
  27.1 0.7 copy-start.4
  27.8 35.3 %copy-start.8 = (s32[1,8,8]{2,1,0:T(8,128)S(1)}, s32[1,8,8]{2,1,0:T(8,128)}, u32[]{:S(2)}) copy-start(s32[1,8,8]{2,1,0:T(8,128)} %param.12) | copy-start | bytes 772
  27.8 35.6 %copy-start.11 = (s32[1,8]{1,0:T(1,128)S(1)}, s32[1,8]{1,0:T(1,128)}, u32[]{:S(2)}) copy-start(s32[1,8]{1,0:T(1,128)} %param.13) | copy-start | bytes 100
  32.1 26.0 %collective-permute-start.4 = (bf16[480,1024]{1,0:T(8,128)(2,1)}, bf16[480,1024]{1,0:T(8,128)(2,1)S(1)}, u32[]{:S(2)}, u32[]{:S(2)}) collective-permute-start(bf16[480,1024]{1,0:T(8,128)(2,1)} %get-tuple-element.31), channel_id=1, source_target_pairs={{0,64},{64,128},{128,192},{192,256},{256,320},{320,384},{384,448},... | collective-permute-start | bytes 2949128 | tf_op jit(solution)/shard_map/ppermute | solution.py:317
  38.1 23.7 %collective-permute-start.5 = (bf16[480,1024]{1,0:T(8,128)(2,1)}, bf16[480,1024]{1,0:T(8,128)(2,1)S(1)}, u32[]{:S(2)}, u32[]{:S(2)}) collective-permute-start(bf16[480,1024]{1,0:T(8,128)(2,1)} %get-tuple-element.32), channel_id=1, source_target_pairs={{0,448},{64,0},{128,64},{192,128},{256,192},{320,256},{384,320},{4... | collective-permute-start | bytes 2949128 | tf_op jit(solution)/shard_map/ppermute | solution.py:317
  58.1 58.3 %copy-start.1 = (bf16[480,1024]{1,0:T(8,128)(2,1)}, bf16[480,1024]{1,0:T(8,128)(2,1)S(1)}, u32[]{:S(2)}) copy-start(bf16[480,1024]{1,0:T(8,128)(2,1)S(1)} %collective-permute-done.4.up.one_up) | copy-start | bytes 2949124
  61.8 54.6 %copy-start.2 = (bf16[480,1024]{1,0:T(8,128)(2,1)}, bf16[480,1024]{1,0:T(8,128)(2,1)S(1)}, u32[]{:S(2)}) copy-start(bf16[480,1024]{1,0:T(8,128)(2,1)S(1)} %collective-permute-done.5.down.one_down) | copy-start | bytes 2949124
  63.2 9.7 %copy-start.10 = (f32[64]{0:T(128)}, f32[64]{0:T(128)S(1)}, u32[]{:S(2)}) copy-start(f32[64]{0:T(128)S(1)} %negate_power_fusion) | copy-start | bytes 772
  64.9 20.8 %collective-permute-start.6 = (bf16[2,128,1024]{2,1,0:T(8,128)(2,1)}, bf16[2,128,1024]{2,1,0:T(8,128)(2,1)}, u32[]{:S(2)}, u32[]{:S(2)}) collective-permute-start(bf16[2,128,1024]{2,1,0:T(8,128)(2,1)} %get-tuple-element.38), channel_id=1, source_target_pairs={{0,128},{64,192},{128,256},{192,320},{256,384},{320,448},{384,0},{... | collective-permute-start | bytes 1572872 | tf_op jit(solution)/shard_map/ppermute | solution.py:317
  68.5 19.0 %collective-permute-start.7 = (bf16[2,128,1024]{2,1,0:T(8,128)(2,1)}, bf16[2,128,1024]{2,1,0:T(8,128)(2,1)}, u32[]{:S(2)}, u32[]{:S(2)}) collective-permute-start(bf16[2,128,1024]{2,1,0:T(8,128)(2,1)} %get-tuple-element.39), channel_id=1, source_target_pairs={{0,384},{64,448},{128,0},{192,64},{256,128},{320,192},{384,256},{4... | collective-permute-start | bytes 1572872 | tf_op jit(solution)/shard_map/ppermute | solution.py:317
  73.7 74.3 %collective-permute-start.11 = (bf16[3,128,1024]{2,1,0:T(8,128)(2,1)}, bf16[3,128,1024]{2,1,0:T(8,128)(2,1)S(1)}, u32[]{:S(2)}, u32[]{:S(2)}) collective-permute-start(bf16[3,128,1024]{2,1,0:T(8,128)(2,1)} %fusion), channel_id=1, source_target_pairs={{0,320},{64,384},{128,448},{192,0},{256,64},{320,128},{384,192},{4... | collective-permute-start | bytes 2359304 | tf_op jit(solution)/shard_map/ppermute | solution.py:317
  76.4 72.9 %copy-start.5 = (s32[8,8]{1,0:T(8,128)S(1)}, s32[8,8]{1,0:T(8,128)}, u32[]{:S(2)}) copy-start(s32[8,8]{1,0:T(8,128)} %owner.3) | copy-start | bytes 772
  76.4 71.7 %collective-permute-start.10 = (bf16[3,128,1024]{2,1,0:T(8,128)(2,1)}, bf16[3,128,1024]{2,1,0:T(8,128)(2,1)S(1)}, u32[]{:S(2)}, u32[]{:S(2)}) collective-permute-start(bf16[3,128,1024]{2,1,0:T(8,128)(2,1)} %fusion.1), channel_id=1, source_target_pairs={{0,192},{64,256},{128,320},{192,384},{256,448},{320,0},{384,64},{4... | collective-permute-start | bytes 2359304 | tf_op jit(solution)/shard_map/ppermute | solution.py:317
  116.4 13.0 %all-to-all-start = ((bf16[8,64,384]{2,1,0:T(8,128)(2,1)}), bf16[8,64,384]{2,1,0:T(8,128)(2,1)S(1)}, u32[]{:S(2)}, u32[]{:S(2)}) async-start(bf16[8,64,384]{2,1,0:T(8,128)(2,1)} %bitcast.24), calls=%async_computation | async-start | bytes 786432 | tf_op jit(solution)/shard_map/all_to_all | solution.py:380
  129.6 18.4 %collective-permute-start.8 = (bf16[64,2176]{1,0:T(8,128)(2,1)S(1)}, bf16[64,2176]{1,0:T(8,128)(2,1)S(1)}, u32[]{:S(2)}, u32[]{:S(2)}) collective-permute-start(bf16[64,2176]{1,0:T(8,128)(2,1)S(1)} %get-tuple-element.42.q0), channel_id=1, source_target_pairs={{1,0},{2,1},{3,2},{4,3},{5,4},{6,5},{7,6},{8,7},{9,8},{10,9},{11,1... | collective-permute-start | bytes 835592 | tf_op jit(solution)/shard_map/ppermute | solution.py:405
  132.4 15.6 %collective-permute-start.9 = (bf16[64,2176]{1,0:T(8,128)(2,1)S(1)}, bf16[64,2176]{1,0:T(8,128)(2,1)S(1)}, u32[]{:S(2)}, u32[]{:S(2)}) collective-permute-start(bf16[64,2176]{1,0:T(8,128)(2,1)S(1)} %get-tuple-element.42.q0), channel_id=1, source_target_pairs={{2,0},{3,1},{4,2},{5,3},{6,4},{7,5},{8,6},{9,7},{10,8},{11,9},{12,... | collective-permute-start | bytes 835592 | tf_op jit(solution)/shard_map/ppermute | solution.py:405
  148.0 0.9 copy-start.6
  148.0 1.2 copy-start.7
  149.2 10.3 %copy-start.9 = (s32[8,8]{1,0:T(8,128)S(1)}, s32[8,8]{1,0:T(8,128)}, u32[]{:S(2)}) copy-start(s32[8,8]{1,0:T(8,128)} %get-tuple-element.60) | copy-start | bytes 772
  155.7 7.4 %collective-permute-start.12 = (bf16[64,2176]{1,0:T(8,128)(2,1)S(1)}, bf16[64,2176]{1,0:T(8,128)(2,1)S(1)}, u32[]{:S(2)}, u32[]{:S(2)}) collective-permute-start(bf16[64,2176]{1,0:T(8,128)(2,1)S(1)} %get-tuple-element.51), channel_id=1, source_target_pairs={{0,1},{1,2},{2,3},{3,4},{4,5},{5,6},{6,7},{7,8},{8,9},{9,10},{10,1... | collective-permute-start | bytes 835592 | tf_op jit(solution)/shard_map/ppermute | solution.py:405
  157.6 15.8 %collective-permute-start.13 = (bf16[64,2176]{1,0:T(8,128)(2,1)S(1)}, bf16[64,2176]{1,0:T(8,128)(2,1)S(1)}, u32[]{:S(2)}, u32[]{:S(2)}) collective-permute-start(bf16[64,2176]{1,0:T(8,128)(2,1)S(1)} %get-tuple-element.52), channel_id=1, source_target_pairs={{0,2},{1,3},{2,4},{3,5},{4,6},{5,7},{6,8},{7,9},{8,10},{9,11},{10,... | collective-permute-start | bytes 835592 | tf_op jit(solution)/shard_map/ppermute | solution.py:405
  159.7 1.6 copy-start.3
Sparse Core Ops, SparseCore 0:
  10.2 39.9 all-gather.2
  63.1 47.0 all-gather.4

commit v7 on v5

--- a/solution.py
+++ b/solution.py
@@ -281,6 +281,9 @@
         ],
         moved=4 * tokens * kvw,
     )(block_owner, me, *kept(cache_pool[0]))
+    one_up, w_qkv = lax.optimization_barrier((one_up, w_qkv))
+    one_up, one_down = turned(one_up, 1), turned(one_down, -1)
+
     def crossed(m):
         pairs = [(a * group + b, (b ^ m) * group + a) for a in range(ny) for b in range(group)]
         return lax.ppermute(w_qkv, ("y", "x", "c"), pairs)
@@ -292,14 +295,14 @@
     w = paired(
         paired(crossed(0), crossed(4), 4, 0), paired(crossed(2), crossed(6), 4, 0), 2, 1
     )
+    w, one_up, one_down = lax.optimization_barrier((w, one_up, one_down))
     w = paired(w, lax.ppermute(w, "y", [(i, i ^ 1) for i in range(ny)]), 1, 2).reshape(-1, cols)
-    w, one_up, one_down, two_up, two_down = lax.optimization_barrier(
-        (w, one_up, one_down, two_up, two_down)
-    )
-    one_up, one_down = turned(one_up, 1), turned(one_down, -1)
+    w, two_up, two_down, one_up, one_down = lax.optimization_barrier(
+        (w, two_up, two_down, one_up, one_down)
+    )
     two_up, two_down = turned(two_up, 2), turned(two_down, -2)
     hidden = lax.all_gather(sel_hidden.reshape(rows, d), XC, axis=0, tiled=True)
-    w, hidden, one_up, one_down = lax.optimization_barrier((w, hidden, one_up, one_down))
+    w, hidden = lax.optimization_barrier((w, hidden))
     w = lax.all_gather(w, "z", axis=0, tiled=True)
     three_up = turned(lax.dynamic_update_slice(three_up, one_up[2:], (2, 0, 0)), 3)
     three_down = turned(lax.dynamic_update_slice(three_down, one_down[2:], (2, 0, 0)), -3)

time: 182 us -> 175 us (0.962)
  the two profiles are of different devices: /device:TPU:273 before, /device:TPU:281 now
where the time goes in v7:
time: 175 us; the launch traced here: 174 us
  starting transfers between devices  74.1 us (42%)
  waiting for transfers between devices  60.6 us (35%)
  between operations  14.5 us (8%)
  Pallas kernels  13 us (7%)
  matrix products  6.24 us (4%)
  local copies, waits for them, and re-layouts  3.68 us (2%)
  other arithmetic  1.8 us (1%)
    all_gather x1, waiting for transfers between devices, on_device(): w = lax.all_gather(w, 'z', axis=0, tiled=True)  28.6 us
    ppermute x4, starting transfers between devices, crossed(): return lax.ppermute(w_qkv, ('y', 'x', 'c'), pairs)  24.9 us
    ppermute x6, starting transfers between devices, turned(): return lax.ppermute(array, 'y', [(i, (i + by) % ny) for i in range(ny)])  20.9 us
    ppermute x4, starting transfers between devices, along(): return lax.ppermute(array, SEQ, pairs)  19.7 us
    ppermute x6, waiting for transfers between devices, turned(): return lax.ppermute(array, 'y', [(i, (i + by) % ny) for i in range(ny)])  9.41 us
    all_to_all x1, waiting for transfers between devices, on_device(): merged = lax.all_to_all(projected, XC, 0, 0, tiled=True)  7.9 us
    pallas_call x1, Pallas kernels, on_device(): call(blend_kernel, (pltpu.HBM((tokens, kvw), BF), partial, partial), [SM,...  6.48 us
    dot_general x1, matrix products, on_device(): projected = jnp.dot(hidden, w, preferred_element_type=F32).astype(BF)  6.24 us
  transfers between devices with their start and end apart: 18, of which 9 were waited for; matrix products, arithmetic and copies ran while one was open for 5% of the time, Pallas kernels for 3%

profile of v7, /device:TPU:281, one launch (start us, length us, event | category | flops | bytes accessed | tf_op | source)
XLA Modules:
  0.0 173.9 jit_solution(17813996093059381724)
XLA Ops:
  8.7 3.4 %shard_map.86 = (bf16[3,128,1024]{2,1,0:T(8,128)(2,1)}, bf16[3,128,1024]{2,1,0:T(8,128)(2,1)}, bf16[2,128,1024]{2,1,0:T(8,128)(2,1)}, bf16[2,128,1024]{2,1,0:T(8...) custom-call(s32[8,8]{1,0:T(8,128)S(1)} %copy-done.2, s32[1]{0:T(128)} %bitcast.me, ...), custom_call_target="tpu_custom_call" | custom-call | bytes 4194304 | tf_op jit(solution)/shard_map/pallas_call | solution.py:272
  12.1 4.5 %collective-permute-start.4 = (bf16[3,128,1024]{2,1,0:T(8,128)(2,1)}, bf16[3,128,1024]{2,1,0:T(8,128)(2,1)S(1)}, u32[]{:S(2)}, u32[]{:S(2)}) collective-permute-start(bf16[3,128,1024]{2,1,0:T(8,128)(2,1)} %get-tuple-element.34), channel_id=1, source_target_pairs={{0,64},{64,128},{128,192},{192,256},{256,320},{320,384},{384,448},... | collective-permute-start | bytes 2359304 | tf_op jit(solution)/shard_map/ppermute | solution.py:267
  16.6 1.9 %collective-permute-start.5 = (bf16[3,128,1024]{2,1,0:T(8,128)(2,1)}, bf16[3,128,1024]{2,1,0:T(8,128)(2,1)S(1)}, u32[]{:S(2)}, u32[]{:S(2)}) collective-permute-start(bf16[3,128,1024]{2,1,0:T(8,128)(2,1)} %get-tuple-element.35), channel_id=1, source_target_pairs={{0,448},{64,0},{128,64},{192,128},{256,192},{320,256},{384,320},{4... | collective-permute-start | bytes 2359304 | tf_op jit(solution)/shard_map/ppermute | solution.py:267
  18.5 1.9 %collective-permute-start = (bf16[64,384]{1,0:T(8,128)(2,1)}, bf16[64,384]{1,0:T(8,128)(2,1)S(1)}, u32[]{:S(2)}, u32[]{:S(2)}) collective-permute-start(bf16[64,384]{1,0:T(8,128)(2,1)} %param.8), channel_id=1, source_target_pairs={{0,0},{1,64},{2,128},{3,192},{4,256},{5,320},{6,384},{7,448},{64,1... | collective-permute-start | bytes 147464 | tf_op jit(solution)/shard_map/ppermute | solution.py:289
  20.5 7.4 %collective-permute-start.1 = (bf16[64,384]{1,0:T(8,128)(2,1)}, bf16[64,384]{1,0:T(8,128)(2,1)S(1)}, u32[]{:S(2)}, u32[]{:S(2)}) collective-permute-start(bf16[64,384]{1,0:T(8,128)(2,1)} %param.8), channel_id=1, source_target_pairs={{0,256},{1,320},{2,384},{3,448},{4,0},{5,64},{6,128},{7,192},{64,2... | collective-permute-start | bytes 147464 | tf_op jit(solution)/shard_map/ppermute | solution.py:289
  27.8 4.8 %collective-permute-start.2 = (bf16[64,384]{1,0:T(8,128)(2,1)}, bf16[64,384]{1,0:T(8,128)(2,1)S(1)}, u32[]{:S(2)}, u32[]{:S(2)}) collective-permute-start(bf16[64,384]{1,0:T(8,128)(2,1)} %param.8), channel_id=1, source_target_pairs={{0,128},{1,192},{2,0},{3,64},{4,384},{5,448},{6,256},{7,320},{64,1... | collective-permute-start | bytes 147464 | tf_op jit(solution)/shard_map/ppermute | solution.py:289
  32.7 3.2 %collective-permute-done = bf16[64,384]{1,0:T(8,128)(2,1)S(1)} collective-permute-done((bf16[64,384]{1,0:T(8,128)(2,1)}, bf16[64,384]{1,0:T(8,128)(2,1)S(1)}, u32[]{:S(2)}, u32[]{:S(2)}) %collective-permute-start) | collective-permute-done | bytes 49184 | tf_op jit(solution)/shard_map/ppermute | solution.py:289
  35.9 10.8 %collective-permute-start.3 = (bf16[64,384]{1,0:T(8,128)(2,1)}, bf16[64,384]{1,0:T(8,128)(2,1)S(1)}, u32[]{:S(2)}, u32[]{:S(2)}) collective-permute-start(bf16[64,384]{1,0:T(8,128)(2,1)} %param.8), channel_id=1, source_target_pairs={{0,384},{1,448},{2,256},{3,320},{4,128},{5,192},{6,0},{7,64},{64,3... | collective-permute-start | bytes 147464 | tf_op jit(solution)/shard_map/ppermute | solution.py:289
  46.7 1.4 collective-permute-done.3
  48.3 3.6 %collective-permute-start.6 = (bf16[2,2,64,384]{3,2,1,0:T(8,128)(2,1)S(1)}, bf16[2,2,64,384]{3,2,1,0:T(8,128)(2,1)S(1)}, u32[]{:S(2)}, u32[]{:S(2)}) collective-permute-start(bf16[2,2,64,384]{3,2,1,0:T(8,128)(2,1)S(1)} %pad_maximum_fusion.1), channel_id=1, source_target_pairs={{0,64},{64,0},{128,192},{192,128},{256,320},{320,256},{384,448},{4... | collective-permute-start | bytes 589832 | tf_op jit(solution)/shard_map/ppermute | solution.py:299
  51.9 3.7 %collective-permute-done.6 = bf16[2,2,64,384]{3,2,1,0:T(8,128)(2,1)S(1)} collective-permute-done((bf16[2,2,64,384]{3,2,1,0:T(8,128)(2,1)S(1)}, bf16[2,2,64,384]{3,2,1,0:T(8,128)(2,1)S(1)}, u32[]{:S(2)}, u32[]{:S(2)}) %collective-permute-start.6) | collective-permute-done | bytes 196640 | tf_op jit(solution)/shard_map/ppermute | solution.py:299
  55.7 0.8 pad_maximum_fusion
  57.2 3.5 %collective-permute-start.7 = (bf16[2,128,1024]{2,1,0:T(8,128)(2,1)}, bf16[2,128,1024]{2,1,0:T(8,128)(2,1)S(1)}, u32[]{:S(2)}, u32[]{:S(2)}) collective-permute-start(bf16[2,128,1024]{2,1,0:T(8,128)(2,1)} %get-tuple-element.44), channel_id=1, source_target_pairs={{0,128},{64,192},{128,256},{192,320},{256,384},{320,448},{384,0},{... | collective-permute-start | bytes 1572872 | tf_op jit(solution)/shard_map/ppermute | solution.py:267
  60.7 2.7 %collective-permute-start.8 = (bf16[2,128,1024]{2,1,0:T(8,128)(2,1)}, bf16[2,128,1024]{2,1,0:T(8,128)(2,1)S(1)}, u32[]{:S(2)}, u32[]{:S(2)}) collective-permute-start(bf16[2,128,1024]{2,1,0:T(8,128)(2,1)} %get-tuple-element.45), channel_id=1, source_target_pairs={{0,384},{64,448},{128,0},{192,64},{256,128},{320,192},{384,256},{4... | collective-permute-start | bytes 1572872 | tf_op jit(solution)/shard_map/ppermute | solution.py:267
  63.6 0.7 slice_dynamic-update-slice_fusion
  64.3 3.8 %collective-permute-start.12 = (bf16[3,128,1024]{2,1,0:T(8,128)(2,1)}, bf16[3,128,1024]{2,1,0:T(8,128)(2,1)}, u32[]{:S(2)}, u32[]{:S(2)}) collective-permute-start(bf16[3,128,1024]{2,1,0:T(8,128)(2,1)} %slice_dynamic-update-slice_fusion), channel_id=1, source_target_pairs={{0,320},{64,384},{128,448},{192,0},{256,64},{320,128},{384,192},{4... | collective-permute-start | bytes 2359304 | tf_op jit(solution)/shard_map/ppermute | solution.py:267
  68.2 4.5 %collective-permute-start.11 = (bf16[3,128,1024]{2,1,0:T(8,128)(2,1)S(1)}, bf16[3,128,1024]{2,1,0:T(8,128)(2,1)}, u32[]{:S(2)}, u32[]{:S(2)}) collective-permute-start(bf16[3,128,1024]{2,1,0:T(8,128)(2,1)S(1)} %slice_dynamic-update-slice_fusion.1), channel_id=1, source_target_pairs={{0,192},{64,256},{128,320},{192,384},{256,448},{320,0},{384,64},{4... | collective-permute-start | bytes 2359304 | tf_op jit(solution)/shard_map/ppermute | solution.py:267
  72.7 4.2 %collective-permute-done.7.two_up = bf16[2,128,1024]{2,1,0:T(8,128)(2,1)S(1)} collective-permute-done((bf16[2,128,1024]{2,1,0:T(8,128)(2,1)}, bf16[2,128,1024]{2,1,0:T(8,128)(2,1)S(1)}, u32[]{:S(2)}, u32[]{:S(2)}) %collective-permute-start.7) | collective-permute-done | bytes 524320 | tf_op jit(solution)/shard_map/ppermute | solution.py:267
  76.9 28.6 %all-gather.5.cloned.1.call-done = bf16[4096,384]{1,0:T(8,128)(2,1)} async-done(((bf16[512,384]{1,0:T(8,128)(2,1)}), bf16[4096,384]{1,0:T(8,128)(2,1)}) %all-gather.5.cloned.1.call-update) | async-done | bytes 3145744 | tf_op jit(solution)/shard_map/all_gather | solution.py:306
  105.5 6.2 %convolution_convert_fusion = bf16[512,384]{1,0:T(8,128)(2,1)} fusion(bf16[512,4096]{1,0:T(8,128)(2,1)} %all-gather.3.cloned.1.call-done, bf16[4096,384]{1,0:T(8,128)(2,1)} %all-gather.5.cloned.1.call-done), kind=kOutput, calls=%fused_computation | convolution fusion | flops 1610809344 | bytes 7733248 | tf_op jit(solution)/shard_map/dot_general | solution.py:310
  111.8 5.0 %all-to-all-start = ((bf16[8,64,384]{2,1,0:T(8,128)(2,1)}), bf16[8,64,384]{2,1,0:T(8,128)(2,1)S(1)}, u32[]{:S(2)}, u32[]{:S(2)}) async-start(bf16[8,64,384]{2,1,0:T(8,128)(2,1)} %bitcast.11), calls=%async_computation | async-start | bytes 786432 | tf_op jit(solution)/shard_map/all_to_all | solution.py:312
  117.0 7.9 %all-to-all-done.proj = bf16[8,64,384]{2,1,0:T(8,128)(2,1)S(1)} async-done(((bf16[8,64,384]{2,1,0:T(8,128)(2,1)}), bf16[8,64,384]{2,1,0:T(8,128)(2,1)S(1)}, u32[]{:S(2)}, u32[]{:S(2)}) %all-to-all-start) | async-done | bytes 393248 | tf_op jit(solution)/shard_map/all_to_all | solution.py:312
  125.2 4.7 %collective-permute-start.10 = (bf16[64,2176]{1,0:T(8,128)(2,1)S(1)}, bf16[64,2176]{1,0:T(8,128)(2,1)S(1)}, u32[]{:S(2)}, u32[]{:S(2)}) collective-permute-start(bf16[64,2176]{1,0:T(8,128)(2,1)S(1)} %get-tuple-element.48.q0), channel_id=1, source_target_pairs={{2,0},{3,1},{4,2},{5,3},{6,4},{7,5},{8,6},{9,7},{10,8},{11,9},{12,... | collective-permute-start | bytes 835592 | tf_op jit(solution)/shard_map/ppermute | solution.py:337
  129.9 3.0 %collective-permute-start.9 = (bf16[64,2176]{1,0:T(8,128)(2,1)S(1)}, bf16[64,2176]{1,0:T(8,128)(2,1)S(1)}, u32[]{:S(2)}, u32[]{:S(2)}) collective-permute-start(bf16[64,2176]{1,0:T(8,128)(2,1)S(1)} %get-tuple-element.48.q0), channel_id=1, source_target_pairs={{1,0},{2,1},{3,2},{4,3},{5,4},{6,5},{7,6},{8,7},{9,8},{10,9},{11,1... | collective-permute-start | bytes 835592 | tf_op jit(solution)/shard_map/ppermute | solution.py:337
  133.2 5.2 %collective-permute-done.12.three_down = bf16[3,128,1024]{2,1,0:T(8,128)(2,1)} collective-permute-done((bf16[3,128,1024]{2,1,0:T(8,128)(2,1)}, bf16[3,128,1024]{2,1,0:T(8,128)(2,1)}, u32[]{:S(2)}, u32[]{:S(2)}) %collective-permute-start.12) | collective-permute-done | bytes 786464 | tf_op jit(solution)/shard_map/ppermute | solution.py:267
  138.8 6.5 %shard_map.88 = (bf16[1024,1024]{1,0:T(8,128)(2,1)}, bf16[64,2176]{1,0:T(8,128)(2,1)S(1)}, bf16[64,2176]{1,0:T(8,128)(2,1)S(1)}) custom-call(s32[8,8]{1,0:T(8,128)S(1)} %copy-done.3, s32[1]{0:T(128)} %bitcast.me, f32[8,128]{1,0:T(8,128)S(1)} %get-tuple-element.80.kcos, f32[8,128]{1,0:T(8,128)S(1)} %get-tuple-element.81.ksin, ...), custom_call_target="tpu_custom_call" | custom-call | flops 1073741824 | bytes 4194304 | tf_op jit(solution)/shard_map/pallas_call | solution.py:341
  145.3 10.1 %collective-permute-start.13 = (bf16[64,2176]{1,0:T(8,128)(2,1)S(1)}, bf16[64,2176]{1,0:T(8,128)(2,1)S(1)}, u32[]{:S(2)}, u32[]{:S(2)}) collective-permute-start(bf16[64,2176]{1,0:T(8,128)(2,1)S(1)} %get-tuple-element.59), channel_id=1, source_target_pairs={{0,1},{1,2},{2,3},{3,4},{4,5},{5,6},{6,7},{7,8},{8,9},{9,10},{10,1... | collective-permute-start | bytes 835592 | tf_op jit(solution)/shard_map/ppermute | solution.py:337
  155.5 1.9 %collective-permute-start.14 = (bf16[64,2176]{1,0:T(8,128)(2,1)S(1)}, bf16[64,2176]{1,0:T(8,128)(2,1)S(1)}, u32[]{:S(2)}, u32[]{:S(2)}) collective-permute-start(bf16[64,2176]{1,0:T(8,128)(2,1)S(1)} %get-tuple-element.60), channel_id=1, source_target_pairs={{0,2},{1,3},{2,4},{3,5},{4,6},{5,7},{6,8},{7,9},{8,10},{9,11},{10,... | collective-permute-start | bytes 835592 | tf_op jit(solution)/shard_map/ppermute | solution.py:337
  157.5 1.6 copy-done.1
  159.1 1.8 %shard_map.89 = (f32[64,2048]{1,0:T(8,128)S(1)}, f32[64,128]{1,0:T(8,128)S(1)}) custom-call(bf16[64,2176]{1,0:T(8,128)(2,1)S(1)} %get-tuple-element.48.q0, bf16[1024,1024]{1,0:T(8,128)(2,1)S(1)} %copy-done.1), custom_call_target="tpu_custom_call" | custom-call | flops 536870912 | bytes 2097152 | tf_op jit(solution)/shard_map/pallas_call | solution.py:360
  160.9 5.2 %collective-permute-done.14.r2 = bf16[64,2176]{1,0:T(8,128)(2,1)S(1)} collective-permute-done((bf16[64,2176]{1,0:T(8,128)(2,1)S(1)}, bf16[64,2176]{1,0:T(8,128)(2,1)S(1)}, u32[]{:S(2)}, u32[]{:S(2)}) %collective-permute-start.14) | collective-permute-done | bytes 278560 | tf_op jit(solution)/shard_map/ppermute | solution.py:337
  166.1 1.0 shard_map.90
  (64 shorter events, 3.8 us)
Async XLA Ops:
  7.2 49.6 %copy-start = (s32[8,32]{1,0:T(8,128)S(1)}, s32[8,32]{1,0:T(8,128)}, u32[]{:S(2)}) copy-start(s32[8,32]{1,0:T(8,128)} %param.11) | copy-start | bytes 3076
  7.2 49.5 %copy-start.8 = (s32[1,8,8]{2,1,0:T(8,128)S(1)}, s32[1,8,8]{2,1,0:T(8,128)}, u32[]{:S(2)}) copy-start(s32[1,8,8]{2,1,0:T(8,128)} %param.12) | copy-start | bytes 772
  7.2 49.7 %copy-start.9 = (s32[1,8]{1,0:T(1,128)S(1)}, s32[1,8]{1,0:T(1,128)}, u32[]{:S(2)}) copy-start(s32[1,8]{1,0:T(1,128)} %param.13) | copy-start | bytes 100
  7.2 49.3 %all-gather.3.cloned.1.call-start = ((), (), s32[]{:S(2)}) async-start(), calls=%async_computation.1 | async-start | bytes 4718592 | tf_op jit(solution)/shard_map/all_gather | solution.py:304
  7.9 97.6 %all-gather.5.cloned.1.call-start = ((), (), s32[]{:S(2)}) async-start(), calls=%async_computation.2 | async-start | bytes 3538944 | tf_op jit(solution)/shard_map/all_gather | solution.py:306
  8.0 0.7 copy-start.2
  12.1 56.1 %copy-start.10 = (bf16[3,128,1024]{2,1,0:T(8,128)(2,1)S(1)}, bf16[3,128,1024]{2,1,0:T(8,128)(2,1)}, u32[]{:S(2)}) copy-start(bf16[3,128,1024]{2,1,0:T(8,128)(2,1)} %get-tuple-element.54) | copy-start | bytes 2359300
  12.1 36.1 %collective-permute-start.4 = (bf16[3,128,1024]{2,1,0:T(8,128)(2,1)}, bf16[3,128,1024]{2,1,0:T(8,128)(2,1)S(1)}, u32[]{:S(2)}, u32[]{:S(2)}) collective-permute-start(bf16[3,128,1024]{2,1,0:T(8,128)(2,1)} %get-tuple-element.34), channel_id=1, source_target_pairs={{0,64},{64,128},{128,192},{192,256},{256,320},{320,384},{384,448},... | collective-permute-start | bytes 2359304 | tf_op jit(solution)/shard_map/ppermute | solution.py:267
  16.6 31.6 %collective-permute-start.5 = (bf16[3,128,1024]{2,1,0:T(8,128)(2,1)}, bf16[3,128,1024]{2,1,0:T(8,128)(2,1)S(1)}, u32[]{:S(2)}, u32[]{:S(2)}) collective-permute-start(bf16[3,128,1024]{2,1,0:T(8,128)(2,1)} %get-tuple-element.35), channel_id=1, source_target_pairs={{0,448},{64,0},{128,64},{192,128},{256,192},{320,256},{384,320},{4... | collective-permute-start | bytes 2359304 | tf_op jit(solution)/shard_map/ppermute | solution.py:267
  18.5 17.3 %collective-permute-start = (bf16[64,384]{1,0:T(8,128)(2,1)}, bf16[64,384]{1,0:T(8,128)(2,1)S(1)}, u32[]{:S(2)}, u32[]{:S(2)}) collective-permute-start(bf16[64,384]{1,0:T(8,128)(2,1)} %param.8), channel_id=1, source_target_pairs={{0,0},{1,64},{2,128},{3,192},{4,256},{5,320},{6,384},{7,448},{64,1... | collective-permute-start | bytes 147464 | tf_op jit(solution)/shard_map/ppermute | solution.py:289
  20.5 26.2 %collective-permute-start.1 = (bf16[64,384]{1,0:T(8,128)(2,1)}, bf16[64,384]{1,0:T(8,128)(2,1)S(1)}, u32[]{:S(2)}, u32[]{:S(2)}) collective-permute-start(bf16[64,384]{1,0:T(8,128)(2,1)} %param.8), channel_id=1, source_target_pairs={{0,256},{1,320},{2,384},{3,448},{4,0},{5,64},{6,128},{7,192},{64,2... | collective-permute-start | bytes 147464 | tf_op jit(solution)/shard_map/ppermute | solution.py:289
  27.8 18.9 %collective-permute-start.2 = (bf16[64,384]{1,0:T(8,128)(2,1)}, bf16[64,384]{1,0:T(8,128)(2,1)S(1)}, u32[]{:S(2)}, u32[]{:S(2)}) collective-permute-start(bf16[64,384]{1,0:T(8,128)(2,1)} %param.8), channel_id=1, source_target_pairs={{0,128},{1,192},{2,0},{3,64},{4,384},{5,448},{6,256},{7,320},{64,1... | collective-permute-start | bytes 147464 | tf_op jit(solution)/shard_map/ppermute | solution.py:289
  35.9 12.3 %collective-permute-start.3 = (bf16[64,384]{1,0:T(8,128)(2,1)}, bf16[64,384]{1,0:T(8,128)(2,1)S(1)}, u32[]{:S(2)}, u32[]{:S(2)}) collective-permute-start(bf16[64,384]{1,0:T(8,128)(2,1)} %param.8), channel_id=1, source_target_pairs={{0,384},{1,448},{2,256},{3,320},{4,128},{5,192},{6,0},{7,64},{64,3... | collective-permute-start | bytes 147464 | tf_op jit(solution)/shard_map/ppermute | solution.py:289
  48.3 63.5 %copy-start.4 = (bf16[3,128,1024]{2,1,0:T(8,128)(2,1)}, bf16[3,128,1024]{2,1,0:T(8,128)(2,1)S(1)}, u32[]{:S(2)}) copy-start(bf16[3,128,1024]{2,1,0:T(8,128)(2,1)S(1)} %collective-permute-done.4.one_up) | copy-start | bytes 2359300
  48.3 63.5 %copy-start.5 = (bf16[3,128,1024]{2,1,0:T(8,128)(2,1)}, bf16[3,128,1024]{2,1,0:T(8,128)(2,1)S(1)}, u32[]{:S(2)}) copy-start(bf16[3,128,1024]{2,1,0:T(8,128)(2,1)S(1)} %collective-permute-done.5.one_down) | copy-start | bytes 2359300
  48.3 7.3 %collective-permute-start.6 = (bf16[2,2,64,384]{3,2,1,0:T(8,128)(2,1)S(1)}, bf16[2,2,64,384]{3,2,1,0:T(8,128)(2,1)S(1)}, u32[]{:S(2)}, u32[]{:S(2)}) collective-permute-start(bf16[2,2,64,384]{3,2,1,0:T(8,128)(2,1)S(1)} %pad_maximum_fusion.1), channel_id=1, source_target_pairs={{0,64},{64,0},{128,192},{192,128},{256,320},{320,256},{384,448},{4... | collective-permute-start | bytes 589832 | tf_op jit(solution)/shard_map/ppermute | solution.py:299
  57.2 19.7 %collective-permute-start.7 = (bf16[2,128,1024]{2,1,0:T(8,128)(2,1)}, bf16[2,128,1024]{2,1,0:T(8,128)(2,1)S(1)}, u32[]{:S(2)}, u32[]{:S(2)}) collective-permute-start(bf16[2,128,1024]{2,1,0:T(8,128)(2,1)} %get-tuple-element.44), channel_id=1, source_target_pairs={{0,128},{64,192},{128,256},{192,320},{256,384},{320,448},{384,0},{... | collective-permute-start | bytes 1572872 | tf_op jit(solution)/shard_map/ppermute | solution.py:267
  60.7 16.2 %collective-permute-start.8 = (bf16[2,128,1024]{2,1,0:T(8,128)(2,1)}, bf16[2,128,1024]{2,1,0:T(8,128)(2,1)S(1)}, u32[]{:S(2)}, u32[]{:S(2)}) collective-permute-start(bf16[2,128,1024]{2,1,0:T(8,128)(2,1)} %get-tuple-element.45), channel_id=1, source_target_pairs={{0,384},{64,448},{128,0},{192,64},{256,128},{320,192},{384,256},{4... | collective-permute-start | bytes 1572872 | tf_op jit(solution)/shard_map/ppermute | solution.py:267
  64.3 74.0 %collective-permute-start.12 = (bf16[3,128,1024]{2,1,0:T(8,128)(2,1)}, bf16[3,128,1024]{2,1,0:T(8,128)(2,1)}, u32[]{:S(2)}, u32[]{:S(2)}) collective-permute-start(bf16[3,128,1024]{2,1,0:T(8,128)(2,1)} %slice_dynamic-update-slice_fusion), channel_id=1, source_target_pairs={{0,320},{64,384},{128,448},{192,0},{256,64},{320,128},{384,192},{4... | collective-permute-start | bytes 2359304 | tf_op jit(solution)/shard_map/ppermute | solution.py:267
  68.2 70.7 %copy-start.3 = (s32[8,8]{1,0:T(8,128)S(1)}, s32[8,8]{1,0:T(8,128)}, u32[]{:S(2)}) copy-start(s32[8,8]{1,0:T(8,128)} %owner.3) | copy-start | bytes 772
  68.2 70.2 %collective-permute-start.11 = (bf16[3,128,1024]{2,1,0:T(8,128)(2,1)S(1)}, bf16[3,128,1024]{2,1,0:T(8,128)(2,1)}, u32[]{:S(2)}, u32[]{:S(2)}) collective-permute-start(bf16[3,128,1024]{2,1,0:T(8,128)(2,1)S(1)} %slice_dynamic-update-slice_fusion.1), channel_id=1, source_target_pairs={{0,192},{64,256},{128,320},{192,384},{256,448},{320,0},{384,64},{4... | collective-permute-start | bytes 2359304 | tf_op jit(solution)/shard_map/ppermute | solution.py:267
  76.9 34.9 %copy-start.6 = (bf16[2,128,1024]{2,1,0:T(8,128)(2,1)}, bf16[2,128,1024]{2,1,0:T(8,128)(2,1)S(1)}, u32[]{:S(2)}) copy-start(bf16[2,128,1024]{2,1,0:T(8,128)(2,1)S(1)} %collective-permute-done.7.two_up) | copy-start | bytes 1572868
  76.9 34.9 %copy-start.7 = (bf16[2,128,1024]{2,1,0:T(8,128)(2,1)}, bf16[2,128,1024]{2,1,0:T(8,128)(2,1)S(1)}, u32[]{:S(2)}) copy-start(bf16[2,128,1024]{2,1,0:T(8,128)(2,1)S(1)} %collective-permute-done.8.two_down) | copy-start | bytes 1572868
  111.8 13.1 %all-to-all-start = ((bf16[8,64,384]{2,1,0:T(8,128)(2,1)}), bf16[8,64,384]{2,1,0:T(8,128)(2,1)S(1)}, u32[]{:S(2)}, u32[]{:S(2)}) async-start(bf16[8,64,384]{2,1,0:T(8,128)(2,1)} %bitcast.11), calls=%async_computation | async-start | bytes 786432 | tf_op jit(solution)/shard_map/all_to_all | solution.py:312
  125.2 13.2 %collective-permute-start.10 = (bf16[64,2176]{1,0:T(8,128)(2,1)S(1)}, bf16[64,2176]{1,0:T(8,128)(2,1)S(1)}, u32[]{:S(2)}, u32[]{:S(2)}) collective-permute-start(bf16[64,2176]{1,0:T(8,128)(2,1)S(1)} %get-tuple-element.48.q0), channel_id=1, source_target_pairs={{2,0},{3,1},{4,2},{5,3},{6,4},{7,5},{8,6},{9,7},{10,8},{11,9},{12,... | collective-permute-start | bytes 835592 | tf_op jit(solution)/shard_map/ppermute | solution.py:337
  129.9 8.9 %collective-permute-start.9 = (bf16[64,2176]{1,0:T(8,128)(2,1)S(1)}, bf16[64,2176]{1,0:T(8,128)(2,1)S(1)}, u32[]{:S(2)}, u32[]{:S(2)}) collective-permute-start(bf16[64,2176]{1,0:T(8,128)(2,1)S(1)} %get-tuple-element.48.q0), channel_id=1, source_target_pairs={{1,0},{2,1},{3,2},{4,3},{5,4},{6,5},{7,6},{8,7},{9,8},{10,9},{11,1... | collective-permute-start | bytes 835592 | tf_op jit(solution)/shard_map/ppermute | solution.py:337
  145.3 15.6 %collective-permute-start.13 = (bf16[64,2176]{1,0:T(8,128)(2,1)S(1)}, bf16[64,2176]{1,0:T(8,128)(2,1)S(1)}, u32[]{:S(2)}, u32[]{:S(2)}) collective-permute-start(bf16[64,2176]{1,0:T(8,128)(2,1)S(1)} %get-tuple-element.59), channel_id=1, source_target_pairs={{0,1},{1,2},{2,3},{3,4},{4,5},{5,6},{6,7},{7,8},{8,9},{9,10},{10,1... | collective-permute-start | bytes 835592 | tf_op jit(solution)/shard_map/ppermute | solution.py:337
  155.5 10.6 %collective-permute-start.14 = (bf16[64,2176]{1,0:T(8,128)(2,1)S(1)}, bf16[64,2176]{1,0:T(8,128)(2,1)S(1)}, u32[]{:S(2)}, u32[]{:S(2)}) collective-permute-start(bf16[64,2176]{1,0:T(8,128)(2,1)S(1)} %get-tuple-element.60), channel_id=1, source_target_pairs={{0,2},{1,3},{2,4},{3,5},{4,6},{5,7},{6,8},{7,9},{8,10},{9,11},{10,... | collective-permute-start | bytes 835592 | tf_op jit(solution)/shard_map/ppermute | solution.py:337
  157.5 1.6 copy-start.1
Sparse Core Ops, SparseCore 0:
  10.2 41.4 all-gather.2
  56.6 48.8 all-gather.4

commit v8 on v4

--- a/solution.py
+++ b/solution.py
@@ -304,15 +304,13 @@
     w, two_up, two_down, one_up, one_down = lax.optimization_barrier(
         (w, two_up, two_down, one_up, one_down)
     )
+    two_up, two_down = turned(two_up, 2), turned(two_down, -2)
     hidden = lax.all_gather(sel_hidden.reshape(rows, d), XC, axis=0, tiled=True)
     w, hidden = lax.optimization_barrier((w, hidden))
     w = lax.all_gather(w, "z", axis=0, tiled=True)
-    two_up, two_down = turned(two_up, 2), turned(two_down, -2)
-    two_up, two_down, three_up, three_down = lax.optimization_barrier(
-        (two_up, two_down, three_up, three_down)
-    )
     three_up = turned(lax.dynamic_update_slice(three_up, one_up[2:], (2, 0, 0)), 3)
     three_down = turned(lax.dynamic_update_slice(three_down, one_down[2:], (2, 0, 0)), -3)
+    hidden, w, two_up, two_down = lax.optimization_barrier((hidden, w, two_up, two_down))
     projected = jnp.dot(hidden, w, preferred_element_type=F32).astype(BF)
     projected = projected.reshape(group, rows, cols)
     merged = lax.all_to_all(projected, XC, 0, 0, tiled=True)

time: 186 us -> 175 us (0.941)
  the two profiles are of different devices: /device:TPU:257 before, /device:TPU:281 now
where the time goes in v8:
time: 175 us; the launch traced here: 174 us
  starting transfers between devices  71.8 us (41%)
  waiting for transfers between devices  63.4 us (36%)
  between operations  14.5 us (8%)
  Pallas kernels  13.9 us (8%)
  matrix products  6.24 us (4%)
  local copies, waits for them, and re-layouts  2.81 us (2%)
  other arithmetic  1.8 us (1%)
    all_gather x1, waiting for transfers between devices, on_device(): w = lax.all_gather(w, 'z', axis=0, tiled=True)  29.4 us
    ppermute x4, starting transfers between devices, crossed(): return lax.ppermute(w_qkv, ('y', 'x', 'c'), pairs)  23.6 us
    ppermute x6, starting transfers between devices, turned(): return lax.ppermute(array, 'y', [(i, (i + by) % ny) for i in range(ny)])  21.1 us
    ppermute x4, starting transfers between devices, along(): return lax.ppermute(array, SEQ, pairs)  17.8 us
    ppermute x6, waiting for transfers between devices, turned(): return lax.ppermute(array, 'y', [(i, (i + by) % ny) for i in range(ny)])  8.94 us
    all_to_all x1, waiting for transfers between devices, on_device(): merged = lax.all_to_all(projected, XC, 0, 0, tiled=True)  7.9 us
    ppermute x4, waiting for transfers between devices, along(): return lax.ppermute(array, SEQ, pairs)  6.76 us
    dot_general x1, matrix products, on_device(): projected = jnp.dot(hidden, w, preferred_element_type=F32).astype(BF)  6.24 us
  transfers between devices with their start and end apart: 18, of which 8 were waited for; matrix products, arithmetic and copies ran while one was open for 6% of the time, Pallas kernels for 6%

profile of v8, /device:TPU:281, one launch (start us, length us, event | category | flops | bytes accessed | tf_op | source)
XLA Modules:
  0.0 174.4 jit_solution(3683828143803734946)
XLA Ops:
  8.7 3.5 %shard_map.86 = (bf16[3,128,1024]{2,1,0:T(8,128)(2,1)}, bf16[3,128,1024]{2,1,0:T(8,128)(2,1)}, bf16[2,128,1024]{2,1,0:T(8,128)(2,1)}, bf16[2,128,1024]{2,1,0:T(8...) custom-call(s32[8,8]{1,0:T(8,128)S(1)} %copy-done.2, s32[1]{0:T(128)} %bitcast.me, ...), custom_call_target="tpu_custom_call" | custom-call | bytes 4194304 | tf_op jit(solution)/shard_map/pallas_call | solution.py:276
  12.2 4.5 %collective-permute-start.4 = (bf16[3,128,1024]{2,1,0:T(8,128)(2,1)}, bf16[3,128,1024]{2,1,0:T(8,128)(2,1)S(1)}, u32[]{:S(2)}, u32[]{:S(2)}) collective-permute-start(bf16[3,128,1024]{2,1,0:T(8,128)(2,1)} %get-tuple-element.37), channel_id=1, source_target_pairs={{0,64},{64,128},{128,192},{192,256},{256,320},{320,384},{384,448},... | collective-permute-start | bytes 2359304 | tf_op jit(solution)/shard_map/ppermute | solution.py:271
  16.8 1.9 %collective-permute-start.5 = (bf16[3,128,1024]{2,1,0:T(8,128)(2,1)}, bf16[3,128,1024]{2,1,0:T(8,128)(2,1)S(1)}, u32[]{:S(2)}, u32[]{:S(2)}) collective-permute-start(bf16[3,128,1024]{2,1,0:T(8,128)(2,1)} %get-tuple-element.38), channel_id=1, source_target_pairs={{0,448},{64,0},{128,64},{192,128},{256,192},{320,256},{384,320},{4... | collective-permute-start | bytes 2359304 | tf_op jit(solution)/shard_map/ppermute | solution.py:271
  18.7 1.9 %collective-permute-start = (bf16[64,384]{1,0:T(8,128)(2,1)}, bf16[64,384]{1,0:T(8,128)(2,1)S(1)}, u32[]{:S(2)}, u32[]{:S(2)}) collective-permute-start(bf16[64,384]{1,0:T(8,128)(2,1)} %param.8), channel_id=1, source_target_pairs={{0,0},{1,64},{2,128},{3,192},{4,256},{5,320},{6,384},{7,448},{64,1... | collective-permute-start | bytes 147464 | tf_op jit(solution)/shard_map/ppermute | solution.py:293
  20.7 7.3 %collective-permute-start.1 = (bf16[64,384]{1,0:T(8,128)(2,1)}, bf16[64,384]{1,0:T(8,128)(2,1)S(1)}, u32[]{:S(2)}, u32[]{:S(2)}) collective-permute-start(bf16[64,384]{1,0:T(8,128)(2,1)} %param.8), channel_id=1, source_target_pairs={{0,256},{1,320},{2,384},{3,448},{4,0},{5,64},{6,128},{7,192},{64,2... | collective-permute-start | bytes 147464 | tf_op jit(solution)/shard_map/ppermute | solution.py:293
  28.0 4.5 %collective-permute-start.2 = (bf16[64,384]{1,0:T(8,128)(2,1)}, bf16[64,384]{1,0:T(8,128)(2,1)S(1)}, u32[]{:S(2)}, u32[]{:S(2)}) collective-permute-start(bf16[64,384]{1,0:T(8,128)(2,1)} %param.8), channel_id=1, source_target_pairs={{0,128},{1,192},{2,0},{3,64},{4,384},{5,448},{6,256},{7,320},{64,1... | collective-permute-start | bytes 147464 | tf_op jit(solution)/shard_map/ppermute | solution.py:293
  32.6 3.9 %collective-permute-done = bf16[64,384]{1,0:T(8,128)(2,1)S(1)} collective-permute-done((bf16[64,384]{1,0:T(8,128)(2,1)}, bf16[64,384]{1,0:T(8,128)(2,1)S(1)}, u32[]{:S(2)}, u32[]{:S(2)}) %collective-permute-start) | collective-permute-done | bytes 49184 | tf_op jit(solution)/shard_map/ppermute | solution.py:293
  36.5 9.9 %collective-permute-start.3 = (bf16[64,384]{1,0:T(8,128)(2,1)}, bf16[64,384]{1,0:T(8,128)(2,1)S(1)}, u32[]{:S(2)}, u32[]{:S(2)}) collective-permute-start(bf16[64,384]{1,0:T(8,128)(2,1)} %param.8), channel_id=1, source_target_pairs={{0,384},{1,448},{2,256},{3,320},{4,128},{5,192},{6,0},{7,64},{64,3... | collective-permute-start | bytes 147464 | tf_op jit(solution)/shard_map/ppermute | solution.py:293
  46.4 1.4 collective-permute-done.3
  48.0 4.3 %collective-permute-start.6 = (bf16[2,2,64,384]{3,2,1,0:T(8,128)(2,1)S(1)}, bf16[2,2,64,384]{3,2,1,0:T(8,128)(2,1)S(1)}, u32[]{:S(2)}, u32[]{:S(2)}) collective-permute-start(bf16[2,2,64,384]{3,2,1,0:T(8,128)(2,1)S(1)} %pad_maximum_fusion.1), channel_id=1, source_target_pairs={{0,64},{64,0},{128,192},{192,128},{256,320},{320,256},{384,448},{4... | collective-permute-start | bytes 589832 | tf_op jit(solution)/shard_map/ppermute | solution.py:303
  52.2 4.3 %collective-permute-done.6 = bf16[2,2,64,384]{3,2,1,0:T(8,128)(2,1)S(1)} collective-permute-done((bf16[2,2,64,384]{3,2,1,0:T(8,128)(2,1)S(1)}, bf16[2,2,64,384]{3,2,1,0:T(8,128)(2,1)S(1)}, u32[]{:S(2)}, u32[]{:S(2)}) %collective-permute-start.6) | collective-permute-done | bytes 196640 | tf_op jit(solution)/shard_map/ppermute | solution.py:303
  56.6 0.8 pad_maximum_fusion
  58.1 3.0 %collective-permute-start.7 = (bf16[2,128,1024]{2,1,0:T(8,128)(2,1)}, bf16[2,128,1024]{2,1,0:T(8,128)(2,1)S(1)}, u32[]{:S(2)}, u32[]{:S(2)}) collective-permute-start(bf16[2,128,1024]{2,1,0:T(8,128)(2,1)} %get-tuple-element.47), channel_id=1, source_target_pairs={{0,128},{64,192},{128,256},{192,320},{256,384},{320,448},{384,0},{... | collective-permute-start | bytes 1572872 | tf_op jit(solution)/shard_map/ppermute | solution.py:271
  61.1 3.2 %collective-permute-start.8 = (bf16[2,128,1024]{2,1,0:T(8,128)(2,1)S(1)}, bf16[2,128,1024]{2,1,0:T(8,128)(2,1)S(1)}, u32[]{:S(2)}, u32[]{:S(2)}) collective-permute-start(bf16[2,128,1024]{2,1,0:T(8,128)(2,1)S(1)} %copy-done.10), channel_id=1, source_target_pairs={{0,384},{64,448},{128,0},{192,64},{256,128},{320,192},{384,256},{4... | collective-permute-start | bytes 1572872 | tf_op jit(solution)/shard_map/ppermute | solution.py:271
  64.5 0.7 slice_dynamic-update-slice_fusion
  65.3 3.8 %collective-permute-start.10 = (bf16[3,128,1024]{2,1,0:T(8,128)(2,1)}, bf16[3,128,1024]{2,1,0:T(8,128)(2,1)}, u32[]{:S(2)}, u32[]{:S(2)}) collective-permute-start(bf16[3,128,1024]{2,1,0:T(8,128)(2,1)} %slice_dynamic-update-slice_fusion), channel_id=1, source_target_pairs={{0,320},{64,384},{128,448},{192,0},{256,64},{320,128},{384,192},{4... | collective-permute-start | bytes 2359304 | tf_op jit(solution)/shard_map/ppermute | solution.py:271
  69.8 4.6 %collective-permute-start.9 = (bf16[3,128,1024]{2,1,0:T(8,128)(2,1)}, bf16[3,128,1024]{2,1,0:T(8,128)(2,1)}, u32[]{:S(2)}, u32[]{:S(2)}) collective-permute-start(bf16[3,128,1024]{2,1,0:T(8,128)(2,1)} %slice_dynamic-update-slice_fusion.1), channel_id=1, source_target_pairs={{0,192},{64,256},{128,320},{192,384},{256,448},{320,0},{384,64},{4... | collective-permute-start | bytes 2359304 | tf_op jit(solution)/shard_map/ppermute | solution.py:271
  74.4 1.7 collective-permute-done.7.two_up
  76.1 29.4 %all-gather.5.cloned.1.call-done = bf16[4096,384]{1,0:T(8,128)(2,1)} async-done(((bf16[512,384]{1,0:T(8,128)(2,1)}), bf16[4096,384]{1,0:T(8,128)(2,1)}) %all-gather.5.cloned.1.call-update) | async-done | bytes 3145744 | tf_op jit(solution)/shard_map/all_gather | solution.py:310
  105.6 6.2 %convolution_convert_fusion = bf16[512,384]{1,0:T(8,128)(2,1)} fusion(bf16[512,4096]{1,0:T(8,128)(2,1)} %all-gather.3.cloned.1.call-done, bf16[4096,384]{1,0:T(8,128)(2,1)} %all-gather.5.cloned.1.call-done), kind=kOutput, calls=%fused_computation | convolution fusion | flops 1610809344 | bytes 7733248 | tf_op jit(solution)/shard_map/dot_general | solution.py:314
  111.8 5.0 %all-to-all-start = ((bf16[8,64,384]{2,1,0:T(8,128)(2,1)}), bf16[8,64,384]{2,1,0:T(8,128)(2,1)S(1)}, u32[]{:S(2)}, u32[]{:S(2)}) async-start(bf16[8,64,384]{2,1,0:T(8,128)(2,1)} %bitcast.11), calls=%async_computation | async-start | bytes 786432 | tf_op jit(solution)/shard_map/all_to_all | solution.py:316
  117.1 7.9 %all-to-all-done.proj = bf16[8,64,384]{2,1,0:T(8,128)(2,1)S(1)} async-done(((bf16[8,64,384]{2,1,0:T(8,128)(2,1)}), bf16[8,64,384]{2,1,0:T(8,128)(2,1)S(1)}, u32[]{:S(2)}, u32[]{:S(2)}) %all-to-all-start) | async-done | bytes 393248 | tf_op jit(solution)/shard_map/all_to_all | solution.py:316
  125.2 2.7 %collective-permute-start.11 = (bf16[64,2176]{1,0:T(8,128)(2,1)S(1)}, bf16[64,2176]{1,0:T(8,128)(2,1)S(1)}, u32[]{:S(2)}, u32[]{:S(2)}) collective-permute-start(bf16[64,2176]{1,0:T(8,128)(2,1)S(1)} %get-tuple-element.51.q0), channel_id=1, source_target_pairs={{1,0},{2,1},{3,2},{4,3},{5,4},{6,5},{7,6},{8,7},{9,8},{10,9},{11,1... | collective-permute-start | bytes 835592 | tf_op jit(solution)/shard_map/ppermute | solution.py:341
  127.9 4.7 %collective-permute-start.12 = (bf16[64,2176]{1,0:T(8,128)(2,1)S(1)}, bf16[64,2176]{1,0:T(8,128)(2,1)S(1)}, u32[]{:S(2)}, u32[]{:S(2)}) collective-permute-start(bf16[64,2176]{1,0:T(8,128)(2,1)S(1)} %get-tuple-element.51.q0), channel_id=1, source_target_pairs={{2,0},{3,1},{4,2},{5,3},{6,4},{7,5},{8,6},{9,7},{10,8},{11,9},{12,... | collective-permute-start | bytes 835592 | tf_op jit(solution)/shard_map/ppermute | solution.py:341
  132.9 7.2 %collective-permute-done.10.three_down = bf16[3,128,1024]{2,1,0:T(8,128)(2,1)} collective-permute-done((bf16[3,128,1024]{2,1,0:T(8,128)(2,1)}, bf16[3,128,1024]{2,1,0:T(8,128)(2,1)}, u32[]{:S(2)}, u32[]{:S(2)}) %collective-permute-start.10) | collective-permute-done | bytes 786464 | tf_op jit(solution)/shard_map/ppermute | solution.py:271
  140.2 4.3 %shard_map.88 = (bf16[1024,1024]{1,0:T(8,128)(2,1)}, bf16[1024,1024]{1,0:T(8,128)(2,1)S(1)}) custom-call(s32[8,8]{1,0:T(8,128)S(1)} %copy-done.3, s32[1]{0:T(128)} %bitcast.me, f32[8,128]{1,0:T(8,128)S(1)} %get-tuple-element.86.kcos, f32[8,128]{1,0:T(8,128)S(1)} %get-tuple-element.87.ksin, s32[1,64]{1,0:T(1,128)S(1)} %add_select_fusion.spots, ...), custom_call_target="tpu_custom_call" | custom-call | bytes 6291456 | tf_op jit(solution)/shard_map/pallas_call | solution.py:344
  144.5 3.0 %shard_map.89 = (bf16[64,2176]{1,0:T(8,128)(2,1)S(1)}, bf16[64,2176]{1,0:T(8,128)(2,1)S(1)}) custom-call(bf16[64,2176]{1,0:T(8,128)(2,1)S(1)} %collective-permute-done.11.q1, bf16[64,2176]{1,0:T(8,128)(2,1)S(1)} %collective-permute-done.12.q2, bf16[1024,1024]{1,0:T(8,128)(2,1)S(1)} %get-tuple-element.60.kv), custom_call_target="tpu_custom_call" | custom-call | flops 1073741824 | bytes 2097152 | tf_op jit(solution)/shard_map/pallas_call | solution.py:354
  147.5 8.5 %collective-permute-start.13 = (bf16[64,2176]{1,0:T(8,128)(2,1)S(1)}, bf16[64,2176]{1,0:T(8,128)(2,1)S(1)}, u32[]{:S(2)}, u32[]{:S(2)}) collective-permute-start(bf16[64,2176]{1,0:T(8,128)(2,1)S(1)} %get-tuple-element.66), channel_id=1, source_target_pairs={{0,1},{1,2},{2,3},{3,4},{4,5},{5,6},{6,7},{7,8},{8,9},{9,10},{10,1... | collective-permute-start | bytes 835592 | tf_op jit(solution)/shard_map/ppermute | solution.py:341
  155.9 1.9 %collective-permute-start.14 = (bf16[64,2176]{1,0:T(8,128)(2,1)S(1)}, bf16[64,2176]{1,0:T(8,128)(2,1)S(1)}, u32[]{:S(2)}, u32[]{:S(2)}) collective-permute-start(bf16[64,2176]{1,0:T(8,128)(2,1)S(1)} %get-tuple-element.67), channel_id=1, source_target_pairs={{0,2},{1,3},{2,4},{3,5},{4,6},{5,7},{6,8},{7,9},{8,10},{9,11},{10,... | collective-permute-start | bytes 835592 | tf_op jit(solution)/shard_map/ppermute | solution.py:341
  157.9 1.9 %shard_map.90 = (f32[64,2048]{1,0:T(8,128)S(1)}, f32[64,128]{1,0:T(8,128)S(1)}) custom-call(bf16[64,2176]{1,0:T(8,128)(2,1)S(1)} %get-tuple-element.51.q0, bf16[1024,1024]{1,0:T(8,128)(2,1)S(1)} %copy-done.1), custom_call_target="tpu_custom_call" | custom-call | flops 536870912 | bytes 2097152 | tf_op jit(solution)/shard_map/pallas_call | solution.py:365
  159.8 6.7 %collective-permute-done.14.r2 = bf16[64,2176]{1,0:T(8,128)(2,1)S(1)} collective-permute-done((bf16[64,2176]{1,0:T(8,128)(2,1)S(1)}, bf16[64,2176]{1,0:T(8,128)(2,1)S(1)}, u32[]{:S(2)}, u32[]{:S(2)}) %collective-permute-start.14) | collective-permute-done | bytes 278560 | tf_op jit(solution)/shard_map/ppermute | solution.py:341
  166.5 1.0 shard_map.91
  (65 shorter events, 4.1 us)
Async XLA Ops:
  7.2 50.6 %copy-start = (s32[8,32]{1,0:T(8,128)S(1)}, s32[8,32]{1,0:T(8,128)}, u32[]{:S(2)}) copy-start(s32[8,32]{1,0:T(8,128)} %param.11) | copy-start | bytes 3076
  7.2 50.4 %copy-start.8 = (s32[1,8,8]{2,1,0:T(8,128)S(1)}, s32[1,8,8]{2,1,0:T(8,128)}, u32[]{:S(2)}) copy-start(s32[1,8,8]{2,1,0:T(8,128)} %param.12) | copy-start | bytes 772
  7.2 50.7 %copy-start.9 = (s32[1,8]{1,0:T(1,128)S(1)}, s32[1,8]{1,0:T(1,128)}, u32[]{:S(2)}) copy-start(s32[1,8]{1,0:T(1,128)} %param.13) | copy-start | bytes 100
  7.2 50.2 %all-gather.3.cloned.1.call-start = ((), (), s32[]{:S(2)}) async-start(), calls=%async_computation.1 | async-start | bytes 4718592 | tf_op jit(solution)/shard_map/all_gather | solution.py:308
  7.9 97.6 %all-gather.5.cloned.1.call-start = ((), (), s32[]{:S(2)}) async-start(), calls=%async_computation.2 | async-start | bytes 3538944 | tf_op jit(solution)/shard_map/all_gather | solution.py:310
  8.0 0.7 copy-start.2
  12.2 48.9 %copy-start.10 = (bf16[2,128,1024]{2,1,0:T(8,128)(2,1)S(1)}, bf16[2,128,1024]{2,1,0:T(8,128)(2,1)}, u32[]{:S(2)}) copy-start(bf16[2,128,1024]{2,1,0:T(8,128)(2,1)} %get-tuple-element.48) | copy-start | bytes 1572868
  12.2 35.7 %collective-permute-start.4 = (bf16[3,128,1024]{2,1,0:T(8,128)(2,1)}, bf16[3,128,1024]{2,1,0:T(8,128)(2,1)S(1)}, u32[]{:S(2)}, u32[]{:S(2)}) collective-permute-start(bf16[3,128,1024]{2,1,0:T(8,128)(2,1)} %get-tuple-element.37), channel_id=1, source_target_pairs={{0,64},{64,128},{128,192},{192,256},{256,320},{320,384},{384,448},... | collective-permute-start | bytes 2359304 | tf_op jit(solution)/shard_map/ppermute | solution.py:271
  16.8 31.2 %collective-permute-start.5 = (bf16[3,128,1024]{2,1,0:T(8,128)(2,1)}, bf16[3,128,1024]{2,1,0:T(8,128)(2,1)S(1)}, u32[]{:S(2)}, u32[]{:S(2)}) collective-permute-start(bf16[3,128,1024]{2,1,0:T(8,128)(2,1)} %get-tuple-element.38), channel_id=1, source_target_pairs={{0,448},{64,0},{128,64},{192,128},{256,192},{320,256},{384,320},{4... | collective-permute-start | bytes 2359304 | tf_op jit(solution)/shard_map/ppermute | solution.py:271
  18.7 17.8 %collective-permute-start = (bf16[64,384]{1,0:T(8,128)(2,1)}, bf16[64,384]{1,0:T(8,128)(2,1)S(1)}, u32[]{:S(2)}, u32[]{:S(2)}) collective-permute-start(bf16[64,384]{1,0:T(8,128)(2,1)} %param.8), channel_id=1, source_target_pairs={{0,0},{1,64},{2,128},{3,192},{4,256},{5,320},{6,384},{7,448},{64,1... | collective-permute-start | bytes 147464 | tf_op jit(solution)/shard_map/ppermute | solution.py:293
  20.7 25.7 %collective-permute-start.1 = (bf16[64,384]{1,0:T(8,128)(2,1)}, bf16[64,384]{1,0:T(8,128)(2,1)S(1)}, u32[]{:S(2)}, u32[]{:S(2)}) collective-permute-start(bf16[64,384]{1,0:T(8,128)(2,1)} %param.8), channel_id=1, source_target_pairs={{0,256},{1,320},{2,384},{3,448},{4,0},{5,64},{6,128},{7,192},{64,2... | collective-permute-start | bytes 147464 | tf_op jit(solution)/shard_map/ppermute | solution.py:293
  28.0 18.4 %collective-permute-start.2 = (bf16[64,384]{1,0:T(8,128)(2,1)}, bf16[64,384]{1,0:T(8,128)(2,1)S(1)}, u32[]{:S(2)}, u32[]{:S(2)}) collective-permute-start(bf16[64,384]{1,0:T(8,128)(2,1)} %param.8), channel_id=1, source_target_pairs={{0,128},{1,192},{2,0},{3,64},{4,384},{5,448},{6,256},{7,320},{64,1... | collective-permute-start | bytes 147464 | tf_op jit(solution)/shard_map/ppermute | solution.py:293
  36.5 11.4 %collective-permute-start.3 = (bf16[64,384]{1,0:T(8,128)(2,1)}, bf16[64,384]{1,0:T(8,128)(2,1)S(1)}, u32[]{:S(2)}, u32[]{:S(2)}) collective-permute-start(bf16[64,384]{1,0:T(8,128)(2,1)} %param.8), channel_id=1, source_target_pairs={{0,384},{1,448},{2,256},{3,320},{4,128},{5,192},{6,0},{7,64},{64,3... | collective-permute-start | bytes 147464 | tf_op jit(solution)/shard_map/ppermute | solution.py:293
  47.9 63.9 %copy-start.4 = (bf16[3,128,1024]{2,1,0:T(8,128)(2,1)}, bf16[3,128,1024]{2,1,0:T(8,128)(2,1)S(1)}, u32[]{:S(2)}) copy-start(bf16[3,128,1024]{2,1,0:T(8,128)(2,1)S(1)} %collective-permute-done.4.one_up) | copy-start | bytes 2359300
  48.0 63.9 %copy-start.5 = (bf16[3,128,1024]{2,1,0:T(8,128)(2,1)}, bf16[3,128,1024]{2,1,0:T(8,128)(2,1)S(1)}, u32[]{:S(2)}) copy-start(bf16[3,128,1024]{2,1,0:T(8,128)(2,1)S(1)} %collective-permute-done.5.one_down) | copy-start | bytes 2359300
  48.0 8.6 %collective-permute-start.6 = (bf16[2,2,64,384]{3,2,1,0:T(8,128)(2,1)S(1)}, bf16[2,2,64,384]{3,2,1,0:T(8,128)(2,1)S(1)}, u32[]{:S(2)}, u32[]{:S(2)}) collective-permute-start(bf16[2,2,64,384]{3,2,1,0:T(8,128)(2,1)S(1)} %pad_maximum_fusion.1), channel_id=1, source_target_pairs={{0,64},{64,0},{128,192},{192,128},{256,320},{320,256},{384,448},{4... | collective-permute-start | bytes 589832 | tf_op jit(solution)/shard_map/ppermute | solution.py:303
  58.1 18.0 %collective-permute-start.7 = (bf16[2,128,1024]{2,1,0:T(8,128)(2,1)}, bf16[2,128,1024]{2,1,0:T(8,128)(2,1)S(1)}, u32[]{:S(2)}, u32[]{:S(2)}) collective-permute-start(bf16[2,128,1024]{2,1,0:T(8,128)(2,1)} %get-tuple-element.47), channel_id=1, source_target_pairs={{0,128},{64,192},{128,256},{192,320},{256,384},{320,448},{384,0},{... | collective-permute-start | bytes 1572872 | tf_op jit(solution)/shard_map/ppermute | solution.py:271
  61.1 15.0 %collective-permute-start.8 = (bf16[2,128,1024]{2,1,0:T(8,128)(2,1)S(1)}, bf16[2,128,1024]{2,1,0:T(8,128)(2,1)S(1)}, u32[]{:S(2)}, u32[]{:S(2)}) collective-permute-start(bf16[2,128,1024]{2,1,0:T(8,128)(2,1)S(1)} %copy-done.10), channel_id=1, source_target_pairs={{0,384},{64,448},{128,0},{192,64},{256,128},{320,192},{384,256},{4... | collective-permute-start | bytes 1572872 | tf_op jit(solution)/shard_map/ppermute | solution.py:271
  65.3 74.9 %collective-permute-start.10 = (bf16[3,128,1024]{2,1,0:T(8,128)(2,1)}, bf16[3,128,1024]{2,1,0:T(8,128)(2,1)}, u32[]{:S(2)}, u32[]{:S(2)}) collective-permute-start(bf16[3,128,1024]{2,1,0:T(8,128)(2,1)} %slice_dynamic-update-slice_fusion), channel_id=1, source_target_pairs={{0,320},{64,384},{128,448},{192,0},{256,64},{320,128},{384,192},{4... | collective-permute-start | bytes 2359304 | tf_op jit(solution)/shard_map/ppermute | solution.py:271
  69.8 70.3 %copy-start.3 = (s32[8,8]{1,0:T(8,128)S(1)}, s32[8,8]{1,0:T(8,128)}, u32[]{:S(2)}) copy-start(s32[8,8]{1,0:T(8,128)} %owner.3) | copy-start | bytes 772
  69.8 70.3 %collective-permute-start.9 = (bf16[3,128,1024]{2,1,0:T(8,128)(2,1)}, bf16[3,128,1024]{2,1,0:T(8,128)(2,1)}, u32[]{:S(2)}, u32[]{:S(2)}) collective-permute-start(bf16[3,128,1024]{2,1,0:T(8,128)(2,1)} %slice_dynamic-update-slice_fusion.1), channel_id=1, source_target_pairs={{0,192},{64,256},{128,320},{192,384},{256,448},{320,0},{384,64},{4... | collective-permute-start | bytes 2359304 | tf_op jit(solution)/shard_map/ppermute | solution.py:271
  76.1 35.7 %copy-start.6 = (bf16[2,128,1024]{2,1,0:T(8,128)(2,1)}, bf16[2,128,1024]{2,1,0:T(8,128)(2,1)S(1)}, u32[]{:S(2)}) copy-start(bf16[2,128,1024]{2,1,0:T(8,128)(2,1)S(1)} %collective-permute-done.7.two_up) | copy-start | bytes 1572868
  76.1 35.7 %copy-start.7 = (bf16[2,128,1024]{2,1,0:T(8,128)(2,1)}, bf16[2,128,1024]{2,1,0:T(8,128)(2,1)S(1)}, u32[]{:S(2)}) copy-start(bf16[2,128,1024]{2,1,0:T(8,128)(2,1)S(1)} %collective-permute-done.8.two_down) | copy-start | bytes 1572868
  111.8 13.1 %all-to-all-start = ((bf16[8,64,384]{2,1,0:T(8,128)(2,1)}), bf16[8,64,384]{2,1,0:T(8,128)(2,1)S(1)}, u32[]{:S(2)}, u32[]{:S(2)}) async-start(bf16[8,64,384]{2,1,0:T(8,128)(2,1)} %bitcast.11), calls=%async_computation | async-start | bytes 786432 | tf_op jit(solution)/shard_map/all_to_all | solution.py:316
  125.2 19.3 %collective-permute-start.11 = (bf16[64,2176]{1,0:T(8,128)(2,1)S(1)}, bf16[64,2176]{1,0:T(8,128)(2,1)S(1)}, u32[]{:S(2)}, u32[]{:S(2)}) collective-permute-start(bf16[64,2176]{1,0:T(8,128)(2,1)S(1)} %get-tuple-element.51.q0), channel_id=1, source_target_pairs={{1,0},{2,1},{3,2},{4,3},{5,4},{6,5},{7,6},{8,7},{9,8},{10,9},{11,1... | collective-permute-start | bytes 835592 | tf_op jit(solution)/shard_map/ppermute | solution.py:341
  127.9 16.6 %collective-permute-start.12 = (bf16[64,2176]{1,0:T(8,128)(2,1)S(1)}, bf16[64,2176]{1,0:T(8,128)(2,1)S(1)}, u32[]{:S(2)}, u32[]{:S(2)}) collective-permute-start(bf16[64,2176]{1,0:T(8,128)(2,1)S(1)} %get-tuple-element.51.q0), channel_id=1, source_target_pairs={{2,0},{3,1},{4,2},{5,3},{6,4},{7,5},{8,6},{9,7},{10,8},{11,9},{12,... | collective-permute-start | bytes 835592 | tf_op jit(solution)/shard_map/ppermute | solution.py:341
  144.4 13.5 %copy-start.1 = (bf16[1024,1024]{1,0:T(8,128)(2,1)S(1)}, bf16[1024,1024]{1,0:T(8,128)(2,1)}, u32[]{:S(2)}) copy-start(bf16[1024,1024]{1,0:T(8,128)(2,1)} %get-tuple-element.63.kv) | copy-start | bytes 6291460
  147.5 12.3 %collective-permute-start.13 = (bf16[64,2176]{1,0:T(8,128)(2,1)S(1)}, bf16[64,2176]{1,0:T(8,128)(2,1)S(1)}, u32[]{:S(2)}, u32[]{:S(2)}) collective-permute-start(bf16[64,2176]{1,0:T(8,128)(2,1)S(1)} %get-tuple-element.66), channel_id=1, source_target_pairs={{0,1},{1,2},{2,3},{3,4},{4,5},{5,6},{6,7},{7,8},{8,9},{9,10},{10,1... | collective-permute-start | bytes 835592 | tf_op jit(solution)/shard_map/ppermute | solution.py:341
  155.9 10.6 %collective-permute-start.14 = (bf16[64,2176]{1,0:T(8,128)(2,1)S(1)}, bf16[64,2176]{1,0:T(8,128)(2,1)S(1)}, u32[]{:S(2)}, u32[]{:S(2)}) collective-permute-start(bf16[64,2176]{1,0:T(8,128)(2,1)S(1)} %get-tuple-element.67), channel_id=1, source_target_pairs={{0,2},{1,3},{2,4},{3,5},{4,6},{5,7},{6,8},{7,9},{8,10},{9,11},{10,... | collective-permute-start | bytes 835592 | tf_op jit(solution)/shard_map/ppermute | solution.py:341
Sparse Core Ops, SparseCore 0:
  10.2 41.4 all-gather.2
  57.6 47.9 all-gather.4
